TPU v7x, 512 devices: a whole 4x8x8 slice. The times are simulated.
512 devices in a mesh: section: 32 (over x, z_hi, core), dp: 16 (over y, z_lo).
Axes of the slice: x: 4, y: 8, z: 8 (z_hi: 4, z_lo: 2; z = z_hi * 2 + z_lo), core: 2. Of those that a mesh axis runs over, the one named last changes fastest.
Arguments:
- layer_input: bfloat16 [32, 128, 12288], P('section', None, 'dp'), may hold values from -6 to 6
- fresh_input: bfloat16 [128, 12288], P(None, 'dp'), may hold values from -6 to 6
- out_grad: bfloat16 [32, 128, 12288], P('section', None, 'dp'), may hold values from -6 to 6
- held_stash: bfloat16 [32, 2, 128, 12288], P('section', None, None, 'dp'), may hold values from -6 to 6
- norm_gain: bfloat16 [32, 12288], P('section', 'dp'), may hold values from 0.099609375 to 1.8984375
- down_proj: bfloat16 [32, 12288, 512], P('section', 'dp'), may hold values from -0.0546875 to 0.0546875
- up_proj: bfloat16 [32, 512, 12288], P('section', None, 'dp'), may hold values from -0.25 to 0.25
- fetch_slot: int32 [32, 2], replicated, may hold values from 0 to 1
- evict_slot: int32 [32, 2], replicated, may hold values from 0 to 1
Outputs:
- next_output: bfloat16 [32, 128, 12288], P('section', None, 'dp')
- input_grad: bfloat16 [32, 128, 12288], P('section', None, 'dp')
- stash_out: bfloat16 [32, 2, 128, 12288], P('section', None, None, 'dp')
- gain_grad: float32 [32, 12288], P('section', 'dp')
- down_grad: bfloat16 [32, 12288, 512], P('section', 'dp')
- up_grad: bfloat16 [32, 512, 12288], P('section', None, 'dp')
All inputs are finite; a program needn't handle non-finite values.
Results may differ from a plain program's by a relative error of at most 0.007.
Values may be sent and summed in bfloat16 or wider, within the bound.
No kernel may reach another device: no remote copies, remote signals or barrier semaphores. Data moves between devices by JAX's collectives and lax.ppermute only.
A program may use at most 64 MiB of HBM per device.

v0:
```python
import jax
import jax.numpy as jnp
from jax import lax
from jax.sharding import PartitionSpec as P


def swapped(value, axis, distance):
    mask = 2**distance
    pairs = [(source, source ^ mask) for source in range(lax.axis_size(axis))]
    return lax.ppermute(value, axis, pairs)


def passed_along(array, axis, by):
    peers = lax.axis_size(axis)
    pairs = [(i, i + by) for i in range(peers) if 0 <= i + by < peers]
    return lax.ppermute(array, axis, pairs)


def row_totals(first, second):
    return lax.psum((first, second), "dp")


def normalize(tokens, scale_gain):
    values = tokens.astype(jnp.float32)
    width = values.shape[-1] * lax.axis_size("dp")
    total_one, total_two = row_totals(
        jnp.sum(values, axis=-1, keepdims=True), jnp.sum(values * values, axis=-1, keepdims=True)
    )
    center_mean = total_one / width
    inverse = lax.rsqrt(total_two / width - center_mean * center_mean + 1e-05)
    normed = (values - center_mean) * inverse
    scaled = (normed * scale_gain).astype(jnp.bfloat16)
    return (normed, inverse, scaled)


def layer_forward(tokens, scale_gain, down_weight, up_weight):
    normed, inverse, scaled = normalize(tokens, scale_gain)
    hidden = lax.psum(jnp.dot(scaled, down_weight, preferred_element_type=jnp.float32), "dp")
    active = jax.nn.gelu(hidden).astype(jnp.bfloat16)
    return (
        tokens.astype(jnp.float32) + jnp.dot(active, up_weight, preferred_element_type=jnp.float32)
    ).astype(jnp.bfloat16)


def layer_backward(tokens, upstream, scale_gain, down_weight, up_weight):
    normed, inverse, scaled = normalize(tokens, scale_gain)
    width = normed.shape[-1] * lax.axis_size("dp")
    hidden_part = jnp.dot(scaled, down_weight, preferred_element_type=jnp.float32)
    slope_part = lax.dot_general(
        upstream, up_weight, (((1,), (1,)), ((), ())), preferred_element_type=jnp.float32
    )
    hidden, grad_active = lax.psum((hidden_part, slope_part), "dp")
    active = jax.nn.gelu(hidden).astype(jnp.bfloat16)
    gelu_slope = jax.jvp(jax.nn.gelu, (hidden,), (jnp.ones_like(hidden),))[1]
    grad_hidden = (grad_active * gelu_slope).astype(jnp.bfloat16)
    grad_scaled = lax.dot_general(
        grad_hidden, down_weight, (((1,), (1,)), ((), ())), preferred_element_type=jnp.float32
    )
    grad_normed = grad_scaled * scale_gain
    total_one, total_two = row_totals(
        jnp.sum(grad_normed, axis=-1, keepdims=True),
        jnp.sum(grad_normed * normed, axis=-1, keepdims=True),
    )
    grad_rows = inverse * (grad_normed - total_one / width - normed * (total_two / width))
    tokens_grad = (upstream.astype(jnp.float32) + grad_rows).astype(jnp.bfloat16)
    gain_term = jnp.sum(grad_scaled * normed, axis=0)
    down_term = lax.dot_general(
        scaled, grad_hidden, (((0,), (0,)), ((), ())), preferred_element_type=jnp.float32
    )
    up_term = lax.dot_general(
        active, upstream, (((0,), (0,)), ((), ())), preferred_element_type=jnp.float32
    )
    return (tokens_grad, gain_term, down_term, up_term)


def table_entry(table, row_index, column):
    return lax.dynamic_slice(table, (row_index, jnp.int32(column)), (1, 1))[0, 0]


def slot_read(stash, slot_index):
    return lax.dynamic_index_in_dim(stash, slot_index, 0, keepdims=False)


def slot_write(stash, value, slot_index):
    return lax.dynamic_update_index_in_dim(stash, value, slot_index, 0)


def mirror(stacked):
    digits = lax.axis_size("section").bit_length() - 1
    sequence = list(range(digits))
    for digit in sequence:
        stacked = swapped(stacked, "section", digit)
    return stacked


def on_device(
    layer_input,
    fresh_input,
    out_grad,
    held_stash,
    norm_gain,
    down_proj,
    up_proj,
    fetch_slot,
    evict_slot,
):
    sections = lax.axis_size("section")
    place = lax.axis_index("section")
    partner = sections - 1 - place
    scale_gain = norm_gain[0].astype(jnp.float32)
    down_weight = down_proj[0]
    up_weight = up_proj[0]
    stash = held_stash[0]
    first_in = layer_input[0]
    first_out = layer_forward(first_in, scale_gain, down_weight, up_weight)
    outgoing = slot_read(stash, table_entry(fetch_slot, partner, 0))
    arrived = mirror(jnp.stack([first_in, outgoing], 0))
    first_fetch = arrived[1]
    stash = slot_write(stash, arrived[0], table_entry(evict_slot, partner, 0))
    first_terms = layer_backward(first_fetch, out_grad[0], scale_gain, down_weight, up_weight)
    first_grad = first_terms[0]
    before_out = passed_along(first_out, "section", 1)
    after_grad = passed_along(first_grad, "section", -1)
    second_in = jnp.where(place == 0, fresh_input, before_out)
    second_up = jnp.where(place == sections - 1, first_out, after_grad)
    next_output = layer_forward(second_in, scale_gain, down_weight, up_weight)
    outgoing = slot_read(stash, table_entry(fetch_slot, partner, 1))
    arrived = mirror(jnp.stack([second_in, outgoing], 0))
    second_fetch = arrived[1]
    stash = slot_write(stash, arrived[0], table_entry(evict_slot, partner, 1))
    second_terms = layer_backward(second_fetch, second_up, scale_gain, down_weight, up_weight)
    gain_grad = first_terms[1] + second_terms[1]
    down_grad = (first_terms[2] + second_terms[2]).astype(jnp.bfloat16)
    up_grad = (first_terms[3] + second_terms[3]).astype(jnp.bfloat16)
    return (
        next_output[None],
        second_terms[0][None],
        stash[None],
        gain_grad[None],
        down_grad[None],
        up_grad[None],
    )


def solution(mesh):
    placed = (
        P("section", None, "dp"),
        P(None, "dp"),
        P("section", None, "dp"),
        P("section", None, None, "dp"),
        P("section", "dp"),
        P("section", "dp", None),
        P("section", None, "dp"),
        P(),
        P(),
    )
    return jax.shard_map(
        on_device,
        mesh=mesh,
        in_specs=placed,
        out_specs=(
            P("section", None, "dp"),
            P("section", None, "dp"),
            P("section", None, None, "dp"),
            P("section", "dp"),
            P("section", "dp", None),
            P("section", None, "dp"),
        ),
        check_vma=False,
    )
```

profile of v0, /device:TPU:1, one launch (start us, length us, event | category | flops | bytes accessed | tf_op | source)
XLA Modules:
  0.0 725.4 jit_solution(16529133342193084386)
XLA Ops:
  7.3 1.9 copy.24
  14.4 8.8 %collective-permute-start.1 = (bf16[2,128,768]{2,1,0:T(8,128)(2,1)S(1)}, bf16[2,128,768]{2,1,0:T(8,128)(2,1)S(1)}, u32[]{:S(2)}, u32[]{:S(2)}) collective-permute-start(bf16[2,128,768]{2,1,0:T(8,128)(2,1)S(1)} %pad_maximum_fusion), channel_id=1, source_target_pairs={{0,16},{16,0},{32,48},{48,32},{64,80},{80,64},{96,112},{112,96},{1... | collective-permute-start | bytes 1179656 | tf_op jit(solution)/shard_map/ppermute | solution.py:10
  24.6 1.9 collective-permute-start.2
  26.5 18.3 %collective-permute-done.2 = bf16[2,128,768]{2,1,0:T(8,128)(2,1)S(1)} collective-permute-done((bf16[2,128,768]{2,1,0:T(8,128)(2,1)S(1)}, bf16[2,128,768]{2,1,0:T(8,128)(2,1)S(1)}, u32[]{:S(2)}, u32[]{:S(2)}) %collective-permute-start.2) | collective-permute-done | bytes 393248 | tf_op jit(solution)/shard_map/ppermute | solution.py:10
  44.8 6.5 collective-permute-start.3
  51.4 17.9 %collective-permute-done.3 = bf16[2,128,768]{2,1,0:T(8,128)(2,1)S(1)} collective-permute-done((bf16[2,128,768]{2,1,0:T(8,128)(2,1)S(1)}, bf16[2,128,768]{2,1,0:T(8,128)(2,1)S(1)}, u32[]{:S(2)}, u32[]{:S(2)}) %collective-permute-start.3) | collective-permute-done | bytes 393248 | tf_op jit(solution)/shard_map/ppermute | solution.py:10
  69.3 1.9 collective-permute-start.4
  71.3 9.1 %collective-permute-done.4 = bf16[2,128,768]{2,1,0:T(8,128)(2,1)S(1)} collective-permute-done((bf16[2,128,768]{2,1,0:T(8,128)(2,1)S(1)}, bf16[2,128,768]{2,1,0:T(8,128)(2,1)S(1)}, u32[]{:S(2)}, u32[]{:S(2)}) %collective-permute-start.4) | collective-permute-done | bytes 393248 | tf_op jit(solution)/shard_map/ppermute | solution.py:10
  80.4 2.9 collective-permute-start.5
  84.6 7.5 %collective-permute-done.5 = bf16[2,128,768]{2,1,0:T(8,128)(2,1)S(1)} collective-permute-done((bf16[2,128,768]{2,1,0:T(8,128)(2,1)S(1)}, bf16[2,128,768]{2,1,0:T(8,128)(2,1)S(1)}, u32[]{:S(2)}, u32[]{:S(2)}) %collective-permute-start.5) | collective-permute-done | bytes 393248 | tf_op jit(solution)/shard_map/ppermute | solution.py:10
  92.3 23.7 %all-reduce.2 = (f32[128,1]{0,1:T(1,128)S(1)}, f32[128,1]{0,1:T(1,128)S(1)}, f32[128,1]{0,1:T(1,128)S(1)}, f32[128,1]{0,1:T(1,128)S(1)}) all-reduce(f32[128,1]{0,1:T(1,128)S(1)} %bitcast.182, f32[128,1]{0,1:T(1,128)S(1)} %bitcast.181, f32[128,1]{0,1:T(1,128)S(1)} %bitcast.184, ...), channel_id=1, replica_groups=mesh['section'=32,'dp'=16] {'dp'}, use_global_device_ids=true, to_apply=%region_3.0 | all-reduce | flops 512 | bytes 4096 | tf_op jit(solution)/shard_map/psum | solution.py:20
  122.0 139.1 %all-reduce.13.cloned.1.call-done = (f32[128,512]{1,0:T(8,128)}, f32[128,512]{1,0:T(8,128)}, f32[128,512]{1,0:T(8,128)}) async-done(((f32[128,512]{1,0:T(8,128)}, f32[128,512]{1,0:T(8,128)}, f32[128,512]{1,0:T(8,128)}), (f32[128,512]{1,0:T(8,128)}, f32[128,512]{1,0:T(8,128)}, f32[128,512]{1,0:T(8,128)})) %all-reduce.13.cloned.1.call-update) | async-done | bytes 786448 | tf_op jit(solution)/shard_map/psum | solution.py:38
  262.4 14.9 %collective-permute-start = (bf16[128,768]{1,0:T(8,128)(2,1)S(1)}, bf16[128,768]{1,0:T(8,128)(2,1)S(1)}, u32[]{:S(2)}, u32[]{:S(2)}) collective-permute-start(bf16[128,768]{1,0:T(8,128)(2,1)S(1)} %fusion.2), channel_id=1, source_target_pairs={{0,16},{16,32},{32,48},{48,64},{64,80},{80,96},{96,112},{112,128},... | collective-permute-start | bytes 589832 | tf_op jit(solution)/shard_map/ppermute | solution.py:16
  281.4 1.9 collective-permute-start.7
  285.0 7.4 %collective-permute-start.8 = (bf16[2,128,768]{2,1,0:T(8,128)(2,1)S(1)}, bf16[2,128,768]{2,1,0:T(8,128)(2,1)S(1)}, u32[]{:S(2)}, u32[]{:S(2)}) collective-permute-start(bf16[2,128,768]{2,1,0:T(8,128)(2,1)S(1)} %collective-permute-done.7), channel_id=1, source_target_pairs={{0,32},{16,48},{32,0},{48,16},{64,96},{80,112},{96,64},{112,80},{1... | collective-permute-start | bytes 1179656 | tf_op jit(solution)/shard_map/ppermute | solution.py:10
  292.5 17.8 %collective-permute-done.8 = bf16[2,128,768]{2,1,0:T(8,128)(2,1)S(1)} collective-permute-done((bf16[2,128,768]{2,1,0:T(8,128)(2,1)S(1)}, bf16[2,128,768]{2,1,0:T(8,128)(2,1)S(1)}, u32[]{:S(2)}, u32[]{:S(2)}) %collective-permute-start.8) | collective-permute-done | bytes 393248 | tf_op jit(solution)/shard_map/ppermute | solution.py:10
  310.2 7.5 %collective-permute-start.9 = (bf16[2,128,768]{2,1,0:T(8,128)(2,1)S(1)}, bf16[2,128,768]{2,1,0:T(8,128)(2,1)S(1)}, u32[]{:S(2)}, u32[]{:S(2)}) collective-permute-start(bf16[2,128,768]{2,1,0:T(8,128)(2,1)S(1)} %collective-permute-done.8), channel_id=1, source_target_pairs={{0,64},{16,80},{32,96},{48,112},{64,0},{80,16},{96,32},{112,48},{1... | collective-permute-start | bytes 1179656 | tf_op jit(solution)/shard_map/ppermute | solution.py:10
  317.8 17.3 %collective-permute-done.9 = bf16[2,128,768]{2,1,0:T(8,128)(2,1)S(1)} collective-permute-done((bf16[2,128,768]{2,1,0:T(8,128)(2,1)S(1)}, bf16[2,128,768]{2,1,0:T(8,128)(2,1)S(1)}, u32[]{:S(2)}, u32[]{:S(2)}) %collective-permute-start.9) | collective-permute-done | bytes 393248 | tf_op jit(solution)/shard_map/ppermute | solution.py:10
  335.0 2.6 collective-permute-start.10
  339.6 6.7 collective-permute-done.10
  346.3 3.7 collective-permute-start.11
  351.2 7.1 collective-permute-done.11
  358.5 24.3 %all-reduce.1 = (f32[128,1]{0,1:T(1,128)S(1)}, f32[128,1]{0,1:T(1,128)S(1)}, f32[128,1]{0,1:T(1,128)S(1)}, f32[128,1]{0,1:T(1,128)S(1)}) all-reduce(f32[128,1]{0,1:T(1,128)S(1)} %bitcast.189, f32[128,1]{0,1:T(1,128)S(1)} %bitcast.190, f32[128,1]{0,1:T(1,128)S(1)} %bitcast.186, ...), channel_id=1, replica_groups=mesh['section'=32,'dp'=16] {'dp'}, use_global_device_ids=true, to_apply=%region_19.20 | all-reduce | flops 512 | bytes 4096 | tf_op jit(solution)/shard_map/psum | solution.py:20
  383.0 11.8 %collective-permute-start.6 = (bf16[128,768]{1,0:T(8,128)(2,1)S(1)}, bf16[128,768]{1,0:T(8,128)(2,1)S(1)}, u32[]{:S(2)}, u32[]{:S(2)}) collective-permute-start(bf16[128,768]{1,0:T(8,128)(2,1)S(1)} %fusion.51), channel_id=1, source_target_pairs={{16,0},{32,16},{48,32},{64,48},{80,64},{96,80},{112,96},{128,112},... | collective-permute-start | bytes 589832 | tf_op jit(solution)/shard_map/ppermute | solution.py:16
  395.8 7.9 %collective-permute-done.6 = bf16[128,768]{1,0:T(8,128)(2,1)S(1)} collective-permute-done((bf16[128,768]{1,0:T(8,128)(2,1)S(1)}, bf16[128,768]{1,0:T(8,128)(2,1)S(1)}, u32[]{:S(2)}, u32[]{:S(2)}) %collective-permute-start.6) | collective-permute-done | bytes 196640 | tf_op jit(solution)/shard_map/ppermute | solution.py:16
  407.1 2.6 fusion.120
  410.4 123.9 %all-reduce.11.cloned.1.call-done = (f32[128,512]{1,0:T(8,128)}, f32[128,512]{1,0:T(8,128)}) async-done(((f32[128,512]{1,0:T(8,128)}, f32[128,512]{1,0:T(8,128)}), (f32[128,512]{1,0:T(8,128)}, f32[128,512]{1,0:T(8,128)})) %all-reduce.11.cloned.1.call-update) | async-done | bytes 524304 | tf_op jit(solution)/shard_map/psum | solution.py:52
  537.9 27.0 %all-reduce = (f32[128,1]{0,1:T(1,128)}, f32[128,1]{0,1:T(1,128)}, f32[128,1]{0,1:T(1,128)}, f32[128,1]{0,1:T(1,128)}) all-reduce(f32[128,1]{0,1:T(1,128)} %bitcast.188, f32[128,1]{0,1:T(1,128)S(1)} %bitcast.187, f32[128,1]{0,1:T(1,128)} %bitcast.191, f32[128,1]{0,1:T(1,128)} %bitcast.192), channel_id=1, replica_groups=mesh['section'=32,'dp'=16] {'dp'}, use_global_device_ids=true, to_apply=%region_8.9 | all-reduce | flops 512 | bytes 4096 | tf_op jit(solution)/shard_map/psum | solution.py:20
  567.9 2.0 fusion.19
  569.9 2.9 fusion.1
  575.7 141.1 %all-reduce.9.cloned.1.call-done = f32[128,512]{1,0:T(8,128)} async-done(((f32[128,512]{1,0:T(8,128)}), f32[128,512]{1,0:T(8,128)}) %all-reduce.9.cloned.1.call-update) | async-done | bytes 262160 | tf_op jit(solution)/shard_map/psum | solution.py:38
  716.8 2.0 fusion.4
  (99 shorter events, 31.7 us)
Async XLA Ops:
  7.2 108.8 %copy-start = (bf16[1,768,512]{2,1,0:T(8,128)(2,1)S(1)}, bf16[1,768,512]{2,1,0:T(8,128)(2,1)}, u32[]{:S(2)}) copy-start(bf16[1,768,512]{2,1,0:T(8,128)(2,1)} %param.14) | copy-start | bytes 2359300
  7.2 64.0 %copy-start.5 = (bf16[1,128,768]{2,1,0:T(8,128)(2,1)S(1)}, bf16[1,128,768]{2,1,0:T(8,128)(2,1)}, u32[]{:S(2)}) copy-start(bf16[1,128,768]{2,1,0:T(8,128)(2,1)} %param.9) | copy-start | bytes 589828
  7.2 76.3 %copy-start.9 = (bf16[1,128,768]{2,1,0:T(8,128)(2,1)S(1)}, bf16[1,128,768]{2,1,0:T(8,128)(2,1)}, u32[]{:S(2)}) copy-start(bf16[1,128,768]{2,1,0:T(8,128)(2,1)} %param.11) | copy-start | bytes 589828
  7.2 76.1 %copy-start.21 = (bf16[1,768]{1,0:T(2,128)(2,1)S(1)}, bf16[1,768]{1,0:T(2,128)(2,1)}, u32[]{:S(2)}) copy-start(bf16[1,768]{1,0:T(2,128)(2,1)} %param.13) | copy-start | bytes 4612
  7.2 76.2 %copy-start.1 = (bf16[1,512,768]{2,1,0:T(8,128)(2,1)S(1)}, bf16[1,512,768]{2,1,0:T(8,128)(2,1)}, u32[]{:S(2)}) copy-start(bf16[1,512,768]{2,1,0:T(8,128)(2,1)} %param.15) | copy-start | bytes 2359300
  7.2 253.8 %all-reduce.13.cloned.1.call-start = ((), (), s32[]{:S(2)}) async-start(), calls=%async_computation.2 | async-start | bytes 1572864 | tf_op jit(solution)/shard_map/psum | solution.py:38
  14.4 10.1 %collective-permute-start.1 = (bf16[2,128,768]{2,1,0:T(8,128)(2,1)S(1)}, bf16[2,128,768]{2,1,0:T(8,128)(2,1)S(1)}, u32[]{:S(2)}, u32[]{:S(2)}) collective-permute-start(bf16[2,128,768]{2,1,0:T(8,128)(2,1)S(1)} %pad_maximum_fusion), channel_id=1, source_target_pairs={{0,16},{16,0},{32,48},{48,32},{64,80},{80,64},{96,112},{112,96},{1... | collective-permute-start | bytes 1179656 | tf_op jit(solution)/shard_map/ppermute | solution.py:10
  24.6 20.2 %collective-permute-start.2 = (bf16[2,128,768]{2,1,0:T(8,128)(2,1)S(1)}, bf16[2,128,768]{2,1,0:T(8,128)(2,1)S(1)}, u32[]{:S(2)}, u32[]{:S(2)}) collective-permute-start(bf16[2,128,768]{2,1,0:T(8,128)(2,1)S(1)} %collective-permute-done.1), channel_id=1, source_target_pairs={{0,32},{16,48},{32,0},{48,16},{64,96},{80,112},{96,64},{112,80},{1... | collective-permute-start | bytes 1179656 | tf_op jit(solution)/shard_map/ppermute | solution.py:10
  44.8 24.5 %collective-permute-start.3 = (bf16[2,128,768]{2,1,0:T(8,128)(2,1)S(1)}, bf16[2,128,768]{2,1,0:T(8,128)(2,1)S(1)}, u32[]{:S(2)}, u32[]{:S(2)}) collective-permute-start(bf16[2,128,768]{2,1,0:T(8,128)(2,1)S(1)} %collective-permute-done.2), channel_id=1, source_target_pairs={{0,64},{16,80},{32,96},{48,112},{64,0},{80,16},{96,32},{112,48},{1... | collective-permute-start | bytes 1179656 | tf_op jit(solution)/shard_map/ppermute | solution.py:10
  69.3 11.1 %collective-permute-start.4 = (bf16[2,128,768]{2,1,0:T(8,128)(2,1)S(1)}, bf16[2,128,768]{2,1,0:T(8,128)(2,1)S(1)}, u32[]{:S(2)}, u32[]{:S(2)}) collective-permute-start(bf16[2,128,768]{2,1,0:T(8,128)(2,1)S(1)} %collective-permute-done.3), channel_id=1, source_target_pairs={{0,128},{16,144},{32,160},{48,176},{64,192},{80,208},{96,224},{112... | collective-permute-start | bytes 1179656 | tf_op jit(solution)/shard_map/ppermute | solution.py:10
  80.4 11.7 %collective-permute-start.5 = (bf16[2,128,768]{2,1,0:T(8,128)(2,1)S(1)}, bf16[2,128,768]{2,1,0:T(8,128)(2,1)S(1)}, u32[]{:S(2)}, u32[]{:S(2)}) collective-permute-start(bf16[2,128,768]{2,1,0:T(8,128)(2,1)S(1)} %collective-permute-done.4), channel_id=1, source_target_pairs={{0,256},{16,272},{32,288},{48,304},{64,320},{80,336},{96,352},{112... | collective-permute-start | bytes 1179656 | tf_op jit(solution)/shard_map/ppermute | solution.py:10
  118.1 161.9 %copy-start.16 = (bf16[128,768]{1,0:T(8,128)(2,1)S(1)}, bf16[128,768]{1,0:T(8,128)(2,1)}, u32[]{:S(2)}) copy-start(bf16[128,768]{1,0:T(8,128)(2,1)} %param.10) | copy-start | bytes 589828
  118.1 416.2 %all-reduce.11.cloned.1.call-start = ((), (), s32[]{:S(2)}) async-start(), calls=%async_computation.1 | async-start | bytes 1048576 | tf_op jit(solution)/shard_map/psum | solution.py:52
  261.1 88.9 %copy-start.10 = (f32[128,512]{1,0:T(8,128)S(1)}, f32[128,512]{1,0:T(8,128)}, u32[]{:S(2)}) copy-start(f32[128,512]{1,0:T(8,128)} %get-tuple-element.30) | copy-start | bytes 786436
  261.1 88.9 %copy-start.15 = (f32[128,512]{1,0:T(8,128)S(1)}, f32[128,512]{1,0:T(8,128)}, u32[]{:S(2)}) copy-start(f32[128,512]{1,0:T(8,128)} %get-tuple-element.29) | copy-start | bytes 786436
  262.4 17.6 %collective-permute-start = (bf16[128,768]{1,0:T(8,128)(2,1)S(1)}, bf16[128,768]{1,0:T(8,128)(2,1)S(1)}, u32[]{:S(2)}, u32[]{:S(2)}) collective-permute-start(bf16[128,768]{1,0:T(8,128)(2,1)S(1)} %fusion.2), channel_id=1, source_target_pairs={{0,16},{16,32},{32,48},{48,64},{64,80},{80,96},{96,112},{112,128},... | collective-permute-start | bytes 589832 | tf_op jit(solution)/shard_map/ppermute | solution.py:16
  281.4 3.6 collective-permute-start.7
  285.0 25.2 %collective-permute-start.8 = (bf16[2,128,768]{2,1,0:T(8,128)(2,1)S(1)}, bf16[2,128,768]{2,1,0:T(8,128)(2,1)S(1)}, u32[]{:S(2)}, u32[]{:S(2)}) collective-permute-start(bf16[2,128,768]{2,1,0:T(8,128)(2,1)S(1)} %collective-permute-done.7), channel_id=1, source_target_pairs={{0,32},{16,48},{32,0},{48,16},{64,96},{80,112},{96,64},{112,80},{1... | collective-permute-start | bytes 1179656 | tf_op jit(solution)/shard_map/ppermute | solution.py:10
  310.2 24.8 %collective-permute-start.9 = (bf16[2,128,768]{2,1,0:T(8,128)(2,1)S(1)}, bf16[2,128,768]{2,1,0:T(8,128)(2,1)S(1)}, u32[]{:S(2)}, u32[]{:S(2)}) collective-permute-start(bf16[2,128,768]{2,1,0:T(8,128)(2,1)S(1)} %collective-permute-done.8), channel_id=1, source_target_pairs={{0,64},{16,80},{32,96},{48,112},{64,0},{80,16},{96,32},{112,48},{1... | collective-permute-start | bytes 1179656 | tf_op jit(solution)/shard_map/ppermute | solution.py:10
  335.0 11.3 %collective-permute-start.10 = (bf16[2,128,768]{2,1,0:T(8,128)(2,1)S(1)}, bf16[2,128,768]{2,1,0:T(8,128)(2,1)}, u32[]{:S(2)}, u32[]{:S(2)}) collective-permute-start(bf16[2,128,768]{2,1,0:T(8,128)(2,1)S(1)} %collective-permute-done.9), channel_id=1, source_target_pairs={{0,128},{16,144},{32,160},{48,176},{64,192},{80,208},{96,224},{112... | collective-permute-start | bytes 1179656 | tf_op jit(solution)/shard_map/ppermute | solution.py:10
  346.3 12.0 %collective-permute-start.11 = (bf16[2,128,768]{2,1,0:T(8,128)(2,1)}, bf16[2,128,768]{2,1,0:T(8,128)(2,1)S(1)}, u32[]{:S(2)}, u32[]{:S(2)}) collective-permute-start(bf16[2,128,768]{2,1,0:T(8,128)(2,1)} %collective-permute-done.10), channel_id=1, source_target_pairs={{0,256},{16,272},{32,288},{48,304},{64,320},{80,336},{96,352},{112... | collective-permute-start | bytes 1179656 | tf_op jit(solution)/shard_map/ppermute | solution.py:10
  350.2 8.1 %copy-start.11 = (bf16[128,512]{1,0:T(8,128)(2,1)}, bf16[128,512]{1,0:T(8,128)(2,1)S(1)}, u32[]{:S(2)}) copy-start(bf16[128,512]{1,0:T(8,128)(2,1)S(1)} %fusion.79) | copy-start | bytes 393220
  358.3 45.5 %copy-start.2 = (bf16[2,128,768]{2,1,0:T(8,128)(2,1)}, bf16[2,128,768]{2,1,0:T(8,128)(2,1)S(1)}, u32[]{:S(2)}) copy-start(bf16[2,128,768]{2,1,0:T(8,128)(2,1)S(1)} %collective-permute-done.11) | copy-start | bytes 1179652
  383.0 20.7 %collective-permute-start.6 = (bf16[128,768]{1,0:T(8,128)(2,1)S(1)}, bf16[128,768]{1,0:T(8,128)(2,1)S(1)}, u32[]{:S(2)}, u32[]{:S(2)}) collective-permute-start(bf16[128,768]{1,0:T(8,128)(2,1)S(1)} %fusion.51), channel_id=1, source_target_pairs={{16,0},{32,16},{48,32},{64,48},{80,64},{96,80},{112,96},{128,112},... | collective-permute-start | bytes 589832 | tf_op jit(solution)/shard_map/ppermute | solution.py:16
  394.8 10.8 %copy-start.17 = (f32[128]{0:T(128)}, f32[128]{0:T(128)S(1)}, u32[]{:S(2)}) copy-start(f32[128]{0:T(128)S(1)} %get-tuple-element.39) | copy-start | bytes 1540
  405.6 311.3 %all-reduce.9.cloned.1.call-start = ((), (), s32[]{:S(2)}) async-start(), calls=%async_computation | async-start | bytes 524288 | tf_op jit(solution)/shard_map/psum | solution.py:38
  405.6 4.1 copy-start.3
  407.1 129.1 %copy-start.4 = (bf16[2,128,768]{2,1,0:T(8,128)(2,1)S(1)}, bf16[2,128,768]{2,1,0:T(8,128)(2,1)}, u32[]{:S(2)}) copy-start(bf16[2,128,768]{2,1,0:T(8,128)(2,1)} %copy-done.2) | copy-start | bytes 1179652
  407.1 129.1 %copy-start.18 = (f32[128]{0:T(128)S(1)}, f32[128]{0:T(128)}, u32[]{:S(2)}) copy-start(f32[128]{0:T(128)} %copy-done.17) | copy-start | bytes 1540
  409.7 128.1 %copy-start.22 = (f32[128]{0:T(128)S(1)}, f32[128]{0:T(128)}, u32[]{:S(2)}) copy-start(f32[128]{0:T(128)} %get-tuple-element.12) | copy-start | bytes 1540
  569.9 3.0 copy-start.13
  572.9 2.0 copy-start.8
  (8 other events, 10.8 us)
Sparse Core Ops, SparseCore 0:
  118.2 142.8 all-reduce.12
  405.7 128.5 all-reduce.10
  570.0 146.7 all-reduce.8
where the time goes:
time: 735 us; the launch traced here: 725 us
  waiting for transfers between devices  518 us (70%)
  blocking collectives  74.9 us (10%)
  starting transfers between devices  72.1 us (10%)
  between operations  21.9 us (3%)
  matrix products  21.6 us (3%)
  local copies, waits for them, and re-layouts  9.26 us (1%)
  other arithmetic  8.06 us (1%)
    psum x2, waiting for transfers between devices, layer_forward(): lax.psum(jnp.dot(scaled, down_weight, preferred_element_type=jnp.float32)...  280 us
    psum x1, waiting for transfers between devices, layer_backward(): hidden, grad_active = lax.psum((hidden_part, slope_part), 'dp')  124 us
    ppermute x10, waiting for transfers between devices, swapped(): return lax.ppermute(value, axis, pairs)  105 us
    psum x3, blocking collectives, row_totals(): return lax.psum((first, second), 'dp')  74.9 us
    ppermute x10, starting transfers between devices, swapped(): return lax.ppermute(value, axis, pairs)  45.2 us
    ppermute x2, starting transfers between devices, passed_along(): return lax.ppermute(array, axis, pairs)  26.7 us
  transfers between devices with their start and end apart: 15, of which 15 were waited for; matrix products, arithmetic and copies ran while one was open for 2% of the time, Pallas kernels for 0%

commit v1 on v0

v1 whole, which is shorter than its diff:
```python
import jax
import jax.numpy as jnp
from jax import lax
from jax.sharding import PartitionSpec as P

BF16 = jnp.bfloat16
F32 = jnp.float32
EPS = 1e-05


def rounded(value):
    return lax.reduce_precision(value, 8, 7)


def pieces(value):
    high = rounded(value)
    middle = rounded(value - high)
    low = rounded(value - high - middle)
    return [high.astype(BF16), middle.astype(BF16), low.astype(BF16)]


def joined(high, middle, low):
    return high.astype(F32) + middle.astype(F32) + low.astype(F32)


def across(block, width=None):
    return lax.all_to_all(block, "dp", 0, 0, tiled=True)


def mirrored(value):
    sections = lax.axis_size("section")
    return lax.ppermute(value, "section", [(i, sections - 1 - i) for i in range(sections)])


def shifted(value, by):
    sections = lax.axis_size("section")
    pairs = [(i, i + by) for i in range(sections) if 0 <= i + by < sections]
    return lax.ppermute(value, "section", pairs)


def lanes(columns, rows):
    block = jnp.concatenate(columns, axis=1)
    return jnp.pad(block, ((0, 0), (0, 128 - block.shape[1])))


def row_sums(values):
    return [jnp.sum(values, axis=1, keepdims=True), jnp.sum(values * values, axis=1, keepdims=True)]


def hidden_part(tokens, weight, column_sum):
    values = tokens.astype(F32)
    one, two = row_sums(values)
    local = one / values.shape[1]
    part = jnp.dot(tokens, weight, preferred_element_type=F32) - local * column_sum
    return part.astype(BF16), pieces(one) + pieces(two)


def slope_part(upstream, up_weight):
    return lax.dot_general(upstream, up_weight, (((1,), (1,)), ((), ())), preferred_element_type=F32).astype(BF16)


def summed(block, groups):
    rows = block.shape[0] // groups
    return jnp.sum(block.astype(F32).reshape(groups, rows, block.shape[1]), axis=0)


def finish_hidden(part, sums, column_sums, width):
    peers = column_sums.shape[0]
    one = joined(sums[:, 0], sums[:, 1], sums[:, 2]).reshape(peers, -1)
    two = joined(sums[:, 3], sums[:, 4], sums[:, 5]).reshape(peers, -1)
    mean = jnp.sum(one, axis=0) / width
    inverse = lax.rsqrt(jnp.sum(two, axis=0) / width - mean * mean + EPS)
    local = one / (width // peers) - mean[None]
    total = summed(part, peers) + lax.dot_general(
        local, column_sums, (((0,), (0,)), ((), ())), precision=lax.Precision.HIGHEST, preferred_element_type=F32
    )
    return total * inverse[:, None], mean[:, None], inverse[:, None]


def gelu_slope(hidden):
    return jax.jvp(jax.nn.gelu, (hidden,), (jnp.ones_like(hidden),))[1]


def to_all(block, peers):
    return jnp.tile(block, (peers, 1))


def back_stats(grad_hidden, hidden, mean, inverse, column_exact, width):
    grad = grad_hidden.astype(F32)
    first = jnp.sum(grad * column_exact, axis=1, keepdims=True) / width
    second = jnp.sum(grad * hidden, axis=1, keepdims=True) / width
    return pieces(mean) + pieces(inverse) + pieces(first) + pieces(second)


def unpack_stats(block):
    return [joined(block[:, 3 * i : 3 * i + 1], block[:, 3 * i + 1 : 3 * i + 2], block[:, 3 * i + 2 : 3 * i + 3]) for i in range(4)]


def backward(tokens, upstream, grad_hidden, active, stats, gain, down_weight):
    mean, inverse, first, second = stats
    normed = (tokens.astype(F32) - mean) * inverse
    scaled = (normed * gain).astype(BF16)
    grad_scaled = lax.dot_general(grad_hidden, down_weight, (((1,), (1,)), ((), ())), preferred_element_type=F32)
    grad_rows = inverse * (grad_scaled * gain - first - normed * second)
    tokens_grad = (upstream.astype(F32) + grad_rows).astype(BF16)
    gain_term = jnp.sum(grad_scaled * normed, axis=0)
    down_term = lax.dot_general(scaled, grad_hidden, (((0,), (0,)), ((), ())), preferred_element_type=F32)
    return tokens_grad, gain_term, down_term


def up_term(active, upstream):
    return lax.dot_general(active, upstream, (((0,), (0,)), ((), ())), preferred_element_type=F32)


def on_device(layer_input, fresh_input, out_grad, held_stash, norm_gain, down_proj, up_proj, fetch_slot, evict_slot):
    sections = lax.axis_size("section")
    peers = lax.axis_size("dp")
    place = lax.axis_index("section")
    partner = sections - 1 - place
    tokens0, grad0, stash = layer_input[0], out_grad[0], held_stash[0]
    gain = norm_gain[0].astype(F32)[None]
    down_weight, up_weight = down_proj[0], up_proj[0]
    rows, features = tokens0.shape
    rank = up_weight.shape[0]
    width = features * peers
    block_rows = rows // peers

    partner_fetch = lax.dynamic_slice(fetch_slot, (partner, 0), (1, 2))[0]
    partner_evict = lax.dynamic_slice(evict_slot, (partner, 0), (1, 2))[0]
    own_fetch = lax.dynamic_slice(fetch_slot, (place, 0), (1, 2))[0]
    own_evict = lax.dynamic_slice(evict_slot, (place, 0), (1, 2))[0]

    fetched0 = mirrored(jnp.where(partner_fetch[0] == 0, stash[0], stash[1]))
    both = mirrored(jnp.stack([jnp.where(partner_fetch[1] == 0, stash[0], stash[1]), tokens0], 0))
    fetched1 = jnp.where(own_fetch[1] == own_evict[0], tokens0, both[0])
    partner_tokens0 = both[1]

    exact = gain.T * down_weight.astype(F32)
    weight = exact.astype(BF16)
    column_sum = jnp.sum(rounded(exact), axis=0, keepdims=True)
    column_exact = jnp.sum(exact, axis=0, keepdims=True)
    columns = jnp.concatenate(pieces(column_sum) + pieces(column_exact), axis=0)
    columns = to_all(jnp.pad(columns, ((0, block_rows - 6), (0, 0))), peers)

    part, sums = hidden_part(tokens0, weight, column_sum)
    got = across(jnp.concatenate([part, slope_part(grad0, up_weight), columns, lanes(sums, rows)], axis=1))
    all_columns = got[:, 2 * rank : 3 * rank].reshape(peers, block_rows, rank)
    column_sums = joined(all_columns[:, 0], all_columns[:, 1], all_columns[:, 2])
    column_exact = jnp.sum(joined(all_columns[:, 3], all_columns[:, 4], all_columns[:, 5]), axis=0, keepdims=True)
    hidden_f0 = finish_hidden(got[:, :rank], got[:, 3 * rank :], column_sums, width)[0]
    slope0 = summed(got[:, rank : 2 * rank], peers)
    active_f0 = jax.nn.gelu(hidden_f0).astype(BF16)

    part, sums = hidden_part(fetched0, weight, column_sum)
    got = across(jnp.concatenate([part, lanes(sums, rows)], axis=1))
    hidden_b0, mean0, inverse0 = finish_hidden(got[:, :rank], got[:, rank:], column_sums, width)
    active_b0 = jax.nn.gelu(hidden_b0).astype(BF16)
    grad_hidden0 = (slope0 * gelu_slope(hidden_b0)).astype(BF16)
    stats = back_stats(grad_hidden0, hidden_b0, mean0, inverse0, column_exact, width)
    got = across(
        to_all(jnp.concatenate([active_f0, grad_hidden0, lanes(stats, block_rows)], axis=1), peers)
    )
    stats0 = unpack_stats(got[:, 2 * rank :])
    active_f0, grad_hidden0 = got[:, :rank], got[:, rank : 2 * rank]
    first_out = (tokens0.astype(F32) + jnp.dot(active_f0, up_weight, preferred_element_type=F32)).astype(BF16)
    first_grad, gain_term0, down_term0 = backward(fetched0, grad0, grad_hidden0, None, stats0, gain, down_weight)

    before_out = shifted(first_out, 1)
    after_grad = shifted(first_grad, -1)
    tokens1 = jnp.where(place == 0, fresh_input, before_out)
    grad1 = jnp.where(place == sections - 1, first_out, after_grad)
    partner_tokens1 = mirrored(tokens1)

    part, sums = hidden_part(tokens1, weight, column_sum)
    part_b, sums_b = hidden_part(fetched1, weight, column_sum)
    got = across(
        jnp.concatenate(
            [part, slope_part(grad1, up_weight), part_b, to_all(active_b0, peers), lanes(sums + sums_b, rows)], axis=1
        )
    )
    sums = got[:, 4 * rank :]
    hidden_f1 = finish_hidden(got[:, :rank], sums[:, :6], column_sums, width)[0]
    slope1 = summed(got[:, rank : 2 * rank], peers)
    hidden_b1, mean1, inverse1 = finish_hidden(got[:, 2 * rank : 3 * rank], sums[:, 6:12], column_sums, width)
    active_b0 = got[:, 3 * rank : 4 * rank]
    up_term0 = up_term(active_b0, grad0)
    active_f1 = jax.nn.gelu(hidden_f1).astype(BF16)
    active_b1 = jax.nn.gelu(hidden_b1).astype(BF16)
    grad_hidden1 = (slope1 * gelu_slope(hidden_b1)).astype(BF16)
    stats = back_stats(grad_hidden1, hidden_b1, mean1, inverse1, column_exact, width)
    got = across(
        to_all(jnp.concatenate([active_f1, grad_hidden1, active_b1, lanes(stats, block_rows)], axis=1), peers)
    )
    stats1 = unpack_stats(got[:, 3 * rank :])
    active_f1, grad_hidden1, active_b1 = got[:, :rank], got[:, rank : 2 * rank], got[:, 2 * rank : 3 * rank]
    next_output = (tokens1.astype(F32) + jnp.dot(active_f1, up_weight, preferred_element_type=F32)).astype(BF16)
    input_grad, gain_term1, down_term1 = backward(fetched1, grad1, grad_hidden1, None, stats1, gain, down_weight)

    stash = lax.dynamic_update_index_in_dim(stash, partner_tokens0, partner_evict[0], 0)
    stash = lax.dynamic_update_index_in_dim(stash, partner_tokens1, partner_evict[1], 0)
    down_grad = (down_term0 + down_term1).astype(BF16)
    up_grad = (up_term0 + up_term(active_b1, grad1)).astype(BF16)
    return (
        next_output[None],
        input_grad[None],
        stash[None],
        (gain_term0 + gain_term1)[None],
        down_grad[None],
        up_grad[None],
    )


def solution(mesh):
    placed = (
        P("section", None, "dp"),
        P(None, "dp"),
        P("section", None, "dp"),
        P("section", None, None, "dp"),
        P("section", "dp"),
        P("section", "dp", None),
        P("section", None, "dp"),
        P(),
        P(),
    )
    return jax.shard_map(
        on_device,
        mesh=mesh,
        in_specs=placed,
        out_specs=(
            P("section", None, "dp"),
            P("section", None, "dp"),
            P("section", None, None, "dp"),
            P("section", "dp"),
            P("section", "dp", None),
            P("section", None, "dp"),
        ),
        check_vma=False,
    )
```

time: 735 us -> 186 us (0.25)
  the two profiles are of different devices: /device:TPU:1 before, /device:TPU:71 now
where the time goes in v1:
time: 186 us; the launch traced here: 185 us
  waiting for transfers between devices  68.7 us (37%)
  starting transfers between devices  46.5 us (25%)
  blocking collectives  21.9 us (12%)
  matrix products  19.3 us (10%)
  other arithmetic  10.5 us (6%)
  local copies, waits for them, and re-layouts  10.4 us (6%)
  between operations  7.7 us (4%)
    ppermute x3, waiting for transfers between devices, mirrored(): lax.ppermute(value, 'section', [(i, sections - 1 - i) for i in range(sect...  38.6 us
    all_to_all x4, waiting for transfers between devices, across(): return lax.all_to_all(block, 'dp', 0, 0, tiled=True)  26.1 us
    all_to_all x4, starting transfers between devices, across(): return lax.all_to_all(block, 'dp', 0, 0, tiled=True)  23.3 us
    all_to_all x1, blocking collectives, across(): return lax.all_to_all(block, 'dp', 0, 0, tiled=True)  21.9 us
    ppermute x3, starting transfers between devices, mirrored(): lax.ppermute(value, 'section', [(i, sections - 1 - i) for i in range(sect...  14.2 us
    ppermute x2, starting transfers between devices, shifted(): return lax.ppermute(value, 'section', pairs)  9.01 us
    dot_general x2, matrix products, up_term(): lax.dot_general(active, upstream, (((0,), (0,)), ((), ())), preferred_ele...  4.78 us
    ppermute x2, waiting for transfers between devices, shifted(): return lax.ppermute(value, 'section', pairs)  3.98 us
  transfers between devices with their start and end apart: 9, of which 8 were waited for; matrix products, arithmetic and copies ran while one was open for 8% of the time, Pallas kernels for 0%

profile of v1, /device:TPU:71, one launch (start us, length us, event | category | flops | bytes accessed | tf_op | source)
XLA Modules:
  0.0 185.0 jit_solution(3846522371497582976)
XLA Ops:
  0.7 1.1 copy.208
  3.8 1.0 pad_maximum_fusion.1
  4.8 10.4 %collective-permute-start.3 = (bf16[2,128,768]{2,1,0:T(8,128)(2,1)S(1)}, bf16[2,128,768]{2,1,0:T(8,128)(2,1)}, u32[]{:S(2)}, u32[]{:S(2)}) collective-permute-start(bf16[2,128,768]{2,1,0:T(8,128)(2,1)S(1)} %pad_maximum_fusion.1), channel_id=1, source_target_pairs={{0,496},{16,480},{32,464},{48,448},{64,432},{80,416},{96,400},{112... | collective-permute-start | bytes 1179656 | tf_op jit(solution)/shard_map/ppermute | solution.py:32
  21.5 11.2 %collective-permute-done.3 = bf16[2,128,768]{2,1,0:T(8,128)(2,1)} collective-permute-done((bf16[2,128,768]{2,1,0:T(8,128)(2,1)S(1)}, bf16[2,128,768]{2,1,0:T(8,128)(2,1)}, u32[]{:S(2)}, u32[]{:S(2)}) %collective-permute-start.3) | collective-permute-done | bytes 393248 | tf_op jit(solution)/shard_map/ppermute | solution.py:32
  32.7 1.0 fusion.66
  33.7 1.9 %collective-permute-start = (bf16[128,768]{1,0:T(8,128)(2,1)S(1)}, bf16[128,768]{1,0:T(8,128)(2,1)S(1)}, u32[]{:S(2)}, u32[]{:S(2)}) collective-permute-start(bf16[128,768]{1,0:T(8,128)(2,1)S(1)} %get-tuple-element.53), channel_id=1, source_target_pairs={{0,496},{16,480},{32,464},{48,448},{64,432},{80,416},{96,400},{112... | collective-permute-start | bytes 589832 | tf_op jit(solution)/shard_map/ppermute | solution.py:32
  35.7 1.7 fusion.46
  37.9 13.0 %collective-permute-done = bf16[128,768]{1,0:T(8,128)(2,1)S(1)} collective-permute-done((bf16[128,768]{1,0:T(8,128)(2,1)S(1)}, bf16[128,768]{1,0:T(8,128)(2,1)S(1)}, u32[]{:S(2)}, u32[]{:S(2)}) %collective-permute-start) | collective-permute-done | bytes 196640 | tf_op jit(solution)/shard_map/ppermute | solution.py:32
  52.4 8.0 %all-to-all-start.1 = ((bf16[16,8,640]{2,1,0:T(8,128)(2,1)}), bf16[16,8,640]{2,1,0:T(8,128)(2,1)S(1)}, u32[]{:S(2)}, u32[]{:S(2)}) async-start(bf16[16,8,640]{2,1,0:T(8,128)(2,1)} %fusion.82), calls=%async_computation.1 | async-start | bytes 327680 | tf_op jit(solution)/shard_map/all_to_all | solution.py:27
  61.2 7.2 %all-to-all-done.1 = bf16[16,8,640]{2,1,0:T(8,128)(2,1)S(1)} async-done(((bf16[16,8,640]{2,1,0:T(8,128)(2,1)}), bf16[16,8,640]{2,1,0:T(8,128)(2,1)S(1)}, u32[]{:S(2)}, u32[]{:S(2)}) %all-to-all-start.1) | async-done | bytes 163872 | tf_op jit(solution)/shard_map/all_to_all | solution.py:27
  68.4 4.5 %all-to-all-start = ((bf16[16,8,1664]{2,1,0:T(8,128)(2,1)}), bf16[16,8,1664]{2,1,0:T(8,128)(2,1)S(1)}, u32[]{:S(2)}, u32[]{:S(2)}) async-start(bf16[16,8,1664]{2,1,0:T(8,128)(2,1)} %pad_maximum_fusion), calls=%async_computation | async-start | bytes 851968 | tf_op jit(solution)/shard_map/all_to_all | solution.py:27
  74.1 10.0 %all-to-all-done = bf16[16,8,1664]{2,1,0:T(8,128)(2,1)S(1)} async-done(((bf16[16,8,1664]{2,1,0:T(8,128)(2,1)}), bf16[16,8,1664]{2,1,0:T(8,128)(2,1)S(1)}, u32[]{:S(2)}, u32[]{:S(2)}) %all-to-all-start) | async-done | bytes 426016 | tf_op jit(solution)/shard_map/all_to_all | solution.py:27
  87.1 5.2 %all-to-all-start.2 = ((bf16[16,8,1152]{2,1,0:T(8,128)(2,1)}), bf16[16,8,1152]{2,1,0:T(8,128)(2,1)S(1)}, u32[]{:S(2)}, u32[]{:S(2)}) async-start(bf16[16,8,1152]{2,1,0:T(8,128)(2,1)} %tile.9), calls=%async_computation.2 | async-start | bytes 589824 | tf_op jit(solution)/shard_map/all_to_all | solution.py:27
  92.4 8.9 %all-to-all-done.2 = bf16[16,8,1152]{2,1,0:T(8,128)(2,1)S(1)} async-done(((bf16[16,8,1152]{2,1,0:T(8,128)(2,1)}), bf16[16,8,1152]{2,1,0:T(8,128)(2,1)S(1)}, u32[]{:S(2)}, u32[]{:S(2)}) %all-to-all-start.2) | async-done | bytes 294944 | tf_op jit(solution)/shard_map/all_to_all | solution.py:27
  101.9 7.1 %collective-permute-start.1 = (bf16[128,768]{1,0:T(8,128)(2,1)S(1)}, bf16[128,768]{1,0:T(8,128)(2,1)S(1)}, u32[]{:S(2)}, u32[]{:S(2)}) collective-permute-start(bf16[128,768]{1,0:T(8,128)(2,1)S(1)} %fusion.4), channel_id=1, source_target_pairs={{0,16},{16,32},{32,48},{48,64},{64,80},{80,96},{96,112},{112,128},... | collective-permute-start | bytes 589832 | tf_op jit(solution)/shard_map/ppermute | solution.py:38
  109.0 1.1 fusion.43
  110.1 1.9 %collective-permute-start.2 = (bf16[128,768]{1,0:T(8,128)(2,1)}, bf16[128,768]{1,0:T(8,128)(2,1)S(1)}, u32[]{:S(2)}, u32[]{:S(2)}) collective-permute-start(bf16[128,768]{1,0:T(8,128)(2,1)} %get-tuple-element.42), channel_id=1, source_target_pairs={{16,0},{32,16},{48,32},{64,48},{80,64},{96,80},{112,96},{128,112},... | collective-permute-start | bytes 589832 | tf_op jit(solution)/shard_map/ppermute | solution.py:38
  112.0 1.7 collective-permute-done.1
  114.7 1.3 fusion.19
  116.0 2.3 %collective-permute-done.2 = bf16[128,768]{1,0:T(8,128)(2,1)S(1)} collective-permute-done((bf16[128,768]{1,0:T(8,128)(2,1)}, bf16[128,768]{1,0:T(8,128)(2,1)S(1)}, u32[]{:S(2)}, u32[]{:S(2)}) %collective-permute-start.2) | collective-permute-done | bytes 196640 | tf_op jit(solution)/shard_map/ppermute | solution.py:38
  118.7 1.3 fusion.17
  120.1 21.9 %all_to_all.48 = bf16[16,8,2176]{2,1,0:T(8,128)(2,1)S(1)} all-to-all(bf16[16,8,2176]{2,1,0:T(8,128)(2,1)S(1)} %fusion.97), channel_id=1, replica_groups=mesh['section'=32,'dp'=16] {'dp'}, dimensions={0} | all-to-all | bytes 1114112 | tf_op jit(solution)/shard_map/all_to_all | solution.py:27
  145.8 5.5 %all-to-all-start.4 = ((bf16[16,8,1664]{2,1,0:T(8,128)(2,1)}), bf16[16,8,1664]{2,1,0:T(8,128)(2,1)}, u32[]{:S(2)}, u32[]{:S(2)}) async-start(bf16[16,8,1664]{2,1,0:T(8,128)(2,1)} %tile.11), calls=%async_computation.4 | async-start | bytes 851968 | tf_op jit(solution)/shard_map/all_to_all | solution.py:27
  153.3 1.9 %collective-permute-start.4 = (bf16[128,768]{1,0:T(8,128)(2,1)}, bf16[128,768]{1,0:T(8,128)(2,1)S(1)}, u32[]{:S(2)}, u32[]{:S(2)}) collective-permute-start(bf16[128,768]{1,0:T(8,128)(2,1)} %get-tuple-element.37), channel_id=1, source_target_pairs={{0,496},{16,480},{32,464},{48,448},{64,432},{80,416},{96,400},{112... | collective-permute-start | bytes 589832 | tf_op jit(solution)/shard_map/ppermute | solution.py:32
  155.2 1.5 fusion.64
  156.7 14.3 %collective-permute-done.4 = bf16[128,768]{1,0:T(8,128)(2,1)S(1)} collective-permute-done((bf16[128,768]{1,0:T(8,128)(2,1)}, bf16[128,768]{1,0:T(8,128)(2,1)S(1)}, u32[]{:S(2)}, u32[]{:S(2)}) %collective-permute-start.4) | collective-permute-done | bytes 196640 | tf_op jit(solution)/shard_map/ppermute | solution.py:32
  171.0 2.6 %fusion.68 = f32[512,768]{1,0:T(8,128)} fusion(bf16[1,128,768]{2,1,0:T(8,128)(2,1)} %param.11, bf16[128,2176]{1,0:T(8,128)(2,1)S(1)} %bitcast.245), kind=kOutput, calls=%fused_computation.101 | convolution fusion | flops 100663296 | bytes 1900544 | tf_op jit(solution)/shard_map/dot_general | solution.py:112
  173.7 2.0 %fusion.11 = bf16[1,128,768]{2,1,0:T(8,128)(2,1)} fusion(bf16[1,512,768]{2,1,0:T(8,128)(2,1)S(1)} %copy-done, bf16[128,768]{1,0:T(8,128)(2,1)} %get-tuple-element.37, bf16[128,1664]{1,0:T(8,128)(2,1)} %bitcast.50), kind=kOutput, calls=%fused_computation.24 | convolution fusion | flops 100958208 | bytes 1310720 | tf_op jit(solution)/shard_map/dot_general | solution.py:196
  175.7 2.2 %add_reduce_fusion.3 = (f32[128]{0:T(128)S(1)}, f32[128]{0:T(128)S(1)}, f32[128]{0:T(128)S(1)}, f32[128]{0:T(128)S(1)}) fusion(bf16[128,1664]{1,0:T(8,128)(2,1)} %bitcast.50), kind=kLoop, calls=%fused_computation.138 | loop fusion | flops 2560 | bytes 5120 | tf_op jit(solution)/shard_map/add | solution.py:23
  178.0 2.0 %fusion.55 = (f32[768]{0:T(1024)S(1)}, bf16[1,128,768]{2,1,0:T(8,128)(2,1)}) fusion(bf16[128,768]{1,0:T(8,128)(2,1)S(1)} %copy-done.8, f32[128]{0:T(128)S(1)} %get-tuple-element.15, f32[128]{0:T(128)S(1)} %get-tuple-element.13, f32[128]{0:T(128)S(1)} %get-tuple-element.16, f32[128]{0:T(128)S(1)} %get-tuple-element.14, f32[768]{0:T(1024)S(1)} %convert_reduce_fusion.10, ...), kind=kOutput, calls=%fused_computation.83 | convolution fusion | flops 101940480 | bytes 1515520 | tf_op jit(solution)/shard_map/dot_general | solution.py:103
  180.6 2.3 %fusion.2 = bf16[1,768,512]{2,1,0:T(8,128)(2,1)} fusion(f32[768,512]{1,0:T(8,128)S(1)} %fusion.64, bf16[128,768]{1,0:T(8,128)(2,1)S(1)} %copy-done.8, f32[128]{0:T(128)S(1)} %get-tuple-element.15, f32[128]{0:T(128)S(1)} %get-tuple-element.13, f32[768]{0:T(1024)S(1)} %convert_reduce_fusion.10, bf16[128,1664]{1,0:T(8,128)(2,1)} %bitcast.50), kind=kOutput, calls=%fused_computation.7 | convolution fusion | flops 101941248 | bytes 2691072 | tf_op jit(solution)/shard_map/dot_general | solution.py:107
  182.8 2.2 %fusion.3 = bf16[1,512,768]{2,1,0:T(8,128)(2,1)} fusion(f32[512,768]{1,0:T(8,128)S(1)} %copy-done.1, bf16[128,768]{1,0:T(8,128)(2,1)S(1)} %broadcast_select_fusion, bf16[128,1664]{1,0:T(8,128)(2,1)} %bitcast.50), kind=kOutput, calls=%fused_computation.8 | convolution fusion | flops 101449728 | bytes 2686976 | tf_op jit(solution)/shard_map/dot_general | solution.py:112
  (164 shorter events, 16.9 us)
Async XLA Ops:
  0.6 20.5 %copy-start = (bf16[1,512,768]{2,1,0:T(8,128)(2,1)S(1)}, bf16[1,512,768]{2,1,0:T(8,128)(2,1)}, u32[]{:S(2)}) copy-start(bf16[1,512,768]{2,1,0:T(8,128)(2,1)} %param.15) | copy-start | bytes 2359300
  0.6 20.5 %copy-start.9 = (bf16[1,128,768]{2,1,0:T(8,128)(2,1)S(1)}, bf16[1,128,768]{2,1,0:T(8,128)(2,1)}, u32[]{:S(2)}) copy-start(bf16[1,128,768]{2,1,0:T(8,128)(2,1)} %param.11) | copy-start | bytes 589828
  0.7 14.5 %copy-start.11 = (bf16[1,768]{1,0:T(2,128)(2,1)S(1)}, bf16[1,768]{1,0:T(2,128)(2,1)}, u32[]{:S(2)}) copy-start(bf16[1,768]{1,0:T(2,128)(2,1)} %param.13) | copy-start | bytes 4612
  0.7 14.6 %copy-start.6 = (bf16[1,768,512]{2,1,0:T(8,128)(2,1)S(1)}, bf16[1,768,512]{2,1,0:T(8,128)(2,1)}, u32[]{:S(2)}) copy-start(bf16[1,768,512]{2,1,0:T(8,128)(2,1)} %param.14) | copy-start | bytes 2359300
  4.8 30.8 %copy-start.4 = (bf16[1,128,768]{2,1,0:T(8,128)(2,1)S(1)}, bf16[1,128,768]{2,1,0:T(8,128)(2,1)}, u32[]{:S(2)}) copy-start(bf16[1,128,768]{2,1,0:T(8,128)(2,1)} %param.9) | copy-start | bytes 589828
  4.8 27.9 %collective-permute-start.3 = (bf16[2,128,768]{2,1,0:T(8,128)(2,1)S(1)}, bf16[2,128,768]{2,1,0:T(8,128)(2,1)}, u32[]{:S(2)}, u32[]{:S(2)}) collective-permute-start(bf16[2,128,768]{2,1,0:T(8,128)(2,1)S(1)} %pad_maximum_fusion.1), channel_id=1, source_target_pairs={{0,496},{16,480},{32,464},{48,448},{64,432},{80,416},{96,400},{112... | collective-permute-start | bytes 1179656 | tf_op jit(solution)/shard_map/ppermute | solution.py:32
  33.7 17.2 %collective-permute-start = (bf16[128,768]{1,0:T(8,128)(2,1)S(1)}, bf16[128,768]{1,0:T(8,128)(2,1)S(1)}, u32[]{:S(2)}, u32[]{:S(2)}) collective-permute-start(bf16[128,768]{1,0:T(8,128)(2,1)S(1)} %get-tuple-element.53), channel_id=1, source_target_pairs={{0,496},{16,480},{32,464},{48,448},{64,432},{80,416},{96,400},{112... | collective-permute-start | bytes 589832 | tf_op jit(solution)/shard_map/ppermute | solution.py:32
  51.0 59.2 %copy-start.5 = (bf16[128,768]{1,0:T(8,128)(2,1)}, bf16[128,768]{1,0:T(8,128)(2,1)S(1)}, u32[]{:S(2)}) copy-start(bf16[128,768]{1,0:T(8,128)(2,1)S(1)} %collective-permute-done) | copy-start | bytes 589828
  52.4 16.0 %all-to-all-start.1 = ((bf16[16,8,640]{2,1,0:T(8,128)(2,1)}), bf16[16,8,640]{2,1,0:T(8,128)(2,1)S(1)}, u32[]{:S(2)}, u32[]{:S(2)}) async-start(bf16[16,8,640]{2,1,0:T(8,128)(2,1)} %fusion.82), calls=%async_computation.1 | async-start | bytes 327680 | tf_op jit(solution)/shard_map/all_to_all | solution.py:27
  68.4 15.8 %all-to-all-start = ((bf16[16,8,1664]{2,1,0:T(8,128)(2,1)}), bf16[16,8,1664]{2,1,0:T(8,128)(2,1)S(1)}, u32[]{:S(2)}, u32[]{:S(2)}) async-start(bf16[16,8,1664]{2,1,0:T(8,128)(2,1)} %pad_maximum_fusion), calls=%async_computation | async-start | bytes 851968 | tf_op jit(solution)/shard_map/all_to_all | solution.py:27
  87.1 14.2 %all-to-all-start.2 = ((bf16[16,8,1152]{2,1,0:T(8,128)(2,1)}), bf16[16,8,1152]{2,1,0:T(8,128)(2,1)S(1)}, u32[]{:S(2)}, u32[]{:S(2)}) async-start(bf16[16,8,1152]{2,1,0:T(8,128)(2,1)} %tile.9), calls=%async_computation.2 | async-start | bytes 589824 | tf_op jit(solution)/shard_map/all_to_all | solution.py:27
  101.3 8.8 %copy-start.3 = (bf16[16,8,1152]{2,1,0:T(8,128)(2,1)}, bf16[16,8,1152]{2,1,0:T(8,128)(2,1)S(1)}, u32[]{:S(2)}) copy-start(bf16[16,8,1152]{2,1,0:T(8,128)(2,1)S(1)} %all-to-all-done.2) | copy-start | bytes 884740
  101.3 12.4 %copy-start.10 = (bf16[128,768]{1,0:T(8,128)(2,1)S(1)}, bf16[128,768]{1,0:T(8,128)(2,1)}, u32[]{:S(2)}) copy-start(bf16[128,768]{1,0:T(8,128)(2,1)} %param.10) | copy-start | bytes 589828
  101.9 11.8 %collective-permute-start.1 = (bf16[128,768]{1,0:T(8,128)(2,1)S(1)}, bf16[128,768]{1,0:T(8,128)(2,1)S(1)}, u32[]{:S(2)}, u32[]{:S(2)}) collective-permute-start(bf16[128,768]{1,0:T(8,128)(2,1)S(1)} %fusion.4), channel_id=1, source_target_pairs={{0,16},{16,32},{32,48},{48,64},{64,80},{80,96},{96,112},{112,128},... | collective-permute-start | bytes 589832 | tf_op jit(solution)/shard_map/ppermute | solution.py:38
  110.1 8.2 %collective-permute-start.2 = (bf16[128,768]{1,0:T(8,128)(2,1)}, bf16[128,768]{1,0:T(8,128)(2,1)S(1)}, u32[]{:S(2)}, u32[]{:S(2)}) collective-permute-start(bf16[128,768]{1,0:T(8,128)(2,1)} %get-tuple-element.42), channel_id=1, source_target_pairs={{16,0},{32,16},{48,32},{64,48},{80,64},{96,80},{112,96},{128,112},... | collective-permute-start | bytes 589832 | tf_op jit(solution)/shard_map/ppermute | solution.py:38
  145.8 27.8 %all-to-all-start.4 = ((bf16[16,8,1664]{2,1,0:T(8,128)(2,1)}), bf16[16,8,1664]{2,1,0:T(8,128)(2,1)}, u32[]{:S(2)}, u32[]{:S(2)}) async-start(bf16[16,8,1664]{2,1,0:T(8,128)(2,1)} %tile.11), calls=%async_computation.4 | async-start | bytes 851968 | tf_op jit(solution)/shard_map/all_to_all | solution.py:27
  153.3 17.7 %collective-permute-start.4 = (bf16[128,768]{1,0:T(8,128)(2,1)}, bf16[128,768]{1,0:T(8,128)(2,1)S(1)}, u32[]{:S(2)}, u32[]{:S(2)}) collective-permute-start(bf16[128,768]{1,0:T(8,128)(2,1)} %get-tuple-element.37), channel_id=1, source_target_pairs={{0,496},{16,480},{32,464},{48,448},{64,432},{80,416},{96,400},{112... | collective-permute-start | bytes 589832 | tf_op jit(solution)/shard_map/ppermute | solution.py:32
  171.0 4.7 %copy-start.2 = (bf16[1,2,128,768]{3,2,1,0:T(8,128)(2,1)}, bf16[1,2,128,768]{3,2,1,0:T(8,128)(2,1)S(1)}, u32[]{:S(2)}) copy-start(bf16[1,2,128,768]{3,2,1,0:T(8,128)(2,1)S(1)} %bitcast_dynamic-update-slice_fusion) | copy-start | bytes 1179652
  173.7 4.3 %copy-start.8 = (bf16[128,768]{1,0:T(8,128)(2,1)S(1)}, bf16[128,768]{1,0:T(8,128)(2,1)}, u32[]{:S(2)}) copy-start(bf16[128,768]{1,0:T(8,128)(2,1)} %get-tuple-element.36) | copy-start | bytes 589828
  173.7 4.3 %copy-start.7 = (bf16[1,768,512]{2,1,0:T(8,128)(2,1)S(1)}, bf16[1,768,512]{2,1,0:T(8,128)(2,1)}, u32[]{:S(2)}) copy-start(bf16[1,768,512]{2,1,0:T(8,128)(2,1)} %param.14) | copy-start | bytes 2359300
  180.0 2.9 %copy-start.1 = (f32[512,768]{1,0:T(8,128)S(1)}, f32[512,768]{1,0:T(8,128)}, u32[]{:S(2)}) copy-start(f32[512,768]{1,0:T(8,128)} %fusion.68) | copy-start | bytes 4718596

commit v2 on v1

v2 whole, which is shorter than its diff:
```python
import math

import jax
import jax.numpy as jnp
from jax import lax
from jax.experimental import pallas as pl
from jax.experimental.pallas import tpu as pltpu
from jax.sharding import PartitionSpec as P

BF16 = jnp.bfloat16
F32 = jnp.float32
EPS = 1e-05
LANES = 128
ROOT = math.sqrt(2 / math.pi)
CUBE = 0.044715


def across(block):
    return lax.all_to_all(block, "dp", 0, 0, tiled=True)


def mirrored(value):
    sections = lax.axis_size("section")
    return lax.ppermute(value, "section", [(i, sections - 1 - i) for i in range(sections)])


def shifted(value, by):
    sections = lax.axis_size("section")
    pairs = [(i, i + by) for i in range(sections) if 0 <= i + by < sections]
    return lax.ppermute(value, "section", pairs)


def pieces(value):
    high = value.astype(BF16).astype(F32)
    middle = (value - high).astype(BF16).astype(F32)
    return [high, middle, value - high - middle]


def in_lanes(columns):
    rows = columns[0].shape[0]
    lane = lax.broadcasted_iota(jnp.int32, (rows, LANES), 1)
    block = jnp.zeros((rows, LANES), F32)
    for i, column in enumerate(columns):
        block = jnp.where(lane == i, column, block)
    return block


def from_lanes(block, first):
    lane = lax.broadcasted_iota(jnp.int32, block.shape, 1)
    return jnp.sum(jnp.where((lane >= first) & (lane < first + 3), block, 0.0), axis=1, keepdims=True)


def row_sums(values):
    one = jnp.sum(values, axis=1, keepdims=True)
    two = jnp.sum(values * values, axis=1, keepdims=True)
    return one, two


def hidden_part(tokens, weight, column_sum):
    values = tokens.astype(F32)
    one, two = row_sums(values)
    part = jnp.dot(tokens, weight, preferred_element_type=F32)
    return part - (one / values.shape[1]) * column_sum, pieces(one) + pieces(two)


def times_transposed(left, right):
    return lax.dot_general(left, right, (((1,), (1,)), ((), ())), preferred_element_type=F32)


def transposed_times(left, right):
    return lax.dot_general(left, right, (((0,), (0,)), ((), ())), preferred_element_type=F32)


def summed(block, peers):
    return jnp.sum(block.astype(F32).reshape(peers, -1, block.shape[1]), axis=0)


def finish_hidden(part, sums, first, column_sums, width):
    peers = len(column_sums)
    one = from_lanes(sums, first).reshape(peers, -1, 1)
    two = from_lanes(sums, first + 3).reshape(peers, -1, 1)
    mean = jnp.sum(one, axis=0) / width
    inverse = lax.rsqrt(jnp.sum(two, axis=0) / width - mean * mean + EPS)
    total = summed(part, peers)
    for peer in range(peers):
        total = total + (one[peer] / (width // peers) - mean) * column_sums[peer]
    return total * inverse, mean, inverse


def gelu(hidden):
    return hidden * (0.5 * (1.0 + jnp.tanh(ROOT * (hidden + CUBE * (hidden * hidden * hidden)))))


def gelu_and_slope(hidden):
    bent = jnp.tanh(ROOT * (hidden + CUBE * (hidden * hidden * hidden)))
    half = 0.5 * (1.0 + bent)
    slope = half + hidden * (0.5 * (1.0 - bent * bent)) * (ROOT * (1.0 + 3.0 * CUBE * (hidden * hidden)))
    return hidden * half, slope


def back_stats(grad_hidden, hidden, mean, inverse, column_exact, width):
    grad = grad_hidden.astype(F32)
    first = jnp.sum(grad * column_exact, axis=1, keepdims=True) / width
    second = jnp.sum(grad * hidden, axis=1, keepdims=True) / width
    return in_lanes(pieces(mean) + pieces(inverse) + pieces(first) + pieces(second))


def to_all(block, peers):
    rows, columns = block.shape
    return jnp.broadcast_to(block[None], (peers, rows, columns)).reshape(peers * rows, columns).astype(BF16)


def backward(tokens, upstream, grad_hidden, sums, gain, down_weight):
    mean, inverse, first, second = [from_lanes(sums, 3 * i) for i in range(4)]
    normed = (tokens.astype(F32) - mean) * inverse
    grad_scaled = times_transposed(grad_hidden, down_weight)
    grad_rows = inverse * (grad_scaled * gain - first - normed * second)
    tokens_grad = (upstream.astype(F32) + grad_rows).astype(BF16)
    gain_term = jnp.sum(grad_scaled * normed, axis=0, keepdims=True)
    return tokens_grad, (normed * gain).astype(BF16), gain_term


def start_kernel(tokens, upstream, gain, down, up, payload, weight, column_sum, *, peers, rank):
    rows = tokens.shape[0]
    features = tokens.shape[1]
    tall = jnp.broadcast_to(gain[...].astype(F32), (LANES, features)).T
    exact = down[...].astype(F32) * jnp.concatenate([tall] * (rank // LANES), axis=1)
    rounded = exact.astype(BF16)
    weight[...] = rounded
    one = jnp.sum(rounded.astype(F32), axis=0, keepdims=True)
    column_sum[...] = one
    two = jnp.sum(exact, axis=0, keepdims=True)
    row = lax.broadcasted_iota(jnp.int32, (rows // peers, rank), 0)
    block = jnp.zeros((rows // peers, rank), F32)
    for i, piece in enumerate(pieces(one) + pieces(two)):
        block = jnp.where(row == i, piece, block)
    part, sums = hidden_part(tokens[...], rounded, one)
    payload[:, :rank] = part.astype(BF16)
    payload[:, rank : 2 * rank] = times_transposed(upstream[...], up[...]).astype(BF16)
    payload[:, 2 * rank : 3 * rank] = to_all(block, peers)
    payload[:, 3 * rank :] = in_lanes(sums).astype(BF16)


def fetched_kernel(tokens, weight, column_sum, payload, zero, *, rank):
    part, sums = hidden_part(tokens[...], weight[...], column_sum[...])
    payload[:, :rank] = part.astype(BF16)
    payload[:, rank:] = in_lanes(sums).astype(BF16)
    zero[0] = 0


def middle_kernel(got_a, got_b, payload, columns, active_back, *, peers, rank, width):
    blocks = got_a[:, 2 * rank : 3 * rank].astype(F32).reshape(peers, -1, rank)
    row = lax.broadcasted_iota(jnp.int32, blocks.shape[1:], 0)
    column_sums, column_exact = [], jnp.zeros(blocks.shape[1:], F32)
    for peer in range(peers):
        column_sums.append(jnp.sum(jnp.where(row < 3, blocks[peer], 0.0), axis=0, keepdims=True))
        columns[peer : peer + 1, :] = column_sums[peer]
        column_exact = column_exact + jnp.where((row >= 3) & (row < 6), blocks[peer], 0.0)
    column_exact = jnp.sum(column_exact, axis=0, keepdims=True)
    columns[peers : peers + 1, :] = column_exact
    hidden_f = finish_hidden(got_a[:, :rank], got_a[:, 3 * rank :].astype(F32), 0, column_sums, width)[0]
    slope = summed(got_a[:, rank : 2 * rank], peers)
    hidden, mean, inverse = finish_hidden(got_b[:, :rank], got_b[:, rank:].astype(F32), 0, column_sums, width)
    active, bent = gelu_and_slope(hidden)
    active_back[...] = active.astype(BF16).astype(F32)
    grad_hidden = (slope * bent).astype(BF16)
    payload[:, :rank] = to_all(gelu(hidden_f), peers)
    payload[:, rank : 2 * rank] = to_all(grad_hidden.astype(F32), peers)
    payload[:, 2 * rank :] = to_all(back_stats(grad_hidden, hidden, mean, inverse, column_exact, width), peers)


def first_kernel(got, tokens, fetched, upstream, gain, down, up, out, grad, scaled, gain_term, *, rank):
    out[...] = (
        tokens[...].astype(F32) + jnp.dot(got[:, :rank], up[...], preferred_element_type=F32)
    ).astype(BF16)
    grad[...], scaled[...], gain_term[...] = backward(
        fetched[...], upstream[...], got[:, rank : 2 * rank], got[:, 2 * rank :].astype(F32), gain[...].astype(F32), down[...]
    )


def side_kernel(flag, arrived, tokens, weight, column_sum, active_back, payload, fetched, *, peers, rank):
    chosen = jnp.where(flag[0] == 1, tokens[...], arrived[...])
    fetched[...] = chosen
    part, sums = hidden_part(chosen, weight[...], column_sum[...])
    payload[:, :rank] = part.astype(BF16)
    payload[:, rank : 2 * rank] = to_all(active_back[...], peers)
    payload[:, 2 * rank :] = in_lanes(sums).astype(BF16)


def second_kernel(before, after, fresh, own, weight, column_sum, up, payload, tokens, upstream, *, rank):
    place = lax.axis_index("section")
    tokens[...] = jnp.where(place == 0, fresh[...], before[...])
    upstream[...] = jnp.where(place == lax.axis_size("section") - 1, own[...], after[...])
    part, sums = hidden_part(tokens[...], weight[...], column_sum[...])
    payload[:, :rank] = part.astype(BF16)
    payload[:, rank : 2 * rank] = times_transposed(upstream[...], up[...]).astype(BF16)
    payload[:, 2 * rank :] = in_lanes(sums).astype(BF16)


def late_kernel(got, side, columns, payload, *, peers, rank, width):
    column_sums = [columns[peer : peer + 1, :] for peer in range(peers)]
    hidden_f = finish_hidden(got[:, :rank], got[:, 2 * rank :].astype(F32), 0, column_sums, width)[0]
    slope = summed(got[:, rank : 2 * rank], peers)
    hidden, mean, inverse = finish_hidden(side[:, :rank], side[:, 2 * rank :].astype(F32), 0, column_sums, width)
    active, bent = gelu_and_slope(hidden)
    grad_hidden = (slope * bent).astype(BF16)
    payload[:, :rank] = to_all(gelu(hidden_f), peers)
    payload[:, rank : 2 * rank] = to_all(grad_hidden.astype(F32), peers)
    payload[:, 2 * rank : 3 * rank] = to_all(active, peers)
    stats = back_stats(grad_hidden, hidden, mean, inverse, columns[peers : peers + 1, :], width)
    payload[:, 3 * rank :] = to_all(stats, peers)


def last_kernel(
    got, got0, side, tokens, fetched, upstream, upstream0, scaled0, gain_term0, gain, down, up,
    out, grad, gain_grad, down_grad, up_grad, *, rank
):
    out[...] = (
        tokens[...].astype(F32) + jnp.dot(got[:, :rank], up[...], preferred_element_type=F32)
    ).astype(BF16)
    grad[...], scaled, gain_term = backward(
        fetched[...], upstream[...], got[:, rank : 2 * rank], got[:, 3 * rank :].astype(F32), gain[...].astype(F32), down[...]
    )
    gain_grad[...] = gain_term0[...] + gain_term
    down_grad[...] = transposed_times(
        jnp.concatenate([scaled0[...], scaled], axis=0),
        jnp.concatenate([got0[:, rank : 2 * rank], got[:, rank : 2 * rank]], axis=0),
    ).astype(BF16)
    up_grad[...] = transposed_times(
        jnp.concatenate([side[:, rank : 2 * rank], got[:, 2 * rank : 3 * rank]], axis=0),
        jnp.concatenate([upstream0[...], upstream[...]], axis=0),
    ).astype(BF16)


def call(body, outs, operands, products=1, smem=(), name=None):
    spaces = [pltpu.SMEM if i in smem else pltpu.VMEM for i in range(len(operands))]
    moved = sum(math.prod(o.shape) * o.dtype.itemsize for o in list(outs) + list(operands))
    results = pl.pallas_call(
        body,
        out_shape=tuple(outs),
        in_specs=[pl.BlockSpec(memory_space=s) for s in spaces],
        out_specs=tuple(pl.BlockSpec(memory_space=pltpu.SMEM if o.dtype == jnp.int32 else pltpu.VMEM) for o in outs),
        compiler_params=pltpu.CompilerParams(vmem_limit_bytes=40 * 2**20),
        cost_estimate=pl.CostEstimate(flops=products * 2 * 128 * 768 * 512, bytes_accessed=moved, transcendentals=0),
        name=name,
    )(*operands)
    return results


def bound(body, **sizes):
    def run(*refs):
        body(*refs, **sizes)

    return run


def on_device(layer_input, fresh_input, out_grad, held_stash, norm_gain, down_proj, up_proj, fetch_slot, evict_slot):
    sections = lax.axis_size("section")
    peers = lax.axis_size("dp")
    place = lax.axis_index("section")
    partner = sections - 1 - place
    tokens0, grad0, stash = layer_input[0], out_grad[0], held_stash[0]
    down, up = down_proj[0], up_proj[0]
    rows, features = tokens0.shape
    rank = up.shape[0]
    width = features * peers
    own = rows // peers

    def shape(*dims, dtype=BF16):
        return jax.ShapeDtypeStruct(dims, dtype)

    partner_fetch = lax.dynamic_slice(fetch_slot, (partner, 0), (1, 2))[0]
    partner_evict = lax.dynamic_slice(evict_slot, (partner, 0), (1, 2))[0]
    own_fetch = lax.dynamic_slice(fetch_slot, (place, 0), (1, 2))[0]
    own_evict = lax.dynamic_slice(evict_slot, (place, 0), (1, 2))[0]
    same = (own_fetch[1:] == own_evict[:1]).astype(jnp.int32)

    fetched0 = mirrored(jnp.where(partner_fetch[0] == 0, stash[0], stash[1]))
    payload, weight, column_sum = call(
        bound(start_kernel, peers=peers, rank=rank),
        [shape(rows, 3 * rank + LANES), shape(features, rank), shape(1, rank, dtype=F32)],
        [tokens0, grad0, norm_gain, down, up],
        products=2,
        name="start",
    )
    got_a = across(payload)
    payload, zero = call(
        bound(fetched_kernel, rank=rank),
        [shape(rows, rank + LANES), shape(1, dtype=jnp.int32)],
        [fetched0, weight, column_sum],
        name="fetched",
    )
    got_b = across(payload)
    both = mirrored(jnp.stack([jnp.where(partner_fetch[1] + zero[0] == 0, stash[0], stash[1]), tokens0], 0))
    payload, columns, active_back = call(
        bound(middle_kernel, peers=peers, rank=rank, width=width),
        [shape(rows, 2 * rank + LANES), shape(peers + 8, rank, dtype=F32), shape(own, rank, dtype=F32)],
        [got_a, got_b],
        name="middle",
    )
    got0 = across(payload)
    first_out, first_grad, scaled0, gain_term0 = call(
        bound(first_kernel, rank=rank),
        [shape(rows, features), shape(rows, features), shape(rows, features), shape(1, features, dtype=F32)],
        [got0, tokens0, fetched0, grad0, norm_gain, down, up],
        products=2,
        name="first",
    )
    before_out = shifted(first_out, 1)
    after_grad = shifted(first_grad, -1)
    payload, fetched1 = call(
        bound(side_kernel, peers=peers, rank=rank),
        [shape(rows, 2 * rank + LANES), shape(rows, features)],
        [same, both[0], tokens0, weight, column_sum, active_back],
        smem=(0,),
        name="side",
    )
    side = across(payload)
    payload, tokens1, grad1 = call(
        bound(second_kernel, rank=rank),
        [shape(rows, 2 * rank + LANES), shape(rows, features), shape(rows, features)],
        [before_out, after_grad, fresh_input, first_out, weight, column_sum, up],
        products=2,
        name="second",
    )
    got = across(payload)
    partner_tokens1 = mirrored(tokens1)
    (payload,) = call(
        bound(late_kernel, peers=peers, rank=rank, width=width),
        [shape(rows, 3 * rank + LANES)],
        [got, side, columns],
        name="late",
    )
    got1 = across(payload)
    next_output, input_grad, gain_grad, down_grad, up_grad = call(
        bound(last_kernel, rank=rank),
        [
            shape(rows, features),
            shape(rows, features),
            shape(1, features, dtype=F32),
            shape(features, rank),
            shape(rank, features),
        ],
        [got1, got0, side, tokens1, fetched1, grad1, grad0, scaled0, gain_term0, norm_gain, down, up],
        products=6,
        name="last",
    )
    slots = lax.broadcasted_iota(jnp.int32, (stash.shape[0], 1, 1), 0)
    stash = jnp.where(slots == partner_evict[0], both[1][None], stash)
    stash = jnp.where(slots == partner_evict[1], partner_tokens1[None], stash)
    return (next_output[None], input_grad[None], stash[None], gain_grad, down_grad[None], up_grad[None])


def solution(mesh):
    placed = (
        P("section", None, "dp"),
        P(None, "dp"),
        P("section", None, "dp"),
        P("section", None, None, "dp"),
        P("section", "dp"),
        P("section", "dp", None),
        P("section", None, "dp"),
        P(),
        P(),
    )
    return jax.shard_map(
        on_device,
        mesh=mesh,
        in_specs=placed,
        out_specs=(
            P("section", None, "dp"),
            P("section", None, "dp"),
            P("section", None, None, "dp"),
            P("section", "dp"),
            P("section", "dp", None),
            P("section", None, "dp"),
        ),
        check_vma=False,
    )
```

time: 186 us -> 147 us (0.79)
  the two profiles are of different devices: /device:TPU:71 before, /device:TPU:129 now
where the time goes in v2:
time: 147 us; the launch traced here: 146 us
  starting transfers between devices  56.7 us (39%)
  blocking collectives  35.5 us (24%)
  waiting for transfers between devices  25.9 us (18%)
  local copies, waits for them, and re-layouts  12.2 us (8%)
  Pallas kernels  6.85 us (5%)
  other arithmetic  4.43 us (3%)
  between operations  4.19 us (3%)
    all_to_all x2, blocking collectives, across(): return lax.all_to_all(block, 'dp', 0, 0, tiled=True)  35.5 us
    ppermute x3, starting transfers between devices, mirrored(): lax.ppermute(value, 'section', [(i, sections - 1 - i) for i in range(sect...  27 us
    all_to_all x4, starting transfers between devices, across(): return lax.all_to_all(block, 'dp', 0, 0, tiled=True)  21.4 us
    ppermute x3, waiting for transfers between devices, mirrored(): lax.ppermute(value, 'section', [(i, sections - 1 - i) for i in range(sect...  16.8 us
    unnamed x48, local copies, waits for them, and re-layouts  9.34 us
    ppermute x2, starting transfers between devices, shifted(): return lax.ppermute(value, 'section', pairs)  8.28 us
    ppermute x2, waiting for transfers between devices, shifted(): return lax.ppermute(value, 'section', pairs)  7.32 us
    pallas_call x8, Pallas kernels, call(): pl.pallas_call(body, out_shape=tuple(outs), in_specs=[pl.BlockSpec(memory...  6.85 us
  transfers between devices with their start and end apart: 9, of which 7 were waited for; matrix products, arithmetic and copies ran while one was open for 4% of the time, Pallas kernels for 3%

profile of v2, /device:TPU:129, one launch (start us, length us, event | category | flops | bytes accessed | tf_op | source)
XLA Modules:
  0.0 145.8 jit_solution(8485460401641346075)
XLA Ops:
  2.6 1.1 select_bitcast_fusion.1
  3.7 9.8 %collective-permute-start = (bf16[128,768]{1,0:T(8,128)(2,1)S(1)}, bf16[128,768]{1,0:T(8,128)(2,1)S(1)}, u32[]{:S(2)}, u32[]{:S(2)}) collective-permute-start(bf16[128,768]{1,0:T(8,128)(2,1)S(1)} %select_bitcast_fusion.1), channel_id=1, source_target_pairs={{0,496},{16,480},{32,464},{48,448},{64,432},{80,416},{96,400},{112... | collective-permute-start | bytes 589832 | tf_op jit(solution)/shard_map/ppermute | solution.py:24
  14.2 1.1 copy-done
  15.3 1.1 copy-done.2
  16.4 1.6 %start.1 = (bf16[128,1664]{1,0:T(8,128)(2,1)}, bf16[768,512]{1,0:T(8,128)(2,1)S(1)}, f32[1,512]{1,0:T(1,128)S(1)}) custom-call(bf16[128,768]{1,0:T(8,128)(2,1)S(1)} %bitcast.41, bf16[128,768]{1,0:T(8,128)(2,1)S(1)} %bitcast.48, bf16[1,768]{1,0:T(2,128)(2,1)S(1)} %copy-done.20, bf16[768,512]{1,0:T(8,128)(2,1)S(1)} %bitcast.38, bf16[512,768]{1,0:T(8,128)(2,1)S(1)} %bitcast.34), custom_call_target="tpu_custom_call" | custom-call | flops 201326592 | bytes 3182080 | tf_op jit(solution)/shard_map/start/pallas_call | solution.py:238
  18.0 4.3 %collective-permute-done.refs_0_.refs_2_ = bf16[128,768]{1,0:T(8,128)(2,1)S(1)} collective-permute-done((bf16[128,768]{1,0:T(8,128)(2,1)S(1)}, bf16[128,768]{1,0:T(8,128)(2,1)S(1)}, u32[]{:S(2)}, u32[]{:S(2)}) %collective-permute-start) | collective-permute-done | bytes 196640 | tf_op jit(solution)/shard_map/ppermute | solution.py:24
  22.9 16.8 %all_to_all.66 = bf16[16,8,640]{2,1,0:T(8,128)(2,1)S(1)} all-to-all(bf16[16,8,640]{2,1,0:T(8,128)(2,1)S(1)} %bitcast.58), channel_id=1, replica_groups=mesh['section'=32,'dp'=16] {'dp'}, dimensions={0} | all-to-all | bytes 327680 | tf_op jit(solution)/shard_map/all_to_all | solution.py:19
  39.8 3.7 %all-to-all-start = ((bf16[16,8,1664]{2,1,0:T(8,128)(2,1)}), bf16[16,8,1664]{2,1,0:T(8,128)(2,1)S(1)}, u32[]{:S(2)}, u32[]{:S(2)}) async-start(bf16[16,8,1664]{2,1,0:T(8,128)(2,1)} %bitcast.4), calls=%async_computation | async-start | bytes 851968 | tf_op jit(solution)/shard_map/all_to_all | solution.py:19
  44.9 10.3 %collective-permute-start.3 = (bf16[2,128,768]{2,1,0:T(8,128)(2,1)S(1)}, bf16[2,128,768]{2,1,0:T(8,128)(2,1)S(1)}, u32[]{:S(2)}, u32[]{:S(2)}) collective-permute-start(bf16[2,128,768]{2,1,0:T(8,128)(2,1)S(1)} %pad_maximum_fusion), channel_id=1, source_target_pairs={{0,496},{16,480},{32,464},{48,448},{64,432},{80,416},{96,400},{112... | collective-permute-start | bytes 1179656 | tf_op jit(solution)/shard_map/ppermute | solution.py:24
  55.2 1.2 all-to-all-done
  56.4 1.0 middle.1
  58.0 6.6 %all-to-all-start.2 = ((bf16[16,8,1152]{2,1,0:T(8,128)(2,1)}), bf16[16,8,1152]{2,1,0:T(8,128)(2,1)S(1)}, u32[]{:S(2)}, u32[]{:S(2)}) async-start(bf16[16,8,1152]{2,1,0:T(8,128)(2,1)} %bitcast.10), calls=%async_computation.2 | async-start | bytes 589824 | tf_op jit(solution)/shard_map/all_to_all | solution.py:19
  66.9 6.7 %collective-permute-done.3 = bf16[2,128,768]{2,1,0:T(8,128)(2,1)S(1)} collective-permute-done((bf16[2,128,768]{2,1,0:T(8,128)(2,1)S(1)}, bf16[2,128,768]{2,1,0:T(8,128)(2,1)S(1)}, u32[]{:S(2)}, u32[]{:S(2)}) %collective-permute-start.3) | collective-permute-done | bytes 393248 | tf_op jit(solution)/shard_map/ppermute | solution.py:24
  73.6 0.7 slice_bitcast_fusion
  74.7 0.7 copy-done.7
  75.4 0.7 copy-done.9
  76.6 7.5 %all-to-all-start.4 = ((bf16[16,8,1152]{2,1,0:T(8,128)(2,1)}), bf16[16,8,1152]{2,1,0:T(8,128)(2,1)S(1)}, u32[]{:S(2)}, u32[]{:S(2)}) async-start(bf16[16,8,1152]{2,1,0:T(8,128)(2,1)} %bitcast.56), calls=%async_computation.4 | async-start | bytes 589824 | tf_op jit(solution)/shard_map/all_to_all | solution.py:19
  84.7 0.7 copy-done.11
  85.4 6.4 %collective-permute-start.1 = (bf16[128,768]{1,0:T(8,128)(2,1)S(1)}, bf16[128,768]{1,0:T(8,128)(2,1)S(1)}, u32[]{:S(2)}, u32[]{:S(2)}) collective-permute-start(bf16[128,768]{1,0:T(8,128)(2,1)S(1)} %get-tuple-element.33.refs_3_), channel_id=1, source_target_pairs={{0,16},{16,32},{32,48},{48,64},{64,80},{80,96},{96,112},{112,128},... | collective-permute-start | bytes 589832 | tf_op jit(solution)/shard_map/ppermute | solution.py:30
  91.7 1.9 %collective-permute-start.2 = (bf16[128,768]{1,0:T(8,128)(2,1)S(1)}, bf16[128,768]{1,0:T(8,128)(2,1)S(1)}, u32[]{:S(2)}, u32[]{:S(2)}) collective-permute-start(bf16[128,768]{1,0:T(8,128)(2,1)S(1)} %get-tuple-element.34), channel_id=1, source_target_pairs={{16,0},{32,16},{48,32},{64,48},{80,64},{96,80},{112,96},{128,112},... | collective-permute-start | bytes 589832 | tf_op jit(solution)/shard_map/ppermute | solution.py:30
  93.6 3.3 %collective-permute-done.1.refs_0_ = bf16[128,768]{1,0:T(8,128)(2,1)S(1)} collective-permute-done((bf16[128,768]{1,0:T(8,128)(2,1)S(1)}, bf16[128,768]{1,0:T(8,128)(2,1)S(1)}, u32[]{:S(2)}, u32[]{:S(2)}) %collective-permute-start.1) | collective-permute-done | bytes 196640 | tf_op jit(solution)/shard_map/ppermute | solution.py:30
  96.9 4.0 %collective-permute-done.2.refs_1_ = bf16[128,768]{1,0:T(8,128)(2,1)S(1)} collective-permute-done((bf16[128,768]{1,0:T(8,128)(2,1)S(1)}, bf16[128,768]{1,0:T(8,128)(2,1)S(1)}, u32[]{:S(2)}, u32[]{:S(2)}) %collective-permute-start.2) | collective-permute-done | bytes 196640 | tf_op jit(solution)/shard_map/ppermute | solution.py:30
  101.5 0.7 copy-done.13
  102.2 0.7 copy-done.16
  102.9 18.7 %all_to_all.67 = bf16[16,8,1152]{2,1,0:T(8,128)(2,1)S(1)} all-to-all(bf16[16,8,1152]{2,1,0:T(8,128)(2,1)S(1)} %bitcast.57), channel_id=1, replica_groups=mesh['section'=32,'dp'=16] {'dp'}, dimensions={0} | all-to-all | bytes 589824 | tf_op jit(solution)/shard_map/all_to_all | solution.py:19
  121.8 0.7 copy-done.6
  122.6 3.7 %all-to-all-start.5 = ((bf16[16,8,1664]{2,1,0:T(8,128)(2,1)}), bf16[16,8,1664]{2,1,0:T(8,128)(2,1)S(1)}, u32[]{:S(2)}, u32[]{:S(2)}) async-start(bf16[16,8,1664]{2,1,0:T(8,128)(2,1)} %bitcast.53), calls=%async_computation.5 | async-start | bytes 851968 | tf_op jit(solution)/shard_map/all_to_all | solution.py:19
  126.8 6.9 %collective-permute-start.4 = (bf16[128,768]{1,0:T(8,128)(2,1)S(1)}, bf16[128,768]{1,0:T(8,128)(2,1)S(1)}, u32[]{:S(2)}, u32[]{:S(2)}) collective-permute-start(bf16[128,768]{1,0:T(8,128)(2,1)S(1)} %copy-done.14), channel_id=1, source_target_pairs={{0,496},{16,480},{32,464},{48,448},{64,432},{80,416},{96,400},{112... | collective-permute-start | bytes 589832 | tf_op jit(solution)/shard_map/ppermute | solution.py:24
  135.1 5.9 %collective-permute-done.4 = bf16[128,768]{1,0:T(8,128)(2,1)S(1)} collective-permute-done((bf16[128,768]{1,0:T(8,128)(2,1)S(1)}, bf16[128,768]{1,0:T(8,128)(2,1)S(1)}, u32[]{:S(2)}, u32[]{:S(2)}) %collective-permute-start.4) | collective-permute-done | bytes 196640 | tf_op jit(solution)/shard_map/ppermute | solution.py:24
  140.9 2.0 %select_select_fusion = bf16[1,2,128,768]{3,2,1,0:T(8,128)(2,1)} fusion(bf16[1,2,128,768]{3,2,1,0:T(8,128)(2,1)} %param.12, pred[2]{0:T(512)(128)(4,1)S(1)} %iota_compare_fusion, pred[2]{0:T(512)(128)(4,1)S(1)} %iota_compare_fusion.1, bf16[128,768]{1,0:T(8,128)(2,1)} %get-tuple-element.50, bf16[128,768]{1,0:T(8,128)(2,1)S(1)} %collective-permute-done.4), kind=kLoop, calls=%fused_computation.1 | loop fusion | flops 393216 | bytes 1179652 | tf_op jit(solution)/shard_map/jit(_where)/select_n | solution.py:350
  142.9 0.9 copy-done.10
  143.9 2.0 %last.1 = (bf16[128,768]{1,0:T(8,128)(2,1)}, bf16[128,768]{1,0:T(8,128)(2,1)}, f32[1,768]{1,0:T(1,128)}, bf16[768,512]{1,0:T(8,128)(2,1)}, bf16[512,768]{1,0:T(8,128)(2,1)}) custom-call(bf16[128,1664]{1,0:T(8,128)(2,1)S(1)} %bitcast.51, bf16[128,1152]{1,0:T(8,128)(2,1)S(1)} %bitcast.45, bf16[128,1152]{1,0:T(8,128)(2,1)S(1)} %bitcast.47, ...), custom_call_target="tpu_custom_call" | custom-call | flops 603979776 | bytes 5545472 | tf_op jit(solution)/shard_map/last/pallas_call | solution.py:238
  (56 shorter events, 8.3 us)
Async XLA Ops:
  0.6 0.7 copy-start.22
  0.6 0.7 copy-start.23
  2.6 10.9 %copy-start.4 = (bf16[1,128,768]{2,1,0:T(8,128)(2,1)S(1)}, bf16[1,128,768]{2,1,0:T(8,128)(2,1)}, u32[]{:S(2)}) copy-start(bf16[1,128,768]{2,1,0:T(8,128)(2,1)} %param.9) | copy-start | bytes 589828
  2.6 10.9 %copy-start.5 = (bf16[1,128,768]{2,1,0:T(8,128)(2,1)S(1)}, bf16[1,128,768]{2,1,0:T(8,128)(2,1)}, u32[]{:S(2)}) copy-start(bf16[1,128,768]{2,1,0:T(8,128)(2,1)} %param.11) | copy-start | bytes 589828
  3.7 18.6 %collective-permute-start = (bf16[128,768]{1,0:T(8,128)(2,1)S(1)}, bf16[128,768]{1,0:T(8,128)(2,1)S(1)}, u32[]{:S(2)}, u32[]{:S(2)}) collective-permute-start(bf16[128,768]{1,0:T(8,128)(2,1)S(1)} %select_bitcast_fusion.1), channel_id=1, source_target_pairs={{0,496},{16,480},{32,464},{48,448},{64,432},{80,416},{96,400},{112... | collective-permute-start | bytes 589832 | tf_op jit(solution)/shard_map/ppermute | solution.py:24
  13.5 0.7 copy-start.20
  14.2 1.1 copy-start
  15.3 1.1 copy-start.2
  39.8 5.0 %copy-start.21 = (bf16[1,2,128,768]{3,2,1,0:T(8,128)(2,1)S(1)}, bf16[1,2,128,768]{3,2,1,0:T(8,128)(2,1)}, u32[]{:S(2)}) copy-start(bf16[1,2,128,768]{3,2,1,0:T(8,128)(2,1)} %param.12) | copy-start | bytes 1179652
  39.8 16.6 %all-to-all-start = ((bf16[16,8,1664]{2,1,0:T(8,128)(2,1)}), bf16[16,8,1664]{2,1,0:T(8,128)(2,1)S(1)}, u32[]{:S(2)}, u32[]{:S(2)}) async-start(bf16[16,8,1664]{2,1,0:T(8,128)(2,1)} %bitcast.4), calls=%async_computation | async-start | bytes 851968 | tf_op jit(solution)/shard_map/all_to_all | solution.py:19
  44.9 28.8 %collective-permute-start.3 = (bf16[2,128,768]{2,1,0:T(8,128)(2,1)S(1)}, bf16[2,128,768]{2,1,0:T(8,128)(2,1)S(1)}, u32[]{:S(2)}, u32[]{:S(2)}) collective-permute-start(bf16[2,128,768]{2,1,0:T(8,128)(2,1)S(1)} %pad_maximum_fusion), channel_id=1, source_target_pairs={{0,496},{16,480},{32,464},{48,448},{64,432},{80,416},{96,400},{112... | collective-permute-start | bytes 1179656 | tf_op jit(solution)/shard_map/ppermute | solution.py:24
  58.0 18.6 %all-to-all-start.2 = ((bf16[16,8,1152]{2,1,0:T(8,128)(2,1)}), bf16[16,8,1152]{2,1,0:T(8,128)(2,1)S(1)}, u32[]{:S(2)}, u32[]{:S(2)}) async-start(bf16[16,8,1152]{2,1,0:T(8,128)(2,1)} %bitcast.10), calls=%async_computation.2 | async-start | bytes 589824 | tf_op jit(solution)/shard_map/all_to_all | solution.py:19
  74.3 9.7 %copy-start.1 = (bf16[1,512,768]{2,1,0:T(8,128)(2,1)S(1)}, bf16[1,512,768]{2,1,0:T(8,128)(2,1)}, u32[]{:S(2)}) copy-start(bf16[1,512,768]{2,1,0:T(8,128)(2,1)} %param.15) | copy-start | bytes 2359300
  74.4 9.7 %copy-start.3 = (bf16[1,768,512]{2,1,0:T(8,128)(2,1)S(1)}, bf16[1,768,512]{2,1,0:T(8,128)(2,1)}, u32[]{:S(2)}) copy-start(bf16[1,768,512]{2,1,0:T(8,128)(2,1)} %param.14) | copy-start | bytes 2359300
  74.6 0.7 copy-start.7
  75.4 0.7 copy-start.9
  76.6 26.3 %all-to-all-start.4 = ((bf16[16,8,1152]{2,1,0:T(8,128)(2,1)}), bf16[16,8,1152]{2,1,0:T(8,128)(2,1)S(1)}, u32[]{:S(2)}, u32[]{:S(2)}) async-start(bf16[16,8,1152]{2,1,0:T(8,128)(2,1)} %bitcast.56), calls=%async_computation.4 | async-start | bytes 589824 | tf_op jit(solution)/shard_map/all_to_all | solution.py:19
  84.1 16.9 %copy-start.8 = (bf16[128,768]{1,0:T(8,128)(2,1)S(1)}, bf16[128,768]{1,0:T(8,128)(2,1)}, u32[]{:S(2)}) copy-start(bf16[128,768]{1,0:T(8,128)(2,1)} %refs_2_.3) | copy-start | bytes 589828
  84.7 0.7 copy-start.11
  85.4 11.6 %collective-permute-start.1 = (bf16[128,768]{1,0:T(8,128)(2,1)S(1)}, bf16[128,768]{1,0:T(8,128)(2,1)S(1)}, u32[]{:S(2)}, u32[]{:S(2)}) collective-permute-start(bf16[128,768]{1,0:T(8,128)(2,1)S(1)} %get-tuple-element.33.refs_3_), channel_id=1, source_target_pairs={{0,16},{16,32},{32,48},{48,64},{64,80},{80,96},{96,112},{112,128},... | collective-permute-start | bytes 589832 | tf_op jit(solution)/shard_map/ppermute | solution.py:30
  91.7 9.2 %collective-permute-start.2 = (bf16[128,768]{1,0:T(8,128)(2,1)S(1)}, bf16[128,768]{1,0:T(8,128)(2,1)S(1)}, u32[]{:S(2)}, u32[]{:S(2)}) collective-permute-start(bf16[128,768]{1,0:T(8,128)(2,1)S(1)} %get-tuple-element.34), channel_id=1, source_target_pairs={{16,0},{32,16},{48,32},{64,48},{80,64},{96,80},{112,96},{128,112},... | collective-permute-start | bytes 589832 | tf_op jit(solution)/shard_map/ppermute | solution.py:30
  101.5 0.7 copy-start.13
  102.2 0.7 copy-start.16
  102.9 18.7 %copy-start.19 = (f32[24,512]{1,0:T(8,128)S(1)}, f32[24,512]{1,0:T(8,128)}, u32[]{:S(2)}) copy-start(f32[24,512]{1,0:T(8,128)} %copy-done.18) | copy-start | bytes 147460
  121.8 0.8 copy-start.6
  122.6 4.2 %copy-start.14 = (bf16[128,768]{1,0:T(8,128)(2,1)S(1)}, bf16[128,768]{1,0:T(8,128)(2,1)}, u32[]{:S(2)}) copy-start(bf16[128,768]{1,0:T(8,128)(2,1)} %copy-done.13) | copy-start | bytes 589828
  122.6 20.3 %all-to-all-start.5 = ((bf16[16,8,1664]{2,1,0:T(8,128)(2,1)}), bf16[16,8,1664]{2,1,0:T(8,128)(2,1)S(1)}, u32[]{:S(2)}, u32[]{:S(2)}) async-start(bf16[16,8,1664]{2,1,0:T(8,128)(2,1)} %bitcast.53), calls=%async_computation.5 | async-start | bytes 851968 | tf_op jit(solution)/shard_map/all_to_all | solution.py:19
  126.8 14.1 %collective-permute-start.4 = (bf16[128,768]{1,0:T(8,128)(2,1)S(1)}, bf16[128,768]{1,0:T(8,128)(2,1)S(1)}, u32[]{:S(2)}, u32[]{:S(2)}) collective-permute-start(bf16[128,768]{1,0:T(8,128)(2,1)S(1)} %copy-done.14), channel_id=1, source_target_pairs={{0,496},{16,480},{32,464},{48,448},{64,432},{80,416},{96,400},{112... | collective-permute-start | bytes 589832 | tf_op jit(solution)/shard_map/ppermute | solution.py:24
  140.9 2.0 %copy-start.12 = (bf16[128,768]{1,0:T(8,128)(2,1)S(1)}, bf16[128,768]{1,0:T(8,128)(2,1)}, u32[]{:S(2)}) copy-start(bf16[128,768]{1,0:T(8,128)(2,1)} %copy-done.11) | copy-start | bytes 589828
  140.9 2.0 %copy-start.15 = (bf16[128,768]{1,0:T(8,128)(2,1)S(1)}, bf16[128,768]{1,0:T(8,128)(2,1)}, u32[]{:S(2)}) copy-start(bf16[128,768]{1,0:T(8,128)(2,1)} %copy-done.13) | copy-start | bytes 589828
  140.9 2.0 %copy-start.17 = (bf16[128,768]{1,0:T(8,128)(2,1)S(1)}, bf16[128,768]{1,0:T(8,128)(2,1)}, u32[]{:S(2)}) copy-start(bf16[128,768]{1,0:T(8,128)(2,1)} %copy-done.16) | copy-start | bytes 589828
  142.9 0.9 copy-start.10
  (1 other events, 0.6 us)

commit v3 on v2

v3 whole, which is shorter than its diff:
```python
import math

import jax
import jax.numpy as jnp
from jax import lax
from jax.experimental import pallas as pl
from jax.experimental.pallas import tpu as pltpu
from jax.sharding import PartitionSpec as P

BF16 = jnp.bfloat16
F32 = jnp.float32
EPS = 1e-05
LANES = 128
ROOT = math.sqrt(2 / math.pi)
CUBE = 0.044715


def across(block):
    return lax.all_to_all(block, "dp", 0, 0, tiled=True)


def mirrored(value):
    sections = lax.axis_size("section")
    return lax.ppermute(value, "section", [(i, sections - 1 - i) for i in range(sections)])


def shifted(value, by):
    sections = lax.axis_size("section")
    pairs = [(i, i + by) for i in range(sections) if 0 <= i + by < sections]
    return lax.ppermute(value, "section", pairs)


def pieces(value):
    high = value.astype(BF16).astype(F32)
    middle = (value - high).astype(BF16).astype(F32)
    return [high, middle, value - high - middle]


def in_lanes(columns):
    rows = columns[-1].shape[0]
    lane = lax.broadcasted_iota(jnp.int32, (rows, LANES), 1)
    block = jnp.zeros((rows, LANES), F32)
    for i, column in enumerate(columns):
        block = jnp.where(lane == i, column, block)
    return block


def from_lanes(block, first):
    lane = lax.broadcasted_iota(jnp.int32, block.shape, 1)
    return jnp.sum(jnp.where((lane >= first) & (lane < first + 3), block, 0.0), axis=1, keepdims=True)


def row_sums(values):
    one = jnp.sum(values, axis=1, keepdims=True)
    two = jnp.sum(values * values, axis=1, keepdims=True)
    return one, two


def hidden_part(tokens, weight, column_sum):
    values = tokens.astype(F32)
    one, two = row_sums(values)
    part = jnp.dot(tokens, weight, preferred_element_type=F32)
    return part - (one / values.shape[1]) * column_sum, pieces(one) + pieces(two)


def times_transposed(left, right):
    return lax.dot_general(left, right, (((1,), (1,)), ((), ())), preferred_element_type=F32)


def transposed_times(left, right):
    return lax.dot_general(left, right, (((0,), (0,)), ((), ())), preferred_element_type=F32)


def summed(block, peers):
    return jnp.sum(block.astype(F32).reshape(peers, -1, block.shape[1]), axis=0)


def finish_hidden(part, sums, first, column_sums, width):
    peers = len(column_sums)
    one = from_lanes(sums, first).reshape(peers, -1, 1)
    two = from_lanes(sums, first + 3).reshape(peers, -1, 1)
    mean = jnp.sum(one, axis=0) / width
    inverse = lax.rsqrt(jnp.sum(two, axis=0) / width - mean * mean + EPS)
    total = summed(part, peers)
    for peer in range(peers):
        total = total + (one[peer] / (width // peers) - mean) * column_sums[peer]
    return total * inverse, mean, inverse


def gelu(hidden):
    return hidden * (0.5 * (1.0 + jnp.tanh(ROOT * (hidden + CUBE * (hidden * hidden * hidden)))))


def gelu_and_slope(hidden):
    bent = jnp.tanh(ROOT * (hidden + CUBE * (hidden * hidden * hidden)))
    half = 0.5 * (1.0 + bent)
    slope = half + hidden * (0.5 * (1.0 - bent * bent)) * (ROOT * (1.0 + 3.0 * CUBE * (hidden * hidden)))
    return hidden * half, slope


def back_stats(grad_hidden, hidden, mean, inverse, column_exact, width):
    grad = grad_hidden.astype(F32)
    first = jnp.sum(grad * column_exact, axis=1, keepdims=True) / width
    second = jnp.sum(grad * hidden, axis=1, keepdims=True) / width
    return in_lanes(pieces(mean) + pieces(inverse) + pieces(first) + pieces(second))


def to_all(block, peers):
    rows, columns = block.shape
    return jnp.broadcast_to(block[None], (peers, rows, columns)).reshape(peers * rows, columns).astype(BF16)


def backward(tokens, upstream, grad_hidden, sums, gain, down_weight):
    mean, inverse, first, second = [from_lanes(sums, 3 * i) for i in range(4)]
    normed = (tokens.astype(F32) - mean) * inverse
    grad_scaled = times_transposed(grad_hidden, down_weight)
    grad_rows = inverse * (grad_scaled * gain - first - normed * second)
    tokens_grad = (upstream.astype(F32) + grad_rows).astype(BF16)
    gain_term = jnp.sum(grad_scaled * normed, axis=0, keepdims=True)
    return tokens_grad, (normed * gain).astype(BF16), gain_term


def copies(pairs, sems):
    started = [pltpu.make_async_copy(source, target, sems.at[i]) for i, (source, target) in enumerate(pairs)]
    for one in started:
        one.start()
    return started


def pick_kernel(fetch, stash, first, second, sems):
    partner = lax.axis_size("section") - 1 - lax.axis_index("section")
    for one in copies(
        [(stash.at[0, fetch[0, partner]], first), (stash.at[0, fetch[1, partner]], second)], sems
    ):
        one.wait()


def start_kernel(tokens, upstream, gain, down, up, payload, weight, column_sum, *, peers, rank):
    rows, features = tokens.shape
    tall = jnp.broadcast_to(gain[...].astype(F32), (LANES, features)).T
    exact = down[...].astype(F32) * jnp.concatenate([tall] * (rank // LANES), axis=1)
    rounded = exact.astype(BF16)
    weight[...] = rounded
    one = jnp.sum(rounded.astype(F32), axis=0, keepdims=True)
    column_sum[...] = one
    two = jnp.sum(exact, axis=0, keepdims=True)
    half = rank // 2
    row = lax.broadcasted_iota(jnp.int32, (rows // peers, half), 0)
    block = jnp.zeros((rows // peers, half), F32)
    for i, piece in enumerate(pieces(one)[:2] + pieces(two)[:2]):
        block = jnp.where(row == 2 * i, piece[:, :half], block)
        block = jnp.where(row == 2 * i + 1, piece[:, half:], block)
    part, sums = hidden_part(tokens[...], rounded, one)
    payload[:, :rank] = part.astype(BF16)
    payload[:, rank : 2 * rank] = times_transposed(upstream[...], up[...]).astype(BF16)
    payload[:, 2 * rank : 2 * rank + half] = to_all(block, peers)
    payload[:, 2 * rank + half :] = in_lanes(sums).astype(BF16)


def fetched_kernel(tokens, weight, column_sum, after, payload, *, rank):
    part, sums = hidden_part(tokens[...], weight[...], column_sum[...])
    payload[:, :rank] = part.astype(BF16)
    payload[:, rank:] = in_lanes(sums).astype(BF16)


def middle_kernel(got, got_b, payload, columns_out, active_back, columns, sems, *, peers, rank, width):
    half = rank // 2
    blocks = got[:, 2 * rank : 2 * rank + half].astype(F32).reshape(peers, -1, half)
    row = lax.broadcasted_iota(jnp.int32, blocks.shape[1:], 0)

    def joined(block, first):
        left = jnp.sum(jnp.where((row == first) | (row == first + 2), block, 0.0), axis=0, keepdims=True)
        right = jnp.sum(jnp.where((row == first + 1) | (row == first + 3), block, 0.0), axis=0, keepdims=True)
        return jnp.concatenate([left, right], axis=1)

    column_sums = []
    for peer in range(peers):
        column_sums.append(joined(blocks[peer], 0))
        columns[peer : peer + 1, :] = column_sums[peer]
    column_exact = joined(jnp.sum(blocks, axis=0), 4)
    columns[peers : peers + 1, :] = column_exact
    columns[peers + 1 :, :] = jnp.zeros((7, rank), F32)
    (saved,) = copies([(columns, columns_out)], sems)
    sums = got[:, 2 * rank + half :].astype(F32)
    hidden_f = finish_hidden(got[:, :rank], sums, 0, column_sums, width)[0]
    slope = summed(got[:, rank : 2 * rank], peers)
    hidden, mean, inverse = finish_hidden(got_b[:, :rank], got_b[:, rank:].astype(F32), 0, column_sums, width)
    active, bent = gelu_and_slope(hidden)
    active_back[...] = active
    grad_hidden = (slope * bent).astype(BF16)
    payload[:, :rank] = to_all(gelu(hidden_f), peers)
    payload[:, rank : 2 * rank] = to_all(grad_hidden.astype(F32), peers)
    payload[:, 2 * rank :] = to_all(back_stats(grad_hidden, hidden, mean, inverse, column_exact, width), peers)
    saved.wait()


def first_kernel(got, tokens, fetched, upstream, gain, down, up, out, grad, *, rank):
    out[...] = (
        tokens[...].astype(F32) + jnp.dot(got[:, :rank], up[...], preferred_element_type=F32)
    ).astype(BF16)
    grad[...] = backward(
        fetched[...], upstream[...], got[:, rank : 2 * rank], got[:, 2 * rank :].astype(F32), gain[...].astype(F32), down[...]
    )[0]


def side_kernel(
    fetch, evict, arrived, tokens, weight, column_sum, got, fetched0, upstream, gain, down, after,
    payload, fetched_out, scaled_out, gain_term, chosen, scaled, sems, *, rank
):
    place = lax.axis_index("section")
    chosen[...] = jnp.where(fetch[1, place] == evict[0, place], tokens[...], arrived[...])
    (saved,) = copies([(chosen, fetched_out)], sems)
    part, sums = hidden_part(chosen[...], weight[...], column_sum[...])
    payload[:, :rank] = part.astype(BF16)
    payload[:, rank:] = in_lanes([0.0] * 6 + sums).astype(BF16)
    scaled[...], gain_term[...] = backward(
        fetched0[...], upstream[...], got[:, rank : 2 * rank], got[:, 2 * rank :].astype(F32), gain[...].astype(F32), down[...]
    )[1:]
    last = pltpu.make_async_copy(scaled, scaled_out, sems.at[1])
    last.start()
    saved.wait()
    last.wait()


def second_kernel(
    before, after, fresh, own, weight, column_sum, up, side, payload, tokens_out, upstream_out,
    tokens, upstream, sems, *, rank
):
    place = lax.axis_index("section")
    tokens[...] = jnp.where(place == 0, fresh[...], before[...])
    upstream[...] = jnp.where(place == lax.axis_size("section") - 1, own[...], after[...])
    saved = copies([(tokens, tokens_out), (upstream, upstream_out)], sems)
    part, sums = hidden_part(tokens[...], weight[...], column_sum[...])
    payload[:, :rank] = part.astype(BF16)
    payload[:, rank : 2 * rank] = times_transposed(upstream[...], up[...]).astype(BF16)
    payload[:, 2 * rank : 3 * rank] = side[:, :rank]
    payload[:, 3 * rank :] = (side[:, rank:].astype(F32) + in_lanes(sums)).astype(BF16)
    for one in saved:
        one.wait()


def late_kernel(got, columns, active_back, after, payload, *, peers, rank, width):
    column_sums = [columns[peer : peer + 1, :] for peer in range(peers)]
    sums = got[:, 3 * rank :].astype(F32)
    hidden_f = finish_hidden(got[:, :rank], sums, 0, column_sums, width)[0]
    slope = summed(got[:, rank : 2 * rank], peers)
    hidden, mean, inverse = finish_hidden(got[:, 2 * rank : 3 * rank], sums, 6, column_sums, width)
    active, bent = gelu_and_slope(hidden)
    grad_hidden = (slope * bent).astype(BF16)
    payload[:, :rank] = to_all(gelu(hidden_f), peers)
    payload[:, rank : 2 * rank] = to_all(grad_hidden.astype(F32), peers)
    payload[:, 2 * rank : 3 * rank] = to_all(active, peers)
    payload[:, 3 * rank : 4 * rank] = to_all(active_back[...], peers)
    stats = back_stats(grad_hidden, hidden, mean, inverse, columns[peers : peers + 1, :], width)
    payload[:, 4 * rank :] = to_all(stats, peers)


def last_kernel(
    evict, stash, partner0, partner1, got, got0, tokens_in, fetched_in, upstream_in, upstream0, scaled_in, gain_term0,
    gain, down, up, out, grad, gain_grad, down_grad, up_grad, stash_out,
    tokens, fetched, upstream, scaled0, sems, slot_sems, *, rank
):
    slots = stash.shape[1]
    partner = lax.axis_size("section") - 1 - lax.axis_index("section")
    early, late = evict[0, partner], evict[1, partner]
    for i in range(slots):
        for source, taken in (
            (partner1, late == i),
            (partner0, (late != i) & (early == i)),
            (stash.at[0, i], (late != i) & (early != i)),
        ):
            @pl.when(taken)
            def _():
                pltpu.make_async_copy(source, stash_out.at[0, i], slot_sems.at[i]).start()

    loads = copies(
        [(tokens_in, tokens), (fetched_in, fetched), (upstream_in, upstream), (scaled_in, scaled0)], sems
    )
    product = jnp.dot(got[:, :rank], up[...], preferred_element_type=F32)
    loads[0].wait()
    out[...] = (tokens[...].astype(F32) + product).astype(BF16)
    loads[1].wait()
    loads[2].wait()
    grad[...], scaled, gain_term = backward(
        fetched[...], upstream[...], got[:, rank : 2 * rank], got[:, 4 * rank :].astype(F32), gain[...].astype(F32), down[...]
    )
    gain_grad[...] = gain_term0[...] + gain_term
    loads[3].wait()
    down_grad[...] = transposed_times(
        jnp.concatenate([scaled0[...], scaled], axis=0),
        jnp.concatenate([got0[:, rank : 2 * rank], got[:, rank : 2 * rank]], axis=0),
    ).astype(BF16)
    up_grad[...] = transposed_times(
        jnp.concatenate([got[:, 3 * rank : 4 * rank], got[:, 2 * rank : 3 * rank]], axis=0),
        jnp.concatenate([upstream0[...], upstream[...]], axis=0),
    ).astype(BF16)
    for i in range(slots):
        pltpu.make_async_copy(stash.at[0, i], stash_out.at[0, i], slot_sems.at[i]).wait()


def call(body, outs, operands, products=1, smem=(), left=(), left_outs=(), scratch=(), name=None):
    spaces = [pltpu.SMEM if i in smem else pl.ANY if i in left else pltpu.VMEM for i in range(len(operands))]
    out_spaces = [pl.ANY if i in left_outs else pltpu.VMEM for i in range(len(outs))]
    moved = sum(math.prod(o.shape) * o.dtype.itemsize for o in list(outs) + list(operands))
    return pl.pallas_call(
        body,
        out_shape=tuple(outs),
        in_specs=[pl.BlockSpec(memory_space=s) for s in spaces],
        out_specs=tuple(pl.BlockSpec(memory_space=s) for s in out_spaces),
        scratch_shapes=list(scratch),
        compiler_params=pltpu.CompilerParams(vmem_limit_bytes=16 * 2**20),
        cost_estimate=pl.CostEstimate(flops=products * 2 * 128 * 768 * 512, bytes_accessed=moved, transcendentals=0),
        name=name,
    )(*operands)


def bound(body, **sizes):
    def run(*refs):
        body(*refs, **sizes)

    return run


def on_device(layer_input, fresh_input, out_grad, held_stash, norm_gain, down_proj, up_proj, fetch_slot, evict_slot):
    peers = lax.axis_size("dp")
    tokens0, grad0 = layer_input[0], out_grad[0]
    down, up = down_proj[0], up_proj[0]
    rows, features = tokens0.shape
    rank = up.shape[0]
    width = features * peers
    own = rows // peers

    def shape(*dims, dtype=BF16):
        return jax.ShapeDtypeStruct(dims, dtype)

    half = rank // 2
    tile = pltpu.VMEM((rows, features), BF16)
    sems = pltpu.SemaphoreType.DMA
    fetch, evict = fetch_slot.T, evict_slot.T

    picked0, picked1 = call(
        pick_kernel,
        [shape(rows, features), shape(rows, features)],
        [fetch, held_stash],
        smem=(0,),
        left=(1,),
        scratch=[sems((2,))],
        name="pick",
    )
    fetched0 = mirrored(picked0)
    payload, weight, column_sum = call(
        bound(start_kernel, peers=peers, rank=rank),
        [shape(rows, 2 * rank + half + LANES), shape(features, rank), shape(1, rank, dtype=F32)],
        [tokens0, grad0, norm_gain, down, up],
        products=2,
        name="start",
    )
    got_a = across(payload)
    (payload,) = call(
        bound(fetched_kernel, rank=rank),
        [shape(rows, rank + LANES)],
        [fetched0, weight, column_sum, got_a],
        left=(3,),
        name="fetched",
    )
    got_b = across(payload)
    arrived1 = mirrored(picked1)
    payload, columns, active_back = call(
        bound(middle_kernel, peers=peers, rank=rank, width=width),
        [shape(rows, 2 * rank + LANES), shape(peers + 8, rank, dtype=F32), shape(own, rank, dtype=F32)],
        [got_a, got_b],
        left_outs=(1,),
        scratch=[pltpu.VMEM((peers + 8, rank), F32), sems((1,))],
        name="middle",
    )
    got0 = across(payload)
    first_out, first_grad = call(
        bound(first_kernel, rank=rank),
        [shape(rows, features), shape(rows, features)],
        [got0, tokens0, fetched0, grad0, norm_gain, down, up],
        products=2,
        name="first",
    )
    before_out = shifted(first_out, 1)
    after_grad = shifted(first_grad, -1)
    side, fetched1, scaled0, gain_term0 = call(
        bound(side_kernel, rank=rank),
        [shape(rows, rank + LANES), shape(rows, features), shape(rows, features), shape(1, features, dtype=F32)],
        [fetch, evict, arrived1, tokens0, weight, column_sum, got0, fetched0, grad0, norm_gain, down, first_out],
        smem=(0, 1),
        left=(11,),
        left_outs=(1, 2),
        scratch=[tile, tile, sems((2,))],
        products=2,
        name="side",
    )
    payload, tokens1, grad1 = call(
        bound(second_kernel, rank=rank),
        [shape(rows, 3 * rank + LANES), shape(rows, features), shape(rows, features)],
        [before_out, after_grad, fresh_input, first_out, weight, column_sum, up, side],
        left_outs=(1, 2),
        scratch=[tile, tile, sems((2,))],
        products=2,
        name="second",
    )
    got = across(payload)
    partner0 = mirrored(tokens0)
    (payload,) = call(
        bound(late_kernel, peers=peers, rank=rank, width=width),
        [shape(rows, 4 * rank + LANES)],
        [got, columns, active_back, partner0],
        left=(3,),
        name="late",
    )
    got1 = across(payload)
    partner1 = mirrored(tokens1)
    next_output, input_grad, gain_grad, down_grad, up_grad, stash = call(
        bound(last_kernel, rank=rank),
        [
            shape(rows, features),
            shape(rows, features),
            shape(1, features, dtype=F32),
            shape(features, rank),
            shape(rank, features),
            shape(*held_stash.shape),
        ],
        [
            evict, held_stash, partner0, partner1, got1, got0, tokens1, fetched1, grad1, grad0, scaled0, gain_term0,
            norm_gain, down, up,
        ],
        smem=(0,),
        left=(1, 2, 3, 6, 7, 8, 10),
        left_outs=(5,),
        scratch=[tile, tile, tile, tile, sems((4,)), sems((held_stash.shape[1],))],
        products=6,
        name="last",
    )
    return (next_output[None], input_grad[None], stash, gain_grad, down_grad[None], up_grad[None])


def solution(mesh):
    placed = (
        P("section", None, "dp"),
        P(None, "dp"),
        P("section", None, "dp"),
        P("section", None, None, "dp"),
        P("section", "dp"),
        P("section", "dp", None),
        P("section", None, "dp"),
        P(),
        P(),
    )
    return jax.shard_map(
        on_device,
        mesh=mesh,
        in_specs=placed,
        out_specs=(
            P("section", None, "dp"),
            P("section", None, "dp"),
            P("section", None, None, "dp"),
            P("section", "dp"),
            P("section", "dp", None),
            P("section", None, "dp"),
        ),
        check_vma=False,
    )
```

time: 147 us -> 148 us (level)
  the two profiles are of different devices: /device:TPU:129 before, /device:TPU:1 now
where the time goes in v3:
time: 148 us; the launch traced here: 147 us
  starting transfers between devices  67.9 us (46%)
  waiting for transfers between devices  35.1 us (24%)
  blocking collectives  16.8 us (11%)
  Pallas kernels  13.6 us (9%)
  local copies, waits for them, and re-layouts  12.2 us (8%)
    ppermute x4, waiting for transfers between devices, mirrored(): lax.ppermute(value, 'section', [(i, sections - 1 - i) for i in range(sect...  33.3 us
    all_to_all x4, starting transfers between devices, across(): return lax.all_to_all(block, 'dp', 0, 0, tiled=True)  30.4 us
    ppermute x4, starting transfers between devices, mirrored(): lax.ppermute(value, 'section', [(i, sections - 1 - i) for i in range(sect...  30.2 us
    all_to_all x1, blocking collectives, across(): return lax.all_to_all(block, 'dp', 0, 0, tiled=True)  16.8 us
    pallas_call x9, Pallas kernels, call(): pl.pallas_call(body, out_shape=tuple(outs), in_specs=[pl.BlockSpec(memory...  13.6 us
    unnamed x50, local copies, waits for them, and re-layouts  12.2 us
    ppermute x2, starting transfers between devices, shifted(): return lax.ppermute(value, 'section', pairs)  7.26 us
  transfers between devices with their start and end apart: 10, of which 5 were waited for; matrix products, arithmetic and copies ran while one was open for 0% of the time, Pallas kernels for 2%

profile of v3, /device:TPU:1, one launch (start us, length us, event | category | flops | bytes accessed | tf_op | source)
XLA Modules:
  0.0 146.6 jit_solution(18164890091168216700)
XLA Ops:
  0.6 0.7 copy-done.21
  1.3 1.1 copy-done
  2.5 1.1 copy-done.2
  3.6 0.9 copy-done.4
  4.5 0.9 copy-done.6
  5.4 1.6 %start.1 = (bf16[128,1408]{1,0:T(8,128)(2,1)}, bf16[768,512]{1,0:T(8,128)(2,1)S(1)}, f32[1,512]{1,0:T(1,128)S(1)}) custom-call(bf16[128,768]{1,0:T(8,128)(2,1)S(1)} %bitcast.38, bf16[128,768]{1,0:T(8,128)(2,1)S(1)} %bitcast.33, bf16[1,768]{1,0:T(2,128)(2,1)S(1)} %copy-done.21, bf16[768,512]{1,0:T(8,128)(2,1)S(1)} %bitcast.20, bf16[512,768]{1,0:T(8,128)(2,1)S(1)} %bitcast.24), custom_call_target="tpu_custom_call" | custom-call | flops 201326592 | bytes 3116544 | tf_op jit(solution)/shard_map/start/pallas_call | solution.py:305
  7.0 9.7 %all-to-all-start = ((bf16[16,8,1408]{2,1,0:T(8,128)(2,1)}), bf16[16,8,1408]{2,1,0:T(8,128)(2,1)S(1)}, u32[]{:S(2)}, u32[]{:S(2)}) async-start(bf16[16,8,1408]{2,1,0:T(8,128)(2,1)} %bitcast.5), calls=%async_computation | async-start | bytes 720896 | tf_op jit(solution)/shard_map/all_to_all | solution.py:19
  17.4 1.1 pick.1
  18.5 12.8 %collective-permute-start.1 = (bf16[128,768]{1,0:T(8,128)(2,1)S(1)}, bf16[128,768]{1,0:T(8,128)(2,1)S(1)}, u32[]{:S(2)}, u32[]{:S(2)}) collective-permute-start(bf16[128,768]{1,0:T(8,128)(2,1)S(1)} %get-tuple-element.30), channel_id=1, source_target_pairs={{0,496},{16,480},{32,464},{48,448},{64,432},{80,416},{96,400},{112... | collective-permute-start | bytes 589832 | tf_op jit(solution)/shard_map/ppermute | solution.py:24
  31.3 8.6 %collective-permute-done.1.refs_0_.refs_2_.refs_7_ = bf16[128,768]{1,0:T(8,128)(2,1)S(1)} collective-permute-done((bf16[128,768]{1,0:T(8,128)(2,1)S(1)}, bf16[128,768]{1,0:T(8,128)(2,1)S(1)}, u32[]{:S(2)}, u32[]{:S(2)}) %collective-permute-start.1) | collective-permute-done | bytes 196640 | tf_op jit(solution)/shard_map/ppermute | solution.py:24
  40.3 16.8 %all_to_all.55 = bf16[16,8,640]{2,1,0:T(8,128)(2,1)S(1)} all-to-all(bf16[16,8,640]{2,1,0:T(8,128)(2,1)S(1)} %bitcast.43), channel_id=1, replica_groups=mesh['section'=32,'dp'=16] {'dp'}, dimensions={0} | all-to-all | bytes 327680 | tf_op jit(solution)/shard_map/all_to_all | solution.py:19
  57.1 1.1 middle.1
  58.3 3.7 %all-to-all-start.2 = ((bf16[16,8,1152]{2,1,0:T(8,128)(2,1)}), bf16[16,8,1152]{2,1,0:T(8,128)(2,1)S(1)}, u32[]{:S(2)}, u32[]{:S(2)}) async-start(bf16[16,8,1152]{2,1,0:T(8,128)(2,1)} %bitcast.10), calls=%async_computation.2 | async-start | bytes 589824 | tf_op jit(solution)/shard_map/all_to_all | solution.py:19
  62.0 8.7 %collective-permute-start.4 = (bf16[128,768]{1,0:T(8,128)(2,1)}, bf16[128,768]{1,0:T(8,128)(2,1)S(1)}, u32[]{:S(2)}, u32[]{:S(2)}) collective-permute-start(bf16[128,768]{1,0:T(8,128)(2,1)} %copy-done.24), channel_id=1, source_target_pairs={{0,496},{16,480},{32,464},{48,448},{64,432},{80,416},{96,400},{112... | collective-permute-start | bytes 589832 | tf_op jit(solution)/shard_map/ppermute | solution.py:24
  70.6 1.7 %all-to-all-done.2 = bf16[16,8,1152]{2,1,0:T(8,128)(2,1)S(1)} async-done(((bf16[16,8,1152]{2,1,0:T(8,128)(2,1)}), bf16[16,8,1152]{2,1,0:T(8,128)(2,1)S(1)}, u32[]{:S(2)}, u32[]{:S(2)}) %all-to-all-start.2) | async-done | bytes 294944 | tf_op jit(solution)/shard_map/all_to_all | solution.py:19
  72.9 5.3 %collective-permute-start.3 = (bf16[128,768]{1,0:T(8,128)(2,1)S(1)}, bf16[128,768]{1,0:T(8,128)(2,1)S(1)}, u32[]{:S(2)}, u32[]{:S(2)}) collective-permute-start(bf16[128,768]{1,0:T(8,128)(2,1)S(1)} %get-tuple-element.35), channel_id=1, source_target_pairs={{16,0},{32,16},{48,32},{64,48},{80,64},{96,80},{112,96},{128,112},... | collective-permute-start | bytes 589832 | tf_op jit(solution)/shard_map/ppermute | solution.py:30
  78.3 1.9 %collective-permute-start.2 = (bf16[128,768]{1,0:T(8,128)(2,1)S(1)}, bf16[128,768]{1,0:T(8,128)(2,1)S(1)}, u32[]{:S(2)}, u32[]{:S(2)}) collective-permute-start(bf16[128,768]{1,0:T(8,128)(2,1)S(1)} %get-tuple-element.34.refs_11_.refs_3_), channel_id=1, source_target_pairs={{0,16},{16,32},{32,48},{48,64},{64,80},{80,96},{96,112},{112,128},... | collective-permute-start | bytes 589832 | tf_op jit(solution)/shard_map/ppermute | solution.py:30
  80.9 0.9 copy-done.20
  81.8 1.7 %side.1 = (bf16[128,640]{1,0:T(8,128)(2,1)S(1)}, bf16[128,768]{1,0:T(8,128)(2,1)S(1)}, bf16[128,768]{1,0:T(8,128)(2,1)S(1)}, f32[1,768]{1,0:T(1,128)S(1)}) custom-call(s32[2,32]{1,0:T(2,128)S(1)} %bitcast.46, s32[2,32]{1,0:T(2,128)S(1)} %bitcast.47, bf16[128,768]{1,0:T(8,128)(2,1)S(1)} %copy-done.20, bf16[128,768]{1,0:T(8,128)(2,1)S(1)} %bitcast.40, ...), custom_call_target="tpu_custom_call" | custom-call | flops 201326592 | bytes 3415040 | tf_op jit(solution)/shard_map/side/pallas_call | solution.py:305
  83.7 1.9 %second.1 = (bf16[128,1664]{1,0:T(8,128)(2,1)}, bf16[128,768]{1,0:T(8,128)(2,1)S(1)}, bf16[128,768]{1,0:T(8,128)(2,1)S(1)}) custom-call(bf16[128,768]{1,0:T(8,128)(2,1)S(1)} %collective-permute-done.2.refs_0_, bf16[128,768]{1,0:T(8,128)(2,1)S(1)} %collective-permute-done.3.refs_1_, bf16[128,768]{1,0:T(8,128)(2,1)S(1)} %copy-done.18, ...), custom_call_target="tpu_custom_call" | custom-call | flops 201326592 | bytes 3344384 | tf_op jit(solution)/shard_map/second/pallas_call | solution.py:305
  86.3 8.1 %all-to-all-start.3 = ((bf16[16,8,1664]{2,1,0:T(8,128)(2,1)}), bf16[16,8,1664]{2,1,0:T(8,128)(2,1)S(1)}, u32[]{:S(2)}, u32[]{:S(2)}) async-start(bf16[16,8,1664]{2,1,0:T(8,128)(2,1)} %bitcast.12), calls=%async_computation.3 | async-start | bytes 851968 | tf_op jit(solution)/shard_map/all_to_all | solution.py:19
  94.4 5.1 %collective-permute-start = (bf16[128,768]{1,0:T(8,128)(2,1)S(1)}, bf16[128,768]{1,0:T(8,128)(2,1)S(1)}, u32[]{:S(2)}, u32[]{:S(2)}) collective-permute-start(bf16[128,768]{1,0:T(8,128)(2,1)S(1)} %bitcast.41), channel_id=1, source_target_pairs={{0,496},{16,480},{32,464},{48,448},{64,432},{80,416},{96,400},{112... | collective-permute-start | bytes 589832 | tf_op jit(solution)/shard_map/ppermute | solution.py:24
  99.5 11.2 %collective-permute-done.refs_3_.refs_2_ = bf16[128,768]{1,0:T(8,128)(2,1)S(1)} collective-permute-done((bf16[128,768]{1,0:T(8,128)(2,1)S(1)}, bf16[128,768]{1,0:T(8,128)(2,1)S(1)}, u32[]{:S(2)}, u32[]{:S(2)}) %collective-permute-start) | collective-permute-done | bytes 196640 | tf_op jit(solution)/shard_map/ppermute | solution.py:24
  110.7 1.1 late.1
  111.8 8.9 %all-to-all-start.4 = ((bf16[16,8,2176]{2,1,0:T(8,128)(2,1)}), bf16[16,8,2176]{2,1,0:T(8,128)(2,1)S(1)}, u32[]{:S(2)}, u32[]{:S(2)}) async-start(bf16[16,8,2176]{2,1,0:T(8,128)(2,1)} %bitcast.14), calls=%async_computation.4 | async-start | bytes 1114112 | tf_op jit(solution)/shard_map/all_to_all | solution.py:19
  120.7 3.6 %collective-permute-start.5 = (bf16[128,768]{1,0:T(8,128)(2,1)}, bf16[128,768]{1,0:T(8,128)(2,1)S(1)}, u32[]{:S(2)}, u32[]{:S(2)}) collective-permute-start(bf16[128,768]{1,0:T(8,128)(2,1)} %copy-done.12), channel_id=1, source_target_pairs={{0,496},{16,480},{32,464},{48,448},{64,432},{80,416},{96,400},{112... | collective-permute-start | bytes 589832 | tf_op jit(solution)/shard_map/ppermute | solution.py:24
  124.3 13.5 %collective-permute-done.5.refs_3_ = bf16[128,768]{1,0:T(8,128)(2,1)S(1)} collective-permute-done((bf16[128,768]{1,0:T(8,128)(2,1)}, bf16[128,768]{1,0:T(8,128)(2,1)S(1)}, u32[]{:S(2)}, u32[]{:S(2)}) %collective-permute-start.5) | collective-permute-done | bytes 196640 | tf_op jit(solution)/shard_map/ppermute | solution.py:24
  138.5 0.9 copy-done.11
  139.4 0.9 copy-done.13
  140.3 0.9 copy-done.15
  141.3 0.9 copy-done.17
  142.2 4.4 %last.1 = (bf16[128,768]{1,0:T(8,128)(2,1)}, bf16[128,768]{1,0:T(8,128)(2,1)}, f32[1,768]{1,0:T(1,128)}, bf16[768,512]{1,0:T(8,128)(2,1)}, bf16[512,768]{1,0:T(8,128)(2,1)}, /*index=5*/bf16[1,2,128,768]{3,2,1,0:T(8,128)(2,1)}) custom-call(s32[2,32]{1,0:T(2,128)S(1)} %bitcast.48, bf16[1,2,128,768]{3,2,1,0:T(8,128)(2,1)S(1)} %copy-done.9, ...), custom_call_target="tpu_custom_call" | custom-call | flops 603979776 | bytes 6561536 | tf_op jit(solution)/shard_map/last/pallas_call | solution.py:305
  (48 shorter events, 3.8 us)
Async XLA Ops:
  0.6 0.7 copy-start.21
  1.3 1.1 copy-start
  2.5 1.1 copy-start.2
  3.6 0.9 copy-start.4
  4.5 0.9 copy-start.6
  7.0 9.7 %copy-start.8 = (bf16[1,2,128,768]{3,2,1,0:T(8,128)(2,1)S(1)}, bf16[1,2,128,768]{3,2,1,0:T(8,128)(2,1)}, u32[]{:S(2)}) copy-start(bf16[1,2,128,768]{3,2,1,0:T(8,128)(2,1)} %refs_1_.1) | copy-start | bytes 1179652
  7.0 32.9 %all-to-all-start = ((bf16[16,8,1408]{2,1,0:T(8,128)(2,1)}), bf16[16,8,1408]{2,1,0:T(8,128)(2,1)S(1)}, u32[]{:S(2)}, u32[]{:S(2)}) async-start(bf16[16,8,1408]{2,1,0:T(8,128)(2,1)} %bitcast.5), calls=%async_computation | async-start | bytes 720896 | tf_op jit(solution)/shard_map/all_to_all | solution.py:19
  16.7 0.7 copy-start.22
  18.5 12.8 %copy-start.24 = (bf16[128,768]{1,0:T(8,128)(2,1)}, bf16[128,768]{1,0:T(8,128)(2,1)S(1)}, u32[]{:S(2)}) copy-start(bf16[128,768]{1,0:T(8,128)(2,1)S(1)} %get-tuple-element.36) | copy-start | bytes 589828
  18.5 21.4 %collective-permute-start.1 = (bf16[128,768]{1,0:T(8,128)(2,1)S(1)}, bf16[128,768]{1,0:T(8,128)(2,1)S(1)}, u32[]{:S(2)}, u32[]{:S(2)}) collective-permute-start(bf16[128,768]{1,0:T(8,128)(2,1)S(1)} %get-tuple-element.30), channel_id=1, source_target_pairs={{0,496},{16,480},{32,464},{48,448},{64,432},{80,416},{96,400},{112... | collective-permute-start | bytes 589832 | tf_op jit(solution)/shard_map/ppermute | solution.py:24
  40.0 32.4 %copy-start.3 = (bf16[1,512,768]{2,1,0:T(8,128)(2,1)S(1)}, bf16[1,512,768]{2,1,0:T(8,128)(2,1)}, u32[]{:S(2)}) copy-start(bf16[1,512,768]{2,1,0:T(8,128)(2,1)} %param.15) | copy-start | bytes 2359300
  40.2 32.1 %copy-start.1 = (bf16[1,768,512]{2,1,0:T(8,128)(2,1)S(1)}, bf16[1,768,512]{2,1,0:T(8,128)(2,1)}, u32[]{:S(2)}) copy-start(bf16[1,768,512]{2,1,0:T(8,128)(2,1)} %param.14) | copy-start | bytes 2359300
  58.3 14.1 %copy-start.5 = (bf16[1,128,768]{2,1,0:T(8,128)(2,1)S(1)}, bf16[1,128,768]{2,1,0:T(8,128)(2,1)}, u32[]{:S(2)}) copy-start(bf16[1,128,768]{2,1,0:T(8,128)(2,1)} %param.11) | copy-start | bytes 589828
  58.3 14.1 %copy-start.7 = (bf16[1,128,768]{2,1,0:T(8,128)(2,1)S(1)}, bf16[1,128,768]{2,1,0:T(8,128)(2,1)}, u32[]{:S(2)}) copy-start(bf16[1,128,768]{2,1,0:T(8,128)(2,1)} %param.9) | copy-start | bytes 589828
  58.3 14.1 %all-to-all-start.2 = ((bf16[16,8,1152]{2,1,0:T(8,128)(2,1)}), bf16[16,8,1152]{2,1,0:T(8,128)(2,1)S(1)}, u32[]{:S(2)}, u32[]{:S(2)}) async-start(bf16[16,8,1152]{2,1,0:T(8,128)(2,1)} %bitcast.10), calls=%async_computation.2 | async-start | bytes 589824 | tf_op jit(solution)/shard_map/all_to_all | solution.py:19
  62.0 18.2 %collective-permute-start.4 = (bf16[128,768]{1,0:T(8,128)(2,1)}, bf16[128,768]{1,0:T(8,128)(2,1)S(1)}, u32[]{:S(2)}, u32[]{:S(2)}) collective-permute-start(bf16[128,768]{1,0:T(8,128)(2,1)} %copy-done.24), channel_id=1, source_target_pairs={{0,496},{16,480},{32,464},{48,448},{64,432},{80,416},{96,400},{112... | collective-permute-start | bytes 589832 | tf_op jit(solution)/shard_map/ppermute | solution.py:24
  72.9 10.7 %collective-permute-start.3 = (bf16[128,768]{1,0:T(8,128)(2,1)S(1)}, bf16[128,768]{1,0:T(8,128)(2,1)S(1)}, u32[]{:S(2)}, u32[]{:S(2)}) collective-permute-start(bf16[128,768]{1,0:T(8,128)(2,1)S(1)} %get-tuple-element.35), channel_id=1, source_target_pairs={{16,0},{32,16},{48,32},{64,48},{80,64},{96,80},{112,96},{128,112},... | collective-permute-start | bytes 589832 | tf_op jit(solution)/shard_map/ppermute | solution.py:30
  78.3 2.6 %copy-start.23 = (s32[32,2]{0,1:T(2,128)S(1)}, s32[32,2]{0,1:T(2,128)}, u32[]{:S(2)}) copy-start(s32[32,2]{0,1:T(2,128)} %param.17) | copy-start | bytes 772
  78.3 5.4 %collective-permute-start.2 = (bf16[128,768]{1,0:T(8,128)(2,1)S(1)}, bf16[128,768]{1,0:T(8,128)(2,1)S(1)}, u32[]{:S(2)}, u32[]{:S(2)}) collective-permute-start(bf16[128,768]{1,0:T(8,128)(2,1)S(1)} %get-tuple-element.34.refs_11_.refs_3_), channel_id=1, source_target_pairs={{0,16},{16,32},{32,48},{48,64},{64,80},{80,96},{96,112},{112,128},... | collective-permute-start | bytes 589832 | tf_op jit(solution)/shard_map/ppermute | solution.py:30
  80.9 0.9 copy-start.20
  81.8 1.8 %copy-start.18 = (bf16[128,768]{1,0:T(8,128)(2,1)S(1)}, bf16[128,768]{1,0:T(8,128)(2,1)}, u32[]{:S(2)}) copy-start(bf16[128,768]{1,0:T(8,128)(2,1)} %refs_2_.3) | copy-start | bytes 589828
  83.5 2.0 %copy-start.10 = (bf16[128,768]{1,0:T(8,128)(2,1)}, bf16[128,768]{1,0:T(8,128)(2,1)S(1)}, u32[]{:S(2)}) copy-start(bf16[128,768]{1,0:T(8,128)(2,1)S(1)} %get-tuple-element.44.refs_10_) | copy-start | bytes 589828
  85.6 0.7 copy-start.14
  86.3 24.4 %all-to-all-start.3 = ((bf16[16,8,1664]{2,1,0:T(8,128)(2,1)}), bf16[16,8,1664]{2,1,0:T(8,128)(2,1)S(1)}, u32[]{:S(2)}, u32[]{:S(2)}) async-start(bf16[16,8,1664]{2,1,0:T(8,128)(2,1)} %bitcast.12), calls=%async_computation.3 | async-start | bytes 851968 | tf_op jit(solution)/shard_map/all_to_all | solution.py:19
  94.4 16.3 %collective-permute-start = (bf16[128,768]{1,0:T(8,128)(2,1)S(1)}, bf16[128,768]{1,0:T(8,128)(2,1)S(1)}, u32[]{:S(2)}, u32[]{:S(2)}) collective-permute-start(bf16[128,768]{1,0:T(8,128)(2,1)S(1)} %bitcast.41), channel_id=1, source_target_pairs={{0,496},{16,480},{32,464},{48,448},{64,432},{80,416},{96,400},{112... | collective-permute-start | bytes 589832 | tf_op jit(solution)/shard_map/ppermute | solution.py:24
  111.8 26.7 %copy-start.9 = (bf16[1,2,128,768]{3,2,1,0:T(8,128)(2,1)S(1)}, bf16[1,2,128,768]{3,2,1,0:T(8,128)(2,1)}, u32[]{:S(2)}) copy-start(bf16[1,2,128,768]{3,2,1,0:T(8,128)(2,1)} %refs_1_.1) | copy-start | bytes 1179652
  111.8 26.7 %all-to-all-start.4 = ((bf16[16,8,2176]{2,1,0:T(8,128)(2,1)}), bf16[16,8,2176]{2,1,0:T(8,128)(2,1)S(1)}, u32[]{:S(2)}, u32[]{:S(2)}) async-start(bf16[16,8,2176]{2,1,0:T(8,128)(2,1)} %bitcast.14), calls=%async_computation.4 | async-start | bytes 1114112 | tf_op jit(solution)/shard_map/all_to_all | solution.py:19
  120.7 17.1 %collective-permute-start.5 = (bf16[128,768]{1,0:T(8,128)(2,1)}, bf16[128,768]{1,0:T(8,128)(2,1)S(1)}, u32[]{:S(2)}, u32[]{:S(2)}) collective-permute-start(bf16[128,768]{1,0:T(8,128)(2,1)} %copy-done.12), channel_id=1, source_target_pairs={{0,496},{16,480},{32,464},{48,448},{64,432},{80,416},{96,400},{112... | collective-permute-start | bytes 589832 | tf_op jit(solution)/shard_map/ppermute | solution.py:24
  138.5 0.9 copy-start.11
  139.4 0.9 copy-start.13
  140.3 0.9 copy-start.15
  141.3 0.9 copy-start.17
  (3 other events, 2.0 us)

commit v4 on v3

--- a/solution.py
+++ b/solution.py
@@ -11,6 +11,7 @@
 F32 = jnp.float32
 EPS = 1e-05
 LANES = 128
+LONG = 6
 ROOT = math.sqrt(2 / math.pi)
 CUBE = 0.044715
 
@@ -135,7 +136,7 @@
         one.wait()
 
 
-def start_kernel(tokens, upstream, gain, down, up, payload, weight, column_sum, *, peers, rank):
+def start_kernel(tokens, upstream, gain, down, up, after, payload, weight, column_sum, *, peers, rank):
     rows, features = tokens.shape
     tall = jnp.broadcast_to(gain[...].astype(F32), (LANES, features)).T
     exact = down[...].astype(F32) * jnp.concatenate([tall] * (rank // LANES), axis=1)
@@ -157,10 +158,14 @@
     payload[:, 2 * rank + half :] = in_lanes(sums).astype(BF16)
 
 
-def fetched_kernel(tokens, weight, column_sum, after, payload, *, rank):
-    part, sums = hidden_part(tokens[...], weight[...], column_sum[...])
-    payload[:, :rank] = part.astype(BF16)
-    payload[:, rank:] = in_lanes(sums).astype(BF16)
+def fetched_kernel(tokens, weight, column_sum, part, sums):
+    part[...], columns = hidden_part(tokens[...], weight[...], column_sum[...])
+    sums[...] = in_lanes(columns)
+
+
+def join_kernel(part, sums, after, payload, *, rank):
+    payload[:, :rank] = part[...].astype(BF16)
+    payload[:, rank:] = sums[...].astype(BF16)
 
 
 def middle_kernel(got, got_b, payload, columns_out, active_back, columns, sems, *, peers, rank, width):
@@ -194,52 +199,68 @@
     saved.wait()
 
 
-def first_kernel(got, tokens, fetched, upstream, gain, down, up, out, grad, *, rank):
+def first_kernel(got, tokens, fetched, upstream, gain, down, up, after, out, grad, out_kept, sems, *, rank):
     out[...] = (
         tokens[...].astype(F32) + jnp.dot(got[:, :rank], up[...], preferred_element_type=F32)
     ).astype(BF16)
+    (saved,) = copies([(out, out_kept)], sems)
     grad[...] = backward(
         fetched[...], upstream[...], got[:, rank : 2 * rank], got[:, 2 * rank :].astype(F32), gain[...].astype(F32), down[...]
     )[0]
-
-
-def side_kernel(
-    fetch, evict, arrived, tokens, weight, column_sum, got, fetched0, upstream, gain, down, after,
-    payload, fetched_out, scaled_out, gain_term, chosen, scaled, sems, *, rank
+    saved.wait()
+
+
+def other_kernel(
+    fetch, evict, arrived, tokens, weight, column_sum, payload, kept, chosen, sems, *, rank
 ):
     place = lax.axis_index("section")
     chosen[...] = jnp.where(fetch[1, place] == evict[0, place], tokens[...], arrived[...])
-    (saved,) = copies([(chosen, fetched_out)], sems)
+    (saved,) = copies([(chosen, kept.at[pl.ds(0, tokens.shape[0])])], sems)
     part, sums = hidden_part(chosen[...], weight[...], column_sum[...])
     payload[:, :rank] = part.astype(BF16)
     payload[:, rank:] = in_lanes([0.0] * 6 + sums).astype(BF16)
+    saved.wait()
+
+
+def terms_kernel(
+    kept_in, got, fetched, upstream, gain, down, after, kept, gain_term, scaled, sems, *, rank
+):
     scaled[...], gain_term[...] = backward(
-        fetched0[...], upstream[...], got[:, rank : 2 * rank], got[:, 2 * rank :].astype(F32), gain[...].astype(F32), down[...]
+        fetched[...], upstream[...], got[:, rank : 2 * rank], got[:, 2 * rank :].astype(F32), gain[...].astype(F32), down[...]
     )[1:]
-    last = pltpu.make_async_copy(scaled, scaled_out, sems.at[1])
-    last.start()
+    rows = scaled.shape[0]
+    (saved,) = copies([(scaled, kept.at[pl.ds(rows, rows)])], sems)
     saved.wait()
-    last.wait()
 
 
 def second_kernel(
-    before, after, fresh, own, weight, column_sum, up, side, payload, tokens_out, upstream_out,
-    tokens, upstream, sems, *, rank
+    kept_in, before, after, fresh, own, weight, column_sum, up, side, payload, kept, tokens, upstream, sems, *, rank
 ):
     place = lax.axis_index("section")
+    rows = before.shape[0]
     tokens[...] = jnp.where(place == 0, fresh[...], before[...])
-    upstream[...] = jnp.where(place == lax.axis_size("section") - 1, own[...], after[...])
-    saved = copies([(tokens, tokens_out), (upstream, upstream_out)], sems)
+    first = pltpu.make_async_copy(tokens, kept.at[pl.ds(2 * rows, rows)], sems.at[0])
+    first.start()
+    upstream[...] = after[...]
+
+    @pl.when(place == lax.axis_size("section") - 1)
+    def _():
+        late = pltpu.make_async_copy(own, upstream, sems.at[2])
+        late.start()
+        late.wait()
+
+    second = pltpu.make_async_copy(upstream, kept.at[pl.ds(3 * rows, rows)], sems.at[1])
+    second.start()
     part, sums = hidden_part(tokens[...], weight[...], column_sum[...])
     payload[:, :rank] = part.astype(BF16)
     payload[:, rank : 2 * rank] = times_transposed(upstream[...], up[...]).astype(BF16)
     payload[:, 2 * rank : 3 * rank] = side[:, :rank]
     payload[:, 3 * rank :] = (side[:, rank:].astype(F32) + in_lanes(sums)).astype(BF16)
-    for one in saved:
-        one.wait()
-
-
-def late_kernel(got, columns, active_back, after, payload, *, peers, rank, width):
+    first.wait()
+    second.wait()
+
+
+def late_kernel(got, columns, active_back, payload, *, peers, rank, width):
     column_sums = [columns[peer : peer + 1, :] for peer in range(peers)]
     sums = got[:, 3 * rank :].astype(F32)
     hidden_f = finish_hidden(got[:, :rank], sums, 0, column_sums, width)[0]
@@ -255,53 +276,59 @@
     payload[:, 4 * rank :] = to_all(stats, peers)
 
 
-def last_kernel(
-    evict, stash, partner0, partner1, got, got0, tokens_in, fetched_in, upstream_in, upstream0, scaled_in, gain_term0,
-    gain, down, up, out, grad, gain_grad, down_grad, up_grad, stash_out,
-    tokens, fetched, upstream, scaled0, sems, slot_sems, *, rank
-):
+def stash_kernel(evict, stash, partner0, partner1, fresh, stash_out, done, sems):
     slots = stash.shape[1]
     partner = lax.axis_size("section") - 1 - lax.axis_index("section")
     early, late = evict[0, partner], evict[1, partner]
     for i in range(slots):
         for source, taken in (
-            (partner1, late == i),
+            (partner1, (late == i) & (partner != 0)),
+            (fresh, (late == i) & (partner == 0)),
             (partner0, (late != i) & (early == i)),
             (stash.at[0, i], (late != i) & (early != i)),
         ):
             @pl.when(taken)
             def _():
-                pltpu.make_async_copy(source, stash_out.at[0, i], slot_sems.at[i]).start()
-
-    loads = copies(
-        [(tokens_in, tokens), (fetched_in, fetched), (upstream_in, upstream), (scaled_in, scaled0)], sems
-    )
+                pltpu.make_async_copy(source, stash_out.at[0, i], sems.at[i]).start()
+
+    for i in range(slots):
+        pltpu.make_async_copy(stash.at[0, i], stash_out.at[0, i], sems.at[i]).wait()
+    done[...] = jnp.zeros_like(done)
+
+
+def last_kernel(
+    kept_in, own, done, got, got0, upstream0, gain_term0, gain, down, up,
+    up_grad_out, out_out, grad, gain_grad, down_grad, kept, out, up_grad, sems, *, rank
+):
+    rows = upstream0.shape[0]
+    (load,) = copies([(kept_in, kept)], sems)
     product = jnp.dot(got[:, :rank], up[...], preferred_element_type=F32)
-    loads[0].wait()
-    out[...] = (tokens[...].astype(F32) + product).astype(BF16)
-    loads[1].wait()
-    loads[2].wait()
+    load.wait()
+    out[...] = (kept[2 * rows : 3 * rows].astype(F32) + product).astype(BF16)
+    first = pltpu.make_async_copy(out, out_out, sems.at[1])
+    first.start()
+    upstream = kept[3 * rows :]
+    up_grad[...] = transposed_times(
+        jnp.concatenate([got[:, 3 * rank : 4 * rank], got[:, 2 * rank : 3 * rank]], axis=0),
+        jnp.concatenate([upstream0[...], upstream], axis=0),
+    ).astype(BF16)
+    second = pltpu.make_async_copy(up_grad, up_grad_out, sems.at[2])
+    second.start()
     grad[...], scaled, gain_term = backward(
-        fetched[...], upstream[...], got[:, rank : 2 * rank], got[:, 4 * rank :].astype(F32), gain[...].astype(F32), down[...]
+        kept[:rows], upstream, got[:, rank : 2 * rank], got[:, 4 * rank :].astype(F32), gain[...].astype(F32), down[...]
     )
     gain_grad[...] = gain_term0[...] + gain_term
-    loads[3].wait()
     down_grad[...] = transposed_times(
-        jnp.concatenate([scaled0[...], scaled], axis=0),
+        jnp.concatenate([kept[rows : 2 * rows], scaled], axis=0),
         jnp.concatenate([got0[:, rank : 2 * rank], got[:, rank : 2 * rank]], axis=0),
     ).astype(BF16)
-    up_grad[...] = transposed_times(
-        jnp.concatenate([got[:, 3 * rank : 4 * rank], got[:, 2 * rank : 3 * rank]], axis=0),
-        jnp.concatenate([upstream0[...], upstream[...]], axis=0),
-    ).astype(BF16)
-    for i in range(slots):
-        pltpu.make_async_copy(stash.at[0, i], stash_out.at[0, i], slot_sems.at[i]).wait()
-
-
-def call(body, outs, operands, products=1, smem=(), left=(), left_outs=(), scratch=(), name=None):
-    spaces = [pltpu.SMEM if i in smem else pl.ANY if i in left else pltpu.VMEM for i in range(len(operands))]
-    out_spaces = [pl.ANY if i in left_outs else pltpu.VMEM for i in range(len(outs))]
-    moved = sum(math.prod(o.shape) * o.dtype.itemsize for o in list(outs) + list(operands))
+    first.wait()
+    second.wait()
+
+
+def call(body, outs, operands, cost=1, smem=(), left=(), left_outs=(), scratch=(), aliases=(), name=None):
+    spaces = [pltpu.SMEM if i in smem else pltpu.HBM if i in left else pltpu.VMEM for i in range(len(operands))]
+    out_spaces = [pltpu.HBM if i in left_outs else pltpu.VMEM for i in range(len(outs))]
     return pl.pallas_call(
         body,
         out_shape=tuple(outs),
@@ -309,7 +336,8 @@
         out_specs=tuple(pl.BlockSpec(memory_space=s) for s in out_spaces),
         scratch_shapes=list(scratch),
         compiler_params=pltpu.CompilerParams(vmem_limit_bytes=16 * 2**20),
-        cost_estimate=pl.CostEstimate(flops=products * 2 * 128 * 768 * 512, bytes_accessed=moved, transcendentals=0),
+        cost_estimate=pl.CostEstimate(flops=cost * 2**31, bytes_accessed=cost * 2**20, transcendentals=0),
+        input_output_aliases=dict(aliases),
         name=name,
     )(*operands)
 
@@ -351,17 +379,25 @@
     payload, weight, column_sum = call(
         bound(start_kernel, peers=peers, rank=rank),
         [shape(rows, 2 * rank + half + LANES), shape(features, rank), shape(1, rank, dtype=F32)],
-        [tokens0, grad0, norm_gain, down, up],
-        products=2,
+        [tokens0, grad0, norm_gain, down, up, picked1],
+        left=(5,),
+        cost=LONG,
         name="start",
     )
     got_a = across(payload)
+    part, sums = call(
+        fetched_kernel,
+        [shape(rows, rank, dtype=F32), shape(rows, LANES, dtype=F32)],
+        [fetched0, weight, column_sum],
+        cost=LONG,
+        name="fetched",
+    )
     (payload,) = call(
-        bound(fetched_kernel, rank=rank),
+        bound(join_kernel, rank=rank),
         [shape(rows, rank + LANES)],
-        [fetched0, weight, column_sum, got_a],
-        left=(3,),
-        name="fetched",
+        [part, sums, got_a],
+        left=(2,),
+        name="join",
     )
     got_b = across(payload)
     arrived1 = mirrored(picked1)
@@ -374,65 +410,84 @@
         name="middle",
     )
     got0 = across(payload)
-    first_out, first_grad = call(
+    other, kept = call(
+        bound(other_kernel, rank=rank),
+        [shape(rows, rank + LANES), shape(rank, features)],
+        [fetch, evict, arrived1, tokens0, weight, column_sum],
+        smem=(0, 1),
+        left_outs=(1,),
+        scratch=[tile, sems((1,))],
+        cost=LONG,
+        name="other",
+    )
+    first_out, first_grad, own_out = call(
         bound(first_kernel, rank=rank),
-        [shape(rows, features), shape(rows, features)],
-        [got0, tokens0, fetched0, grad0, norm_gain, down, up],
-        products=2,
+        [shape(rows, features)] * 3,
+        [got0, tokens0, fetched0, grad0, norm_gain, down, up, other],
+        left=(7,),
+        left_outs=(2,),
+        scratch=[sems((1,))],
         name="first",
     )
     before_out = shifted(first_out, 1)
     after_grad = shifted(first_grad, -1)
-    side, fetched1, scaled0, gain_term0 = call(
-        bound(side_kernel, rank=rank),
-        [shape(rows, rank + LANES), shape(rows, features), shape(rows, features), shape(1, features, dtype=F32)],
-        [fetch, evict, arrived1, tokens0, weight, column_sum, got0, fetched0, grad0, norm_gain, down, first_out],
-        smem=(0, 1),
-        left=(11,),
-        left_outs=(1, 2),
-        scratch=[tile, tile, sems((2,))],
-        products=2,
-        name="side",
-    )
-    payload, tokens1, grad1 = call(
+    partner0 = mirrored(tokens0)
+    kept, gain_term0 = call(
+        bound(terms_kernel, rank=rank),
+        [shape(rank, features), shape(1, features, dtype=F32)],
+        [kept, got0, fetched0, grad0, norm_gain, down, partner0],
+        left=(0, 6),
+        left_outs=(0,),
+        aliases=[(0, 0)],
+        scratch=[tile, sems((1,))],
+        cost=LONG,
+        name="terms",
+    )
+    payload, kept = call(
         bound(second_kernel, rank=rank),
-        [shape(rows, 3 * rank + LANES), shape(rows, features), shape(rows, features)],
-        [before_out, after_grad, fresh_input, first_out, weight, column_sum, up, side],
-        left_outs=(1, 2),
-        scratch=[tile, tile, sems((2,))],
-        products=2,
+        [shape(rows, 3 * rank + LANES), shape(rank, features)],
+        [kept, before_out, after_grad, fresh_input, own_out, weight, column_sum, up, other],
+        left=(0, 4),
+        left_outs=(1,),
+        aliases=[(0, 1)],
+        scratch=[tile, tile, sems((3,))],
         name="second",
     )
     got = across(payload)
-    partner0 = mirrored(tokens0)
+    sections = lax.axis_size("section")
+    partner1 = lax.ppermute(own_out, "section", [(i, sections - 2 - i) for i in range(sections - 1)])
     (payload,) = call(
         bound(late_kernel, peers=peers, rank=rank, width=width),
         [shape(rows, 4 * rank + LANES)],
-        [got, columns, active_back, partner0],
-        left=(3,),
+        [got, columns, active_back],
         name="late",
     )
     got1 = across(payload)
-    partner1 = mirrored(tokens1)
-    next_output, input_grad, gain_grad, down_grad, up_grad, stash = call(
+    stash, done = call(
+        stash_kernel,
+        [shape(*held_stash.shape), shape(8, LANES, dtype=F32)],
+        [evict, held_stash, partner0, partner1, fresh_input],
+        smem=(0,),
+        left=(1, 2, 3, 4),
+        left_outs=(0,),
+        scratch=[sems((held_stash.shape[1],))],
+        cost=LONG,
+        name="stash",
+    )
+    up_grad, next_output, input_grad, gain_grad, down_grad = call(
         bound(last_kernel, rank=rank),
         [
+            shape(rank, features),
             shape(rows, features),
             shape(rows, features),
             shape(1, features, dtype=F32),
             shape(features, rank),
-            shape(rank, features),
-            shape(*held_stash.shape),
         ],
-        [
-            evict, held_stash, partner0, partner1, got1, got0, tokens1, fetched1, grad1, grad0, scaled0, gain_term0,
-            norm_gain, down, up,
-        ],
-        smem=(0,),
-        left=(1, 2, 3, 6, 7, 8, 10),
-        left_outs=(5,),
-        scratch=[tile, tile, tile, tile, sems((4,)), sems((held_stash.shape[1],))],
-        products=6,
+        [kept, own_out, done, got1, got0, grad0, gain_term0, norm_gain, down, up],
+        left=(0, 1, 2),
+        left_outs=(0, 1),
+        aliases=[(0, 0), (1, 1)],
+        scratch=[pltpu.VMEM((4 * rows, features), BF16), tile, pltpu.VMEM((rank, features), BF16), sems((3,))],
         name="last",
     )
     return (next_output[None], input_grad[None], stash, gain_grad, down_grad[None], up_grad[None])

time: 148 us -> 139 us (0.939)
  the two profiles are of different devices: /device:TPU:1 before, /device:TPU:2 now
where the time goes in v4:
time: 139 us; the launch traced here: 138 us
  starting transfers between devices  61.3 us (44%)
  waiting for transfers between devices  47.1 us (34%)
  Pallas kernels  22.8 us (16%)
  local copies, waits for them, and re-layouts  5.56 us (4%)
    all_to_all x5, waiting for transfers between devices, across(): return lax.all_to_all(block, 'dp', 0, 0, tiled=True)  44.3 us
    all_to_all x5, starting transfers between devices, across(): return lax.all_to_all(block, 'dp', 0, 0, tiled=True)  30.9 us
    pallas_call x12, Pallas kernels, call(): pl.pallas_call(body, out_shape=tuple(outs), in_specs=[pl.BlockSpec(memory...  22.8 us
    ppermute x3, starting transfers between devices, mirrored(): lax.ppermute(value, 'section', [(i, sections - 1 - i) for i in range(sect...  19.9 us
    ppermute x2, starting transfers between devices, shifted(): return lax.ppermute(value, 'section', pairs)  8.57 us
    unnamed x28, local copies, waits for them, and re-layouts  5.56 us
  transfers between devices with their start and end apart: 11, of which 7 were waited for; matrix products, arithmetic and copies ran while one was open for 0% of the time, Pallas kernels for 11%

profile of v4, /device:TPU:2, one launch (start us, length us, event | category | flops | bytes accessed | tf_op | source)
XLA Modules:
  0.0 137.7 jit_solution(7529183251618184558)
XLA Ops:
  1.3 1.0 copy-done.2
  2.3 1.1 pick.1
  3.4 11.3 %collective-permute-start.1 = (bf16[128,768]{1,0:T(8,128)(2,1)S(1)}, bf16[128,768]{1,0:T(8,128)(2,1)S(1)}, u32[]{:S(2)}, u32[]{:S(2)}) collective-permute-start(bf16[128,768]{1,0:T(8,128)(2,1)S(1)} %get-tuple-element.37), channel_id=1, source_target_pairs={{0,496},{16,480},{32,464},{48,448},{64,432},{80,416},{96,400},{112... | collective-permute-start | bytes 589832 | tf_op jit(solution)/shard_map/ppermute | solution.py:25
  15.4 1.6 %start.1 = (bf16[128,1408]{1,0:T(8,128)(2,1)}, bf16[768,512]{1,0:T(8,128)(2,1)S(1)}, f32[1,512]{1,0:T(1,128)S(1)}) custom-call(bf16[128,768]{1,0:T(8,128)(2,1)S(1)} %bitcast.36, bf16[128,768]{1,0:T(8,128)(2,1)S(1)} %bitcast.40, bf16[1,768]{1,0:T(2,128)(2,1)S(1)} %copy-done.7, bf16[768,512]{1,0:T(8,128)(2,1)S(1)} %bitcast.28, bf16[512,768]{1,0:T(8,128)(2,1)S(1)} %bitcast.32, ...), custom_call_target="tpu_custom_call" | custom-call | flops 12884901888 | bytes 6291456 | tf_op jit(solution)/shard_map/start/pallas_call | solution.py:332
  17.0 0.9 copy-done.10
  17.9 8.1 %all-to-all-start = ((bf16[16,8,1408]{2,1,0:T(8,128)(2,1)}), bf16[16,8,1408]{2,1,0:T(8,128)(2,1)S(1)}, u32[]{:S(2)}, u32[]{:S(2)}) async-start(bf16[16,8,1408]{2,1,0:T(8,128)(2,1)} %bitcast.6), calls=%async_computation | async-start | bytes 720896 | tf_op jit(solution)/shard_map/all_to_all | solution.py:20
  26.0 1.1 copy-done.11
  27.4 13.9 %all-to-all-done = bf16[16,8,1408]{2,1,0:T(8,128)(2,1)S(1)} async-done(((bf16[16,8,1408]{2,1,0:T(8,128)(2,1)}), bf16[16,8,1408]{2,1,0:T(8,128)(2,1)S(1)}, u32[]{:S(2)}, u32[]{:S(2)}) %all-to-all-start) | async-done | bytes 360480 | tf_op jit(solution)/shard_map/all_to_all | solution.py:20
  41.3 0.7 join.1
  42.0 3.5 %all-to-all-start.1 = ((bf16[16,8,640]{2,1,0:T(8,128)(2,1)}), bf16[16,8,640]{2,1,0:T(8,128)(2,1)S(1)}, u32[]{:S(2)}, u32[]{:S(2)}) async-start(bf16[16,8,640]{2,1,0:T(8,128)(2,1)} %bitcast.8), calls=%async_computation.1 | async-start | bytes 327680 | tf_op jit(solution)/shard_map/all_to_all | solution.py:20
  45.5 1.9 %collective-permute-start.2 = (bf16[128,768]{1,0:T(8,128)(2,1)S(1)}, bf16[128,768]{1,0:T(8,128)(2,1)S(1)}, u32[]{:S(2)}, u32[]{:S(2)}) collective-permute-start(bf16[128,768]{1,0:T(8,128)(2,1)S(1)} %bitcast.37), channel_id=1, source_target_pairs={{0,496},{16,480},{32,464},{48,448},{64,432},{80,416},{96,400},{112... | collective-permute-start | bytes 589832 | tf_op jit(solution)/shard_map/ppermute | solution.py:25
  47.4 6.7 %collective-permute-start = (bf16[128,768]{1,0:T(8,128)(2,1)S(1)}, bf16[128,768]{1,0:T(8,128)(2,1)}, u32[]{:S(2)}, u32[]{:S(2)}) collective-permute-start(bf16[128,768]{1,0:T(8,128)(2,1)S(1)} %get-tuple-element.32.refs_5_), channel_id=1, source_target_pairs={{0,496},{16,480},{32,464},{48,448},{64,432},{80,416},{96,400},{112... | collective-permute-start | bytes 589832 | tf_op jit(solution)/shard_map/ppermute | solution.py:25
  54.1 1.4 %all-to-all-done.1 = bf16[16,8,640]{2,1,0:T(8,128)(2,1)S(1)} async-done(((bf16[16,8,640]{2,1,0:T(8,128)(2,1)}), bf16[16,8,640]{2,1,0:T(8,128)(2,1)S(1)}, u32[]{:S(2)}, u32[]{:S(2)}) %all-to-all-start.1) | async-done | bytes 163872 | tf_op jit(solution)/shard_map/all_to_all | solution.py:20
  55.5 1.1 middle.1
  56.7 6.6 %all-to-all-start.2 = ((bf16[16,8,1152]{2,1,0:T(8,128)(2,1)}), bf16[16,8,1152]{2,1,0:T(8,128)(2,1)S(1)}, u32[]{:S(2)}, u32[]{:S(2)}) async-start(bf16[16,8,1152]{2,1,0:T(8,128)(2,1)} %bitcast.10), calls=%async_computation.2 | async-start | bytes 589824 | tf_op jit(solution)/shard_map/all_to_all | solution.py:20
  64.0 1.1 copy-done.12
  65.1 1.7 %other.1 = (bf16[128,640]{1,0:T(8,128)(2,1)S(1)}, bf16[512,768]{1,0:T(8,128)(2,1)}) custom-call(s32[2,32]{1,0:T(2,128)S(1)} %bitcast.45, s32[2,32]{1,0:T(2,128)S(1)} %bitcast.46, bf16[128,768]{1,0:T(8,128)(2,1)} %collective-permute-done.refs_2_, bf16[128,768]{1,0:T(8,128)(2,1)S(1)} %bitcast.38, bf16[768,512]{1,0:T(8,128)(2,1)S(1)} %copy-done.12, ...), custom_call_target="tpu_custom_call" | custom-call | flops 12884901888 | bytes 6291456 | tf_op jit(solution)/shard_map/other/pallas_call | solution.py:332
  66.9 7.8 %all-to-all-done.2 = bf16[16,8,1152]{2,1,0:T(8,128)(2,1)S(1)} async-done(((bf16[16,8,1152]{2,1,0:T(8,128)(2,1)}), bf16[16,8,1152]{2,1,0:T(8,128)(2,1)S(1)}, u32[]{:S(2)}, u32[]{:S(2)}) %all-to-all-start.2) | async-done | bytes 294944 | tf_op jit(solution)/shard_map/all_to_all | solution.py:20
  74.7 1.0 first.1
  75.8 1.9 %collective-permute-start.3 = (bf16[128,768]{1,0:T(8,128)(2,1)S(1)}, bf16[128,768]{1,0:T(8,128)(2,1)S(1)}, u32[]{:S(2)}, u32[]{:S(2)}) collective-permute-start(bf16[128,768]{1,0:T(8,128)(2,1)S(1)} %get-tuple-element.43), channel_id=1, source_target_pairs={{0,16},{16,32},{32,48},{48,64},{64,80},{80,96},{96,112},{112,128},... | collective-permute-start | bytes 589832 | tf_op jit(solution)/shard_map/ppermute | solution.py:31
  77.7 6.7 %collective-permute-start.4 = (bf16[128,768]{1,0:T(8,128)(2,1)S(1)}, bf16[128,768]{1,0:T(8,128)(2,1)S(1)}, u32[]{:S(2)}, u32[]{:S(2)}) collective-permute-start(bf16[128,768]{1,0:T(8,128)(2,1)S(1)} %get-tuple-element.44), channel_id=1, source_target_pairs={{16,0},{32,16},{48,32},{64,48},{80,64},{96,80},{112,96},{128,112},... | collective-permute-start | bytes 589832 | tf_op jit(solution)/shard_map/ppermute | solution.py:31
  84.4 1.0 terms.1
  85.4 2.2 %collective-permute-done.3.refs_1_ = bf16[128,768]{1,0:T(8,128)(2,1)S(1)} collective-permute-done((bf16[128,768]{1,0:T(8,128)(2,1)S(1)}, bf16[128,768]{1,0:T(8,128)(2,1)S(1)}, u32[]{:S(2)}, u32[]{:S(2)}) %collective-permute-start.3) | collective-permute-done | bytes 196640 | tf_op jit(solution)/shard_map/ppermute | solution.py:31
  87.6 1.6 %second.1 = (bf16[128,1664]{1,0:T(8,128)(2,1)}, bf16[512,768]{1,0:T(8,128)(2,1)}) custom-call(bf16[512,768]{1,0:T(8,128)(2,1)} %get-tuple-element.41.refs_0_, bf16[128,768]{1,0:T(8,128)(2,1)S(1)} %collective-permute-done.3.refs_1_, bf16[128,768]{1,0:T(8,128)(2,1)S(1)} %collective-permute-done.4.refs_2_, ...), custom_call_target="tpu_custom_call", output_to_operand_aliasing={{1}: (0, {})} | custom-call | flops 2147483648 | bytes 1048576 | tf_op jit(solution)/shard_map/second/pallas_call | solution.py:332
  89.2 8.9 %all-to-all-start.3 = ((bf16[16,8,1664]{2,1,0:T(8,128)(2,1)}), bf16[16,8,1664]{2,1,0:T(8,128)(2,1)S(1)}, u32[]{:S(2)}, u32[]{:S(2)}) async-start(bf16[16,8,1664]{2,1,0:T(8,128)(2,1)} %bitcast.12), calls=%async_computation.3 | async-start | bytes 851968 | tf_op jit(solution)/shard_map/all_to_all | solution.py:20
  98.1 1.9 %collective-permute-start.5 = (bf16[128,768]{1,0:T(8,128)(2,1)}, bf16[128,768]{1,0:T(8,128)(2,1)}, u32[]{:S(2)}, u32[]{:S(2)}) collective-permute-start(bf16[128,768]{1,0:T(8,128)(2,1)} %get-tuple-element.45.refs_4_.refs_1_), channel_id=1, source_target_pairs={{0,480},{16,464},{32,448},{48,432},{64,416},{80,400},{96,384},{112... | collective-permute-start | bytes 589832 | tf_op jit(solution)/shard_map/ppermute | solution.py:458
  100.0 12.3 %all-to-all-done.3 = bf16[16,8,1664]{2,1,0:T(8,128)(2,1)S(1)} async-done(((bf16[16,8,1664]{2,1,0:T(8,128)(2,1)}), bf16[16,8,1664]{2,1,0:T(8,128)(2,1)S(1)}, u32[]{:S(2)}, u32[]{:S(2)}) %all-to-all-start.3) | async-done | bytes 426016 | tf_op jit(solution)/shard_map/all_to_all | solution.py:20
  112.4 1.1 late.1
  113.4 3.7 %all-to-all-start.4 = ((bf16[16,8,2176]{2,1,0:T(8,128)(2,1)}), bf16[16,8,2176]{2,1,0:T(8,128)(2,1)S(1)}, u32[]{:S(2)}, u32[]{:S(2)}) async-start(bf16[16,8,2176]{2,1,0:T(8,128)(2,1)} %bitcast.14), calls=%async_computation.4 | async-start | bytes 1114112 | tf_op jit(solution)/shard_map/all_to_all | solution.py:20
  117.2 7.6 %stash.4 = (bf16[1,2,128,768]{3,2,1,0:T(8,128)(2,1)}, f32[8,128]{1,0:T(8,128)S(1)}) custom-call(s32[2,32]{1,0:T(2,128)S(1)} %bitcast.47, bf16[1,2,128,768]{3,2,1,0:T(8,128)(2,1)S(1)} %copy-done.3, bf16[128,768]{1,0:T(8,128)(2,1)S(1)} %collective-permute-done.2.refs_6_.partner0, bf16[128,768]{1,0:T(8,128)(2,1)} %collective-permute-done.5.partner1, ...), custom_call_target="tpu_custom_call" | custom-call | flops 12884901888 | bytes 6291456 | tf_op jit(solution)/shard_map/stash/pallas_call | solution.py:332
  124.8 8.9 %all-to-all-done.4 = bf16[16,8,2176]{2,1,0:T(8,128)(2,1)S(1)} async-done(((bf16[16,8,2176]{2,1,0:T(8,128)(2,1)}), bf16[16,8,2176]{2,1,0:T(8,128)(2,1)S(1)}, u32[]{:S(2)}, u32[]{:S(2)}) %all-to-all-start.4) | async-done | bytes 557088 | tf_op jit(solution)/shard_map/all_to_all | solution.py:20
  133.7 4.0 %last.1 = (bf16[512,768]{1,0:T(8,128)(2,1)}, bf16[128,768]{1,0:T(8,128)(2,1)}, bf16[128,768]{1,0:T(8,128)(2,1)}, f32[1,768]{1,0:T(1,128)}, bf16[768,512]{1,0:T(8,128)(2,1)}) custom-call(bf16[512,768]{1,0:T(8,128)(2,1)} %get-tuple-element.46.refs_0_, ...), custom_call_target="tpu_custom_call", output_to_operand_aliasing={{0}: (0, {}), {1}: (1, {})} | custom-call | flops 2147483648 | bytes 1048576 | tf_op jit(solution)/shard_map/last/pallas_call | solution.py:332
  (30 shorter events, 2.3 us)
Async XLA Ops:
  0.6 0.7 copy-start.8
  1.3 1.0 copy-start.2
  2.3 12.4 %copy-start = (bf16[1,768,512]{2,1,0:T(8,128)(2,1)S(1)}, bf16[1,768,512]{2,1,0:T(8,128)(2,1)}, u32[]{:S(2)}) copy-start(bf16[1,768,512]{2,1,0:T(8,128)(2,1)} %param.14) | copy-start | bytes 2359300
  2.3 12.4 %copy-start.1 = (bf16[1,512,768]{2,1,0:T(8,128)(2,1)S(1)}, bf16[1,512,768]{2,1,0:T(8,128)(2,1)}, u32[]{:S(2)}) copy-start(bf16[1,512,768]{2,1,0:T(8,128)(2,1)} %param.15) | copy-start | bytes 2359300
  2.3 12.5 %copy-start.4 = (bf16[1,128,768]{2,1,0:T(8,128)(2,1)S(1)}, bf16[1,128,768]{2,1,0:T(8,128)(2,1)}, u32[]{:S(2)}) copy-start(bf16[1,128,768]{2,1,0:T(8,128)(2,1)} %param.9) | copy-start | bytes 589828
  2.3 12.5 %copy-start.6 = (bf16[1,128,768]{2,1,0:T(8,128)(2,1)S(1)}, bf16[1,128,768]{2,1,0:T(8,128)(2,1)}, u32[]{:S(2)}) copy-start(bf16[1,128,768]{2,1,0:T(8,128)(2,1)} %param.11) | copy-start | bytes 589828
  3.4 22.6 %collective-permute-start.1 = (bf16[128,768]{1,0:T(8,128)(2,1)S(1)}, bf16[128,768]{1,0:T(8,128)(2,1)S(1)}, u32[]{:S(2)}, u32[]{:S(2)}) collective-permute-start(bf16[128,768]{1,0:T(8,128)(2,1)S(1)} %get-tuple-element.37), channel_id=1, source_target_pairs={{0,496},{16,480},{32,464},{48,448},{64,432},{80,416},{96,400},{112... | collective-permute-start | bytes 589832 | tf_op jit(solution)/shard_map/ppermute | solution.py:25
  14.7 0.7 copy-start.7
  17.0 0.9 copy-start.10
  17.9 23.4 %all-to-all-start = ((bf16[16,8,1408]{2,1,0:T(8,128)(2,1)}), bf16[16,8,1408]{2,1,0:T(8,128)(2,1)S(1)}, u32[]{:S(2)}, u32[]{:S(2)}) async-start(bf16[16,8,1408]{2,1,0:T(8,128)(2,1)} %bitcast.6), calls=%async_computation | async-start | bytes 720896 | tf_op jit(solution)/shard_map/all_to_all | solution.py:20
  26.0 1.1 copy-start.11
  42.0 13.5 %all-to-all-start.1 = ((bf16[16,8,640]{2,1,0:T(8,128)(2,1)}), bf16[16,8,640]{2,1,0:T(8,128)(2,1)S(1)}, u32[]{:S(2)}, u32[]{:S(2)}) async-start(bf16[16,8,640]{2,1,0:T(8,128)(2,1)} %bitcast.8), calls=%async_computation.1 | async-start | bytes 327680 | tf_op jit(solution)/shard_map/all_to_all | solution.py:20
  45.5 38.8 %collective-permute-start.2 = (bf16[128,768]{1,0:T(8,128)(2,1)S(1)}, bf16[128,768]{1,0:T(8,128)(2,1)S(1)}, u32[]{:S(2)}, u32[]{:S(2)}) collective-permute-start(bf16[128,768]{1,0:T(8,128)(2,1)S(1)} %bitcast.37), channel_id=1, source_target_pairs={{0,496},{16,480},{32,464},{48,448},{64,432},{80,416},{96,400},{112... | collective-permute-start | bytes 589832 | tf_op jit(solution)/shard_map/ppermute | solution.py:25
  47.4 16.5 %collective-permute-start = (bf16[128,768]{1,0:T(8,128)(2,1)S(1)}, bf16[128,768]{1,0:T(8,128)(2,1)}, u32[]{:S(2)}, u32[]{:S(2)}) collective-permute-start(bf16[128,768]{1,0:T(8,128)(2,1)S(1)} %get-tuple-element.32.refs_5_), channel_id=1, source_target_pairs={{0,496},{16,480},{32,464},{48,448},{64,432},{80,416},{96,400},{112... | collective-permute-start | bytes 589832 | tf_op jit(solution)/shard_map/ppermute | solution.py:25
  56.7 18.0 %all-to-all-start.2 = ((bf16[16,8,1152]{2,1,0:T(8,128)(2,1)}), bf16[16,8,1152]{2,1,0:T(8,128)(2,1)S(1)}, u32[]{:S(2)}, u32[]{:S(2)}) async-start(bf16[16,8,1152]{2,1,0:T(8,128)(2,1)} %bitcast.10), calls=%async_computation.2 | async-start | bytes 589824 | tf_op jit(solution)/shard_map/all_to_all | solution.py:20
  63.3 0.7 copy-start.9
  64.0 1.1 copy-start.12
  75.8 11.9 %collective-permute-start.3 = (bf16[128,768]{1,0:T(8,128)(2,1)S(1)}, bf16[128,768]{1,0:T(8,128)(2,1)S(1)}, u32[]{:S(2)}, u32[]{:S(2)}) collective-permute-start(bf16[128,768]{1,0:T(8,128)(2,1)S(1)} %get-tuple-element.43), channel_id=1, source_target_pairs={{0,16},{16,32},{32,48},{48,64},{64,80},{80,96},{96,112},{112,128},... | collective-permute-start | bytes 589832 | tf_op jit(solution)/shard_map/ppermute | solution.py:31
  77.7 9.9 %collective-permute-start.4 = (bf16[128,768]{1,0:T(8,128)(2,1)S(1)}, bf16[128,768]{1,0:T(8,128)(2,1)S(1)}, u32[]{:S(2)}, u32[]{:S(2)}) collective-permute-start(bf16[128,768]{1,0:T(8,128)(2,1)S(1)} %get-tuple-element.44), channel_id=1, source_target_pairs={{16,0},{32,16},{48,32},{64,48},{80,64},{96,80},{112,96},{128,112},... | collective-permute-start | bytes 589832 | tf_op jit(solution)/shard_map/ppermute | solution.py:31
  84.4 3.3 %copy-start.5 = (bf16[128,768]{1,0:T(8,128)(2,1)S(1)}, bf16[128,768]{1,0:T(8,128)(2,1)}, u32[]{:S(2)}) copy-start(bf16[128,768]{1,0:T(8,128)(2,1)} %fresh.1) | copy-start | bytes 589828
  84.4 3.3 %copy-start.13 = (bf16[768,512]{1,0:T(8,128)(2,1)S(1)}, bf16[768,512]{1,0:T(8,128)(2,1)}, u32[]{:S(2)}) copy-start(bf16[768,512]{1,0:T(8,128)(2,1)} %copy-done.10) | copy-start | bytes 2359300
  89.2 23.2 %all-to-all-start.3 = ((bf16[16,8,1664]{2,1,0:T(8,128)(2,1)}), bf16[16,8,1664]{2,1,0:T(8,128)(2,1)S(1)}, u32[]{:S(2)}, u32[]{:S(2)}) async-start(bf16[16,8,1664]{2,1,0:T(8,128)(2,1)} %bitcast.12), calls=%async_computation.3 | async-start | bytes 851968 | tf_op jit(solution)/shard_map/all_to_all | solution.py:20
  98.1 19.0 %collective-permute-start.5 = (bf16[128,768]{1,0:T(8,128)(2,1)}, bf16[128,768]{1,0:T(8,128)(2,1)}, u32[]{:S(2)}, u32[]{:S(2)}) collective-permute-start(bf16[128,768]{1,0:T(8,128)(2,1)} %get-tuple-element.45.refs_4_.refs_1_), channel_id=1, source_target_pairs={{0,480},{16,464},{32,448},{48,432},{64,416},{80,400},{96,384},{112... | collective-permute-start | bytes 589832 | tf_op jit(solution)/shard_map/ppermute | solution.py:458
  113.4 3.7 %copy-start.3 = (bf16[1,2,128,768]{3,2,1,0:T(8,128)(2,1)S(1)}, bf16[1,2,128,768]{3,2,1,0:T(8,128)(2,1)}, u32[]{:S(2)}) copy-start(bf16[1,2,128,768]{3,2,1,0:T(8,128)(2,1)} %stash.5) | copy-start | bytes 1179652
  113.4 20.2 %all-to-all-start.4 = ((bf16[16,8,2176]{2,1,0:T(8,128)(2,1)}), bf16[16,8,2176]{2,1,0:T(8,128)(2,1)S(1)}, u32[]{:S(2)}, u32[]{:S(2)}) async-start(bf16[16,8,2176]{2,1,0:T(8,128)(2,1)} %bitcast.14), calls=%async_computation.4 | async-start | bytes 1114112 | tf_op jit(solution)/shard_map/all_to_all | solution.py:20

commit v5 on v4

--- a/solution.py
+++ b/solution.py
@@ -136,7 +136,9 @@
         one.wait()
 
 
-def start_kernel(tokens, upstream, gain, down, up, after, payload, weight, column_sum, *, peers, rank):
+def start_kernel(tokens, upstream, gain, down, up, other, payload, weight, column_sum, both, *, peers, rank):
+    both[0] = other[...]
+    both[1] = tokens[...]
     rows, features = tokens.shape
     tall = jnp.broadcast_to(gain[...].astype(F32), (LANES, features)).T
     exact = down[...].astype(F32) * jnp.concatenate([tall] * (rank // LANES), axis=1)
@@ -158,17 +160,15 @@
     payload[:, 2 * rank + half :] = in_lanes(sums).astype(BF16)
 
 
-def fetched_kernel(tokens, weight, column_sum, part, sums):
-    part[...], columns = hidden_part(tokens[...], weight[...], column_sum[...])
-    sums[...] = in_lanes(columns)
-
-
-def join_kernel(part, sums, after, payload, *, rank):
-    payload[:, :rank] = part[...].astype(BF16)
-    payload[:, rank:] = sums[...].astype(BF16)
-
-
-def middle_kernel(got, got_b, payload, columns_out, active_back, columns, sems, *, peers, rank, width):
+def fetched_kernel(tokens, weight, column_sum, early, payload, *, rank):
+    part, sums = hidden_part(tokens[...], weight[...], column_sum[...])
+    block = early.shape[1] - LANES
+    payload[:, :block] = early[:, :block]
+    payload[:, block : block + rank] = part.astype(BF16)
+    payload[:, block + rank :] = (early[:, block:].astype(F32) + in_lanes([0.0] * 6 + sums)).astype(BF16)
+
+
+def middle_kernel(got, payload, columns_out, active_back, columns, sems, *, peers, rank, width):
     half = rank // 2
     blocks = got[:, 2 * rank : 2 * rank + half].astype(F32).reshape(peers, -1, half)
     row = lax.broadcasted_iota(jnp.int32, blocks.shape[1:], 0)
@@ -186,10 +186,12 @@
     columns[peers : peers + 1, :] = column_exact
     columns[peers + 1 :, :] = jnp.zeros((7, rank), F32)
     (saved,) = copies([(columns, columns_out)], sems)
-    sums = got[:, 2 * rank + half :].astype(F32)
+    sums = got[:, 3 * rank + half :].astype(F32)
     hidden_f = finish_hidden(got[:, :rank], sums, 0, column_sums, width)[0]
     slope = summed(got[:, rank : 2 * rank], peers)
-    hidden, mean, inverse = finish_hidden(got_b[:, :rank], got_b[:, rank:].astype(F32), 0, column_sums, width)
+    hidden, mean, inverse = finish_hidden(
+        got[:, 2 * rank + half : 3 * rank + half], sums, 6, column_sums, width
+    )
     active, bent = gelu_and_slope(hidden)
     active_back[...] = active
     grad_hidden = (slope * bent).astype(BF16)
@@ -199,22 +201,20 @@
     saved.wait()
 
 
-def first_kernel(got, tokens, fetched, upstream, gain, down, up, after, out, grad, out_kept, sems, *, rank):
+def first_kernel(got, tokens, fetched, upstream, gain, down, up, after, out, grad, *, rank):
     out[...] = (
         tokens[...].astype(F32) + jnp.dot(got[:, :rank], up[...], preferred_element_type=F32)
     ).astype(BF16)
-    (saved,) = copies([(out, out_kept)], sems)
     grad[...] = backward(
         fetched[...], upstream[...], got[:, rank : 2 * rank], got[:, 2 * rank :].astype(F32), gain[...].astype(F32), down[...]
     )[0]
-    saved.wait()
 
 
 def other_kernel(
     fetch, evict, arrived, tokens, weight, column_sum, payload, kept, chosen, sems, *, rank
 ):
     place = lax.axis_index("section")
-    chosen[...] = jnp.where(fetch[1, place] == evict[0, place], tokens[...], arrived[...])
+    chosen[...] = jnp.where(fetch[1, place] == evict[0, place], tokens[...], arrived[0])
     (saved,) = copies([(chosen, kept.at[pl.ds(0, tokens.shape[0])])], sems)
     part, sums = hidden_part(chosen[...], weight[...], column_sum[...])
     payload[:, :rank] = part.astype(BF16)
@@ -223,7 +223,7 @@
 
 
 def terms_kernel(
-    kept_in, got, fetched, upstream, gain, down, after, kept, gain_term, scaled, sems, *, rank
+    kept_in, got, fetched, upstream, gain, down, kept, gain_term, scaled, sems, *, rank
 ):
     scaled[...], gain_term[...] = backward(
         fetched[...], upstream[...], got[:, rank : 2 * rank], got[:, 2 * rank :].astype(F32), gain[...].astype(F32), down[...]
@@ -234,22 +234,16 @@
 
 
 def second_kernel(
-    kept_in, before, after, fresh, own, weight, column_sum, up, side, payload, kept, tokens, upstream, sems, *, rank
+    kept_in, before, after, fresh, own, weight, column_sum, up, side, payload, kept, tokens_out, tokens, upstream, sems,
+    *, rank
 ):
     place = lax.axis_index("section")
     rows = before.shape[0]
     tokens[...] = jnp.where(place == 0, fresh[...], before[...])
-    first = pltpu.make_async_copy(tokens, kept.at[pl.ds(2 * rows, rows)], sems.at[0])
+    first = pltpu.make_async_copy(tokens, tokens_out, sems.at[0])
     first.start()
-    upstream[...] = after[...]
-
-    @pl.when(place == lax.axis_size("section") - 1)
-    def _():
-        late = pltpu.make_async_copy(own, upstream, sems.at[2])
-        late.start()
-        late.wait()
-
-    second = pltpu.make_async_copy(upstream, kept.at[pl.ds(3 * rows, rows)], sems.at[1])
+    upstream[...] = jnp.where(place == lax.axis_size("section") - 1, own[...], after[...])
+    second = pltpu.make_async_copy(upstream, kept.at[pl.ds(2 * rows, rows)], sems.at[1])
     second.start()
     part, sums = hidden_part(tokens[...], weight[...], column_sum[...])
     payload[:, :rank] = part.astype(BF16)
@@ -276,15 +270,14 @@
     payload[:, 4 * rank :] = to_all(stats, peers)
 
 
-def stash_kernel(evict, stash, partner0, partner1, fresh, stash_out, done, sems):
+def stash_kernel(evict, stash, arrived, partner1, stash_out, done, sems):
     slots = stash.shape[1]
     partner = lax.axis_size("section") - 1 - lax.axis_index("section")
     early, late = evict[0, partner], evict[1, partner]
     for i in range(slots):
         for source, taken in (
-            (partner1, (late == i) & (partner != 0)),
-            (fresh, (late == i) & (partner == 0)),
-            (partner0, (late != i) & (early == i)),
+            (partner1, late == i),
+            (arrived.at[1], (late != i) & (early == i)),
             (stash.at[0, i], (late != i) & (early != i)),
         ):
             @pl.when(taken)
@@ -297,33 +290,49 @@
 
 
 def last_kernel(
-    kept_in, own, done, got, got0, upstream0, gain_term0, gain, down, up,
-    up_grad_out, out_out, grad, gain_grad, down_grad, kept, out, up_grad, sems, *, rank
+    kept_in, tokens_in, done, got, got0, upstream0, gain_term0, gain, down, up,
+    up_grad_out, out_out, grad_out, gain_grad, down_grad_out, kept, tokens, up_grad, out, grad, down_grad, sems, *, rank
 ):
     rows = upstream0.shape[0]
-    (load,) = copies([(kept_in, kept)], sems)
+    span = pl.ds(2 * rows, rows)
+    loads = copies(
+        [
+            (kept_in.at[span], kept.at[span]),
+            (tokens_in, tokens),
+            (kept_in.at[pl.ds(0, 2 * rows)], kept.at[pl.ds(0, 2 * rows)]),
+        ],
+        sems,
+    )
     product = jnp.dot(got[:, :rank], up[...], preferred_element_type=F32)
-    load.wait()
-    out[...] = (kept[2 * rows : 3 * rows].astype(F32) + product).astype(BF16)
-    first = pltpu.make_async_copy(out, out_out, sems.at[1])
-    first.start()
-    upstream = kept[3 * rows :]
+    loads[0].wait()
+    upstream = kept[2 * rows : 3 * rows]
     up_grad[...] = transposed_times(
         jnp.concatenate([got[:, 3 * rank : 4 * rank], got[:, 2 * rank : 3 * rank]], axis=0),
         jnp.concatenate([upstream0[...], upstream], axis=0),
     ).astype(BF16)
-    second = pltpu.make_async_copy(up_grad, up_grad_out, sems.at[2])
-    second.start()
+    loads[1].wait()
+    out[...] = (tokens[...].astype(F32) + product).astype(BF16)
+    loads[2].wait()
+    stores = [
+        pltpu.make_async_copy(up_grad, up_grad_out, sems.at[3]),
+        pltpu.make_async_copy(out, out_out, sems.at[4]),
+        pltpu.make_async_copy(down_grad, down_grad_out, sems.at[5]),
+        pltpu.make_async_copy(grad, grad_out, sems.at[6]),
+    ]
+    stores[0].start()
+    stores[1].start()
     grad[...], scaled, gain_term = backward(
         kept[:rows], upstream, got[:, rank : 2 * rank], got[:, 4 * rank :].astype(F32), gain[...].astype(F32), down[...]
     )
+    stores[3].start()
     gain_grad[...] = gain_term0[...] + gain_term
     down_grad[...] = transposed_times(
         jnp.concatenate([kept[rows : 2 * rows], scaled], axis=0),
         jnp.concatenate([got0[:, rank : 2 * rank], got[:, rank : 2 * rank]], axis=0),
     ).astype(BF16)
-    first.wait()
-    second.wait()
+    stores[2].start()
+    for one in stores:
+        one.wait()
 
 
 def call(body, outs, operands, cost=1, smem=(), left=(), left_outs=(), scratch=(), aliases=(), name=None):
@@ -366,7 +375,7 @@
     sems = pltpu.SemaphoreType.DMA
     fetch, evict = fetch_slot.T, evict_slot.T
 
-    picked0, picked1 = call(
+    picked, other = call(
         pick_kernel,
         [shape(rows, features), shape(rows, features)],
         [fetch, held_stash],
@@ -375,36 +384,25 @@
         scratch=[sems((2,))],
         name="pick",
     )
-    fetched0 = mirrored(picked0)
-    payload, weight, column_sum = call(
+    fetched0 = mirrored(picked)
+    early, weight, column_sum, both = call(
         bound(start_kernel, peers=peers, rank=rank),
-        [shape(rows, 2 * rank + half + LANES), shape(features, rank), shape(1, rank, dtype=F32)],
-        [tokens0, grad0, norm_gain, down, up, picked1],
-        left=(5,),
-        cost=LONG,
+        [shape(rows, 2 * rank + half + LANES), shape(features, rank), shape(1, rank, dtype=F32), shape(2, rows, features)],
+        [tokens0, grad0, norm_gain, down, up, other],
         name="start",
     )
-    got_a = across(payload)
-    part, sums = call(
-        fetched_kernel,
-        [shape(rows, rank, dtype=F32), shape(rows, LANES, dtype=F32)],
-        [fetched0, weight, column_sum],
-        cost=LONG,
+    (payload,) = call(
+        bound(fetched_kernel, rank=rank),
+        [shape(rows, 3 * rank + half + LANES)],
+        [fetched0, weight, column_sum, early],
         name="fetched",
     )
-    (payload,) = call(
-        bound(join_kernel, rank=rank),
-        [shape(rows, rank + LANES)],
-        [part, sums, got_a],
-        left=(2,),
-        name="join",
-    )
-    got_b = across(payload)
-    arrived1 = mirrored(picked1)
+    got = across(payload)
+    both = mirrored(both)
     payload, columns, active_back = call(
         bound(middle_kernel, peers=peers, rank=rank, width=width),
         [shape(rows, 2 * rank + LANES), shape(peers + 8, rank, dtype=F32), shape(own, rank, dtype=F32)],
-        [got_a, got_b],
+        [got],
         left_outs=(1,),
         scratch=[pltpu.VMEM((peers + 8, rank), F32), sems((1,))],
         name="middle",
@@ -413,49 +411,45 @@
     other, kept = call(
         bound(other_kernel, rank=rank),
         [shape(rows, rank + LANES), shape(rank, features)],
-        [fetch, evict, arrived1, tokens0, weight, column_sum],
+        [fetch, evict, both, tokens0, weight, column_sum],
         smem=(0, 1),
         left_outs=(1,),
         scratch=[tile, sems((1,))],
         cost=LONG,
         name="other",
     )
-    first_out, first_grad, own_out = call(
+    first_out, first_grad = call(
         bound(first_kernel, rank=rank),
-        [shape(rows, features)] * 3,
+        [shape(rows, features)] * 2,
         [got0, tokens0, fetched0, grad0, norm_gain, down, up, other],
         left=(7,),
-        left_outs=(2,),
-        scratch=[sems((1,))],
         name="first",
     )
     before_out = shifted(first_out, 1)
     after_grad = shifted(first_grad, -1)
-    partner0 = mirrored(tokens0)
     kept, gain_term0 = call(
         bound(terms_kernel, rank=rank),
         [shape(rank, features), shape(1, features, dtype=F32)],
-        [kept, got0, fetched0, grad0, norm_gain, down, partner0],
-        left=(0, 6),
+        [kept, got0, fetched0, grad0, norm_gain, down],
+        left=(0,),
         left_outs=(0,),
         aliases=[(0, 0)],
         scratch=[tile, sems((1,))],
         cost=LONG,
         name="terms",
     )
-    payload, kept = call(
+    payload, kept, tokens1 = call(
         bound(second_kernel, rank=rank),
-        [shape(rows, 3 * rank + LANES), shape(rank, features)],
-        [kept, before_out, after_grad, fresh_input, own_out, weight, column_sum, up, other],
-        left=(0, 4),
-        left_outs=(1,),
+        [shape(rows, 3 * rank + LANES), shape(rank, features), shape(rows, features)],
+        [kept, before_out, after_grad, fresh_input, first_out, weight, column_sum, up, other],
+        left=(0,),
+        left_outs=(1, 2),
         aliases=[(0, 1)],
-        scratch=[tile, tile, sems((3,))],
+        scratch=[tile, tile, sems((2,))],
         name="second",
     )
     got = across(payload)
-    sections = lax.axis_size("section")
-    partner1 = lax.ppermute(own_out, "section", [(i, sections - 2 - i) for i in range(sections - 1)])
+    partner1 = mirrored(tokens1)
     (payload,) = call(
         bound(late_kernel, peers=peers, rank=rank, width=width),
         [shape(rows, 4 * rank + LANES)],
@@ -466,9 +460,9 @@
     stash, done = call(
         stash_kernel,
         [shape(*held_stash.shape), shape(8, LANES, dtype=F32)],
-        [evict, held_stash, partner0, partner1, fresh_input],
+        [evict, held_stash, both, partner1],
         smem=(0,),
-        left=(1, 2, 3, 4),
+        left=(1, 2, 3),
         left_outs=(0,),
         scratch=[sems((held_stash.shape[1],))],
         cost=LONG,
@@ -483,11 +477,19 @@
             shape(1, features, dtype=F32),
             shape(features, rank),
         ],
-        [kept, own_out, done, got1, got0, grad0, gain_term0, norm_gain, down, up],
+        [kept, tokens1, done, got1, got0, grad0, gain_term0, norm_gain, down, up],
         left=(0, 1, 2),
-        left_outs=(0, 1),
+        left_outs=(0, 1, 2, 4),
         aliases=[(0, 0), (1, 1)],
-        scratch=[pltpu.VMEM((4 * rows, features), BF16), tile, pltpu.VMEM((rank, features), BF16), sems((3,))],
+        scratch=[
+            pltpu.VMEM((3 * rows, features), BF16),
+            tile,
+            pltpu.VMEM((rank, features), BF16),
+            tile,
+            tile,
+            pltpu.VMEM((features, rank), BF16),
+            sems((7,)),
+        ],
         name="last",
     )
     return (next_output[None], input_grad[None], stash, gain_grad, down_grad[None], up_grad[None])

time: 139 us -> 127 us (0.914)
  the two profiles are of different devices: /device:TPU:2 before, /device:TPU:1 now
where the time goes in v5:
time: 127 us; the launch traced here: 124 us
  starting transfers between devices  62.3 us (49%)
  waiting for transfers between devices  36.2 us (29%)
  Pallas kernels  21.5 us (17%)
  local copies, waits for them, and re-layouts  3.5 us (3%)
    ppermute x3, starting transfers between devices, mirrored(): lax.ppermute(value, 'section', [(i, sections - 1 - i) for i in range(sect...  32.6 us
    all_to_all x4, waiting for transfers between devices, across(): return lax.all_to_all(block, 'dp', 0, 0, tiled=True)  22.7 us
    all_to_all x4, starting transfers between devices, across(): return lax.all_to_all(block, 'dp', 0, 0, tiled=True)  22.3 us
    pallas_call x11, Pallas kernels, call(): pl.pallas_call(body, out_shape=tuple(outs), in_specs=[pl.BlockSpec(memory...  21.5 us
    ppermute x3, waiting for transfers between devices, mirrored(): lax.ppermute(value, 'section', [(i, sections - 1 - i) for i in range(sect...  11.3 us
    ppermute x2, starting transfers between devices, shifted(): return lax.ppermute(value, 'section', pairs)  7.44 us
    unnamed x34, local copies, waits for them, and re-layouts  3.5 us
  transfers between devices with their start and end apart: 9, of which 7 were waited for; matrix products, arithmetic and copies ran while one was open for 0% of the time, Pallas kernels for 11%

profile of v5, /device:TPU:1, one launch (start us, length us, event | category | flops | bytes accessed | tf_op | source)
XLA Modules:
  0.0 124.4 jit_solution(12737966720105675953)
XLA Ops:
  0.6 0.7 copy-done.12
  1.3 1.0 copy-done.2
  2.3 1.1 pick.1
  3.4 14.2 %collective-permute-start.1 = (bf16[128,768]{1,0:T(8,128)(2,1)S(1)}, bf16[128,768]{1,0:T(8,128)(2,1)S(1)}, u32[]{:S(2)}, u32[]{:S(2)}) collective-permute-start(bf16[128,768]{1,0:T(8,128)(2,1)S(1)} %get-tuple-element.36), channel_id=1, source_target_pairs={{0,496},{16,480},{32,464},{48,448},{64,432},{80,416},{96,400},{112... | collective-permute-start | bytes 589832 | tf_op jit(solution)/shard_map/ppermute | solution.py:25
  17.7 0.6 copy-done.11
  18.4 0.8 start.1
  19.2 0.0 copy-start.14
  19.2 7.4 %collective-permute-done.1.refs_0_.refs_2_ = bf16[128,768]{1,0:T(8,128)(2,1)S(1)} collective-permute-done((bf16[128,768]{1,0:T(8,128)(2,1)S(1)}, bf16[128,768]{1,0:T(8,128)(2,1)S(1)}, u32[]{:S(2)}, u32[]{:S(2)}) %collective-permute-start.1) | collective-permute-done | bytes 196640 | tf_op jit(solution)/shard_map/ppermute | solution.py:25
  26.6 1.1 fetched.1
  27.6 7.9 %all-to-all-start = ((bf16[16,8,1920]{2,1,0:T(8,128)(2,1)}), bf16[16,8,1920]{2,1,0:T(8,128)(2,1)S(1)}, u32[]{:S(2)}, u32[]{:S(2)}) async-start(bf16[16,8,1920]{2,1,0:T(8,128)(2,1)} %bitcast.6), calls=%async_computation | async-start | bytes 983040 | tf_op jit(solution)/shard_map/all_to_all | solution.py:20
  35.6 7.9 %collective-permute-start = (bf16[2,128,768]{2,1,0:T(8,128)(2,1)S(1)}, bf16[2,128,768]{2,1,0:T(8,128)(2,1)S(1)}, u32[]{:S(2)}, u32[]{:S(2)}) collective-permute-start(bf16[2,128,768]{2,1,0:T(8,128)(2,1)S(1)} %get-tuple-element.32), channel_id=1, source_target_pairs={{0,496},{16,480},{32,464},{48,448},{64,432},{80,416},{96,400},{112... | collective-permute-start | bytes 1179656 | tf_op jit(solution)/shard_map/ppermute | solution.py:25
  43.5 7.5 %all-to-all-done = bf16[16,8,1920]{2,1,0:T(8,128)(2,1)S(1)} async-done(((bf16[16,8,1920]{2,1,0:T(8,128)(2,1)}), bf16[16,8,1920]{2,1,0:T(8,128)(2,1)S(1)}, u32[]{:S(2)}, u32[]{:S(2)}) %all-to-all-start) | async-done | bytes 491552 | tf_op jit(solution)/shard_map/all_to_all | solution.py:20
  50.9 1.1 middle.1
  52.1 4.8 %all-to-all-start.1 = ((bf16[16,8,1152]{2,1,0:T(8,128)(2,1)}), bf16[16,8,1152]{2,1,0:T(8,128)(2,1)S(1)}, u32[]{:S(2)}, u32[]{:S(2)}) async-start(bf16[16,8,1152]{2,1,0:T(8,128)(2,1)} %bitcast.8), calls=%async_computation.1 | async-start | bytes 589824 | tf_op jit(solution)/shard_map/all_to_all | solution.py:20
  56.9 3.9 %collective-permute-done.refs_2_.arrived = bf16[2,128,768]{2,1,0:T(8,128)(2,1)S(1)} collective-permute-done((bf16[2,128,768]{2,1,0:T(8,128)(2,1)S(1)}, bf16[2,128,768]{2,1,0:T(8,128)(2,1)S(1)}, u32[]{:S(2)}, u32[]{:S(2)}) %collective-permute-start) | collective-permute-done | bytes 393248 | tf_op jit(solution)/shard_map/ppermute | solution.py:25
  60.8 1.1 copy-done.15
  61.9 1.4 %other.1 = (bf16[128,640]{1,0:T(8,128)(2,1)S(1)}, bf16[512,768]{1,0:T(8,128)(2,1)}) custom-call(s32[2,32]{1,0:T(2,128)S(1)} %bitcast.40, s32[2,32]{1,0:T(2,128)S(1)} %bitcast.41, bf16[2,128,768]{2,1,0:T(8,128)(2,1)S(1)} %collective-permute-done.refs_2_.arrived, bf16[128,768]{1,0:T(8,128)(2,1)S(1)} %bitcast.33, bf16[768,512]{1,0:T(8,128)(2,1)S(1)} %copy-done.15, ...), custom_call_target="tpu_custom_call" | custom-call | flops 12884901888 | bytes 6291456 | tf_op jit(solution)/shard_map/other/pallas_call | solution.py:341
  63.3 3.7 %all-to-all-done.1 = bf16[16,8,1152]{2,1,0:T(8,128)(2,1)S(1)} async-done(((bf16[16,8,1152]{2,1,0:T(8,128)(2,1)}), bf16[16,8,1152]{2,1,0:T(8,128)(2,1)S(1)}, u32[]{:S(2)}, u32[]{:S(2)}) %all-to-all-start.1) | async-done | bytes 294944 | tf_op jit(solution)/shard_map/all_to_all | solution.py:20
  67.0 0.5 first.1
  67.5 5.5 %collective-permute-start.3 = (bf16[128,768]{1,0:T(8,128)(2,1)S(1)}, bf16[128,768]{1,0:T(8,128)(2,1)S(1)}, u32[]{:S(2)}, u32[]{:S(2)}) collective-permute-start(bf16[128,768]{1,0:T(8,128)(2,1)S(1)} %get-tuple-element.42), channel_id=1, source_target_pairs={{16,0},{32,16},{48,32},{64,48},{80,64},{96,80},{112,96},{128,112},... | collective-permute-start | bytes 589832 | tf_op jit(solution)/shard_map/ppermute | solution.py:31
  73.1 1.9 %collective-permute-start.2 = (bf16[128,768]{1,0:T(8,128)(2,1)S(1)}, bf16[128,768]{1,0:T(8,128)(2,1)S(1)}, u32[]{:S(2)}, u32[]{:S(2)}) collective-permute-start(bf16[128,768]{1,0:T(8,128)(2,1)S(1)} %get-tuple-element.41.refs_4_), channel_id=1, source_target_pairs={{0,16},{16,32},{32,48},{48,64},{64,80},{80,96},{96,112},{112,128},... | collective-permute-start | bytes 589832 | tf_op jit(solution)/shard_map/ppermute | solution.py:31
  75.0 1.0 terms.1
  76.0 2.2 %collective-permute-done.3.refs_2_ = bf16[128,768]{1,0:T(8,128)(2,1)S(1)} collective-permute-done((bf16[128,768]{1,0:T(8,128)(2,1)S(1)}, bf16[128,768]{1,0:T(8,128)(2,1)S(1)}, u32[]{:S(2)}, u32[]{:S(2)}) %collective-permute-start.3) | collective-permute-done | bytes 196640 | tf_op jit(solution)/shard_map/ppermute | solution.py:31
  78.3 1.8 %second.1 = (bf16[128,1664]{1,0:T(8,128)(2,1)}, bf16[512,768]{1,0:T(8,128)(2,1)}, bf16[128,768]{1,0:T(8,128)(2,1)}) custom-call(bf16[512,768]{1,0:T(8,128)(2,1)} %get-tuple-element.39.refs_0_, bf16[128,768]{1,0:T(8,128)(2,1)S(1)} %collective-permute-done.2.refs_1_, ...), custom_call_target="tpu_custom_call", output_to_operand_aliasing={{1}: (0, {})} | custom-call | flops 2147483648 | bytes 1048576 | tf_op jit(solution)/shard_map/second/pallas_call | solution.py:341
  80.1 4.7 %all-to-all-start.2 = ((bf16[16,8,1664]{2,1,0:T(8,128)(2,1)}), bf16[16,8,1664]{2,1,0:T(8,128)(2,1)S(1)}, u32[]{:S(2)}, u32[]{:S(2)}) async-start(bf16[16,8,1664]{2,1,0:T(8,128)(2,1)} %bitcast.10), calls=%async_computation.2 | async-start | bytes 851968 | tf_op jit(solution)/shard_map/all_to_all | solution.py:20
  84.8 10.5 %collective-permute-start.4 = (bf16[128,768]{1,0:T(8,128)(2,1)}, bf16[128,768]{1,0:T(8,128)(2,1)}, u32[]{:S(2)}, u32[]{:S(2)}) collective-permute-start(bf16[128,768]{1,0:T(8,128)(2,1)} %get-tuple-element.44.refs_1_), channel_id=1, source_target_pairs={{0,496},{16,480},{32,464},{48,448},{64,432},{80,416},{96,400},{112... | collective-permute-start | bytes 589832 | tf_op jit(solution)/shard_map/ppermute | solution.py:25
  95.3 3.1 %all-to-all-done.2 = bf16[16,8,1664]{2,1,0:T(8,128)(2,1)S(1)} async-done(((bf16[16,8,1664]{2,1,0:T(8,128)(2,1)}), bf16[16,8,1664]{2,1,0:T(8,128)(2,1)S(1)}, u32[]{:S(2)}, u32[]{:S(2)}) %all-to-all-start.2) | async-done | bytes 426016 | tf_op jit(solution)/shard_map/all_to_all | solution.py:20
  98.4 1.1 late.1
  99.5 4.8 %all-to-all-start.3 = ((bf16[16,8,2176]{2,1,0:T(8,128)(2,1)}), bf16[16,8,2176]{2,1,0:T(8,128)(2,1)S(1)}, u32[]{:S(2)}, u32[]{:S(2)}) async-start(bf16[16,8,2176]{2,1,0:T(8,128)(2,1)} %bitcast.12), calls=%async_computation.3 | async-start | bytes 1114112 | tf_op jit(solution)/shard_map/all_to_all | solution.py:20
  104.4 7.6 %stash.4 = (bf16[1,2,128,768]{3,2,1,0:T(8,128)(2,1)}, f32[8,128]{1,0:T(8,128)S(1)}) custom-call(s32[2,32]{1,0:T(2,128)S(1)} %bitcast.42, bf16[1,2,128,768]{3,2,1,0:T(8,128)(2,1)S(1)} %copy-done.3, bf16[2,128,768]{2,1,0:T(8,128)(2,1)S(1)} %collective-permute-done.refs_2_.arrived, bf16[128,768]{1,0:T(8,128)(2,1)} %collective-permute-done.4.partner1), custom_call_target="tpu_custom_call" | custom-call | flops 12884901888 | bytes 6291456 | tf_op jit(solution)/shard_map/stash/pallas_call | solution.py:341
  112.0 8.4 %all-to-all-done.3 = bf16[16,8,2176]{2,1,0:T(8,128)(2,1)S(1)} async-done(((bf16[16,8,2176]{2,1,0:T(8,128)(2,1)}), bf16[16,8,2176]{2,1,0:T(8,128)(2,1)S(1)}, u32[]{:S(2)}, u32[]{:S(2)}) %all-to-all-start.3) | async-done | bytes 557088 | tf_op jit(solution)/shard_map/all_to_all | solution.py:20
  120.4 4.0 %last.1 = (bf16[512,768]{1,0:T(8,128)(2,1)}, bf16[128,768]{1,0:T(8,128)(2,1)}, bf16[128,768]{1,0:T(8,128)(2,1)}, f32[1,768]{1,0:T(1,128)}, bf16[768,512]{1,0:T(8,128)(2,1)}) custom-call(bf16[512,768]{1,0:T(8,128)(2,1)} %get-tuple-element.43.refs_0_, bf16[128,768]{1,0:T(8,128)(2,1)} %get-tuple-element.44.refs_1_, ...), custom_call_target="tpu_custom_call", output_to_operand_aliasing={{0}: (0, {}), {1}: (1, {})} | custom-call | flops 2147483648 | bytes 1048576 | tf_op jit(solution)/shard_map/last/pallas_call | solution.py:341
  (31 shorter events, 0.1 us)
Async XLA Ops:
  0.6 0.7 copy-start.12
  1.3 1.0 copy-start.2
  2.3 15.4 %copy-start = (bf16[1,768,512]{2,1,0:T(8,128)(2,1)S(1)}, bf16[1,768,512]{2,1,0:T(8,128)(2,1)}, u32[]{:S(2)}) copy-start(bf16[1,768,512]{2,1,0:T(8,128)(2,1)} %param.14) | copy-start | bytes 2359300
  2.3 15.4 %copy-start.1 = (bf16[1,512,768]{2,1,0:T(8,128)(2,1)S(1)}, bf16[1,512,768]{2,1,0:T(8,128)(2,1)}, u32[]{:S(2)}) copy-start(bf16[1,512,768]{2,1,0:T(8,128)(2,1)} %param.15) | copy-start | bytes 2359300
  2.3 15.4 %copy-start.4 = (bf16[1,128,768]{2,1,0:T(8,128)(2,1)S(1)}, bf16[1,128,768]{2,1,0:T(8,128)(2,1)}, u32[]{:S(2)}) copy-start(bf16[1,128,768]{2,1,0:T(8,128)(2,1)} %param.9) | copy-start | bytes 589828
  2.3 15.4 %copy-start.6 = (bf16[1,128,768]{2,1,0:T(8,128)(2,1)S(1)}, bf16[1,128,768]{2,1,0:T(8,128)(2,1)}, u32[]{:S(2)}) copy-start(bf16[1,128,768]{2,1,0:T(8,128)(2,1)} %param.11) | copy-start | bytes 589828
  3.4 23.1 %collective-permute-start.1 = (bf16[128,768]{1,0:T(8,128)(2,1)S(1)}, bf16[128,768]{1,0:T(8,128)(2,1)S(1)}, u32[]{:S(2)}, u32[]{:S(2)}) collective-permute-start(bf16[128,768]{1,0:T(8,128)(2,1)S(1)} %get-tuple-element.36), channel_id=1, source_target_pairs={{0,496},{16,480},{32,464},{48,448},{64,432},{80,416},{96,400},{112... | collective-permute-start | bytes 589832 | tf_op jit(solution)/shard_map/ppermute | solution.py:25
  17.7 0.7 copy-start.11
  19.2 8.4 %copy-start.14 = (bf16[768,512]{1,0:T(8,128)(2,1)}, bf16[768,512]{1,0:T(8,128)(2,1)S(1)}, u32[]{:S(2)}) copy-start(bf16[768,512]{1,0:T(8,128)(2,1)S(1)} %get-tuple-element.33.refs_4_.refs_1_.refs_5_) | copy-start | bytes 2359300
  26.6 1.1 copy-start.9
  27.6 23.3 %all-to-all-start = ((bf16[16,8,1920]{2,1,0:T(8,128)(2,1)}), bf16[16,8,1920]{2,1,0:T(8,128)(2,1)S(1)}, u32[]{:S(2)}, u32[]{:S(2)}) async-start(bf16[16,8,1920]{2,1,0:T(8,128)(2,1)} %bitcast.6), calls=%async_computation | async-start | bytes 983040 | tf_op jit(solution)/shard_map/all_to_all | solution.py:20
  35.6 25.2 %collective-permute-start = (bf16[2,128,768]{2,1,0:T(8,128)(2,1)S(1)}, bf16[2,128,768]{2,1,0:T(8,128)(2,1)S(1)}, u32[]{:S(2)}, u32[]{:S(2)}) collective-permute-start(bf16[2,128,768]{2,1,0:T(8,128)(2,1)S(1)} %get-tuple-element.32), channel_id=1, source_target_pairs={{0,496},{16,480},{32,464},{48,448},{64,432},{80,416},{96,400},{112... | collective-permute-start | bytes 1179656 | tf_op jit(solution)/shard_map/ppermute | solution.py:25
  52.1 14.9 %all-to-all-start.1 = ((bf16[16,8,1152]{2,1,0:T(8,128)(2,1)}), bf16[16,8,1152]{2,1,0:T(8,128)(2,1)S(1)}, u32[]{:S(2)}, u32[]{:S(2)}) async-start(bf16[16,8,1152]{2,1,0:T(8,128)(2,1)} %bitcast.8), calls=%async_computation.1 | async-start | bytes 589824 | tf_op jit(solution)/shard_map/all_to_all | solution.py:20
  56.8 3.9 %copy-start.13 = (s32[32,2]{0,1:T(2,128)S(1)}, s32[32,2]{0,1:T(2,128)}, u32[]{:S(2)}) copy-start(s32[32,2]{0,1:T(2,128)} %param.17) | copy-start | bytes 772
  60.8 1.1 copy-start.15
  61.9 5.1 %copy-start.7 = (bf16[1,128,768]{2,1,0:T(8,128)(2,1)S(1)}, bf16[1,128,768]{2,1,0:T(8,128)(2,1)}, u32[]{:S(2)}) copy-start(bf16[1,128,768]{2,1,0:T(8,128)(2,1)} %param.11) | copy-start | bytes 589828
  61.9 5.1 %copy-start.10 = (bf16[128,768]{1,0:T(8,128)(2,1)S(1)}, bf16[128,768]{1,0:T(8,128)(2,1)}, u32[]{:S(2)}) copy-start(bf16[128,768]{1,0:T(8,128)(2,1)} %copy-done.9) | copy-start | bytes 589828
  67.5 10.7 %collective-permute-start.3 = (bf16[128,768]{1,0:T(8,128)(2,1)S(1)}, bf16[128,768]{1,0:T(8,128)(2,1)S(1)}, u32[]{:S(2)}, u32[]{:S(2)}) collective-permute-start(bf16[128,768]{1,0:T(8,128)(2,1)S(1)} %get-tuple-element.42), channel_id=1, source_target_pairs={{16,0},{32,16},{48,32},{64,48},{80,64},{96,80},{112,96},{128,112},... | collective-permute-start | bytes 589832 | tf_op jit(solution)/shard_map/ppermute | solution.py:31
  73.1 5.2 %collective-permute-start.2 = (bf16[128,768]{1,0:T(8,128)(2,1)S(1)}, bf16[128,768]{1,0:T(8,128)(2,1)S(1)}, u32[]{:S(2)}, u32[]{:S(2)}) collective-permute-start(bf16[128,768]{1,0:T(8,128)(2,1)S(1)} %get-tuple-element.41.refs_4_), channel_id=1, source_target_pairs={{0,16},{16,32},{32,48},{48,64},{64,80},{80,96},{96,112},{112,128},... | collective-permute-start | bytes 589832 | tf_op jit(solution)/shard_map/ppermute | solution.py:31
  75.0 3.3 %copy-start.5 = (bf16[128,768]{1,0:T(8,128)(2,1)S(1)}, bf16[128,768]{1,0:T(8,128)(2,1)}, u32[]{:S(2)}) copy-start(bf16[128,768]{1,0:T(8,128)(2,1)} %refs_3_.1) | copy-start | bytes 589828
  75.0 3.3 %copy-start.16 = (bf16[768,512]{1,0:T(8,128)(2,1)S(1)}, bf16[768,512]{1,0:T(8,128)(2,1)}, u32[]{:S(2)}) copy-start(bf16[768,512]{1,0:T(8,128)(2,1)} %copy-done.14) | copy-start | bytes 2359300
  80.1 18.4 %all-to-all-start.2 = ((bf16[16,8,1664]{2,1,0:T(8,128)(2,1)}), bf16[16,8,1664]{2,1,0:T(8,128)(2,1)S(1)}, u32[]{:S(2)}, u32[]{:S(2)}) async-start(bf16[16,8,1664]{2,1,0:T(8,128)(2,1)} %bitcast.10), calls=%async_computation.2 | async-start | bytes 851968 | tf_op jit(solution)/shard_map/all_to_all | solution.py:20
  84.8 19.5 %collective-permute-start.4 = (bf16[128,768]{1,0:T(8,128)(2,1)}, bf16[128,768]{1,0:T(8,128)(2,1)}, u32[]{:S(2)}, u32[]{:S(2)}) collective-permute-start(bf16[128,768]{1,0:T(8,128)(2,1)} %get-tuple-element.44.refs_1_), channel_id=1, source_target_pairs={{0,496},{16,480},{32,464},{48,448},{64,432},{80,416},{96,400},{112... | collective-permute-start | bytes 589832 | tf_op jit(solution)/shard_map/ppermute | solution.py:25
  99.5 4.9 %copy-start.3 = (bf16[1,2,128,768]{3,2,1,0:T(8,128)(2,1)S(1)}, bf16[1,2,128,768]{3,2,1,0:T(8,128)(2,1)}, u32[]{:S(2)}) copy-start(bf16[1,2,128,768]{3,2,1,0:T(8,128)(2,1)} %stash.5) | copy-start | bytes 1179652
  99.5 20.9 %all-to-all-start.3 = ((bf16[16,8,2176]{2,1,0:T(8,128)(2,1)}), bf16[16,8,2176]{2,1,0:T(8,128)(2,1)S(1)}, u32[]{:S(2)}, u32[]{:S(2)}) async-start(bf16[16,8,2176]{2,1,0:T(8,128)(2,1)} %bitcast.12), calls=%async_computation.3 | async-start | bytes 1114112 | tf_op jit(solution)/shard_map/all_to_all | solution.py:20
  104.3 16.1 %copy-start.8 = (bf16[1,128,768]{2,1,0:T(8,128)(2,1)S(1)}, bf16[1,128,768]{2,1,0:T(8,128)(2,1)}, u32[]{:S(2)}) copy-start(bf16[1,128,768]{2,1,0:T(8,128)(2,1)} %param.11) | copy-start | bytes 589828

commit v6 on v5

--- a/solution.py
+++ b/solution.py
@@ -12,6 +12,7 @@
 EPS = 1e-05
 LANES = 128
 LONG = 6
+CHUNKS = 4
 ROOT = math.sqrt(2 / math.pi)
 CUBE = 0.044715
 
@@ -128,12 +129,15 @@
     return started
 
 
-def pick_kernel(fetch, stash, first, second, sems):
+def pick_kernel(fetch, stash, first, second):
     partner = lax.axis_size("section") - 1 - lax.axis_index("section")
-    for one in copies(
-        [(stash.at[0, fetch[0, partner]], first), (stash.at[0, fetch[1, partner]], second)], sems
-    ):
-        one.wait()
+    first[...] = stash[0, fetch[0, partner]]
+    second[...] = stash[0, fetch[1, partner]]
+
+
+def chunks(source, target, count):
+    step = source.shape[0] // count
+    return [(source.at[pl.ds(i * step, step)], target.at[pl.ds(i * step, step)]) for i in range(count)]
 
 
 def start_kernel(tokens, upstream, gain, down, up, other, payload, weight, column_sum, both, *, peers, rank):
@@ -270,28 +274,18 @@
     payload[:, 4 * rank :] = to_all(stats, peers)
 
 
-def stash_kernel(evict, stash, arrived, partner1, stash_out, done, sems):
-    slots = stash.shape[1]
+def stash_kernel(evict, stash, arrived, partner1, stash_out, done):
     partner = lax.axis_size("section") - 1 - lax.axis_index("section")
     early, late = evict[0, partner], evict[1, partner]
-    for i in range(slots):
-        for source, taken in (
-            (partner1, late == i),
-            (arrived.at[1], (late != i) & (early == i)),
-            (stash.at[0, i], (late != i) & (early != i)),
-        ):
-            @pl.when(taken)
-            def _():
-                pltpu.make_async_copy(source, stash_out.at[0, i], sems.at[i]).start()
-
-    for i in range(slots):
-        pltpu.make_async_copy(stash.at[0, i], stash_out.at[0, i], sems.at[i]).wait()
+    for i in range(stash.shape[1]):
+        stash_out[0, i] = jnp.where(late == i, partner1[...], jnp.where(early == i, arrived[1], stash[0, i]))
     done[...] = jnp.zeros_like(done)
 
 
 def last_kernel(
     kept_in, tokens_in, done, got, got0, upstream0, gain_term0, gain, down, up,
-    up_grad_out, out_out, grad_out, gain_grad, down_grad_out, kept, tokens, up_grad, out, grad, down_grad, sems, *, rank
+    up_grad_out, out_out, grad_out, gain_grad, down_grad_out, kept, tokens, up_grad, out, grad, down_grad,
+    sems, up_sems, down_sems, *, rank
 ):
     rows = upstream0.shape[0]
     span = pl.ds(2 * rows, rows)
@@ -313,25 +307,25 @@
     loads[1].wait()
     out[...] = (tokens[...].astype(F32) + product).astype(BF16)
     loads[2].wait()
-    stores = [
-        pltpu.make_async_copy(up_grad, up_grad_out, sems.at[3]),
-        pltpu.make_async_copy(out, out_out, sems.at[4]),
-        pltpu.make_async_copy(down_grad, down_grad_out, sems.at[5]),
-        pltpu.make_async_copy(grad, grad_out, sems.at[6]),
-    ]
-    stores[0].start()
-    stores[1].start()
+    up_stores = copies(chunks(up_grad, up_grad_out, CHUNKS), up_sems)
+    out_store = pltpu.make_async_copy(out, out_out, sems.at[3])
+    out_store.start()
     grad[...], scaled, gain_term = backward(
         kept[:rows], upstream, got[:, rank : 2 * rank], got[:, 4 * rank :].astype(F32), gain[...].astype(F32), down[...]
     )
-    stores[3].start()
+    grad_store = pltpu.make_async_copy(grad, grad_out, sems.at[4])
+    grad_store.start()
     gain_grad[...] = gain_term0[...] + gain_term
-    down_grad[...] = transposed_times(
-        jnp.concatenate([kept[rows : 2 * rows], scaled], axis=0),
-        jnp.concatenate([got0[:, rank : 2 * rank], got[:, rank : 2 * rank]], axis=0),
-    ).astype(BF16)
-    stores[2].start()
-    for one in stores:
+    tokens_both = jnp.concatenate([kept[rows : 2 * rows], scaled], axis=0)
+    hidden_both = jnp.concatenate([got0[:, rank : 2 * rank], got[:, rank : 2 * rank]], axis=0)
+    down_stores = []
+    step = down_grad.shape[0] // 2
+    for i, (part, target) in enumerate(chunks(down_grad, down_grad_out, 2)):
+        part[...] = transposed_times(tokens_both[:, i * step : (i + 1) * step], hidden_both).astype(BF16)
+        for j, (source, place) in enumerate(chunks(part, target, CHUNKS // 2)):
+            down_stores.append(pltpu.make_async_copy(source, place, down_sems.at[i * (CHUNKS // 2) + j]))
+            down_stores[-1].start()
+    for one in up_stores + down_stores + [out_store, grad_store]:
         one.wait()
 
 
@@ -380,8 +374,6 @@
         [shape(rows, features), shape(rows, features)],
         [fetch, held_stash],
         smem=(0,),
-        left=(1,),
-        scratch=[sems((2,))],
         name="pick",
     )
     fetched0 = mirrored(picked)
@@ -462,9 +454,6 @@
         [shape(*held_stash.shape), shape(8, LANES, dtype=F32)],
         [evict, held_stash, both, partner1],
         smem=(0,),
-        left=(1, 2, 3),
-        left_outs=(0,),
-        scratch=[sems((held_stash.shape[1],))],
         cost=LONG,
         name="stash",
     )
@@ -488,7 +477,9 @@
             tile,
             tile,
             pltpu.VMEM((features, rank), BF16),
-            sems((7,)),
+            sems((5,)),
+            sems((CHUNKS,)),
+            sems((CHUNKS,)),
         ],
         name="last",
     )

time: 127 us -> 126 us (level)
  Pallas kernels: 21.5 us -> 15 us
  waiting for transfers between devices: 36.2 us -> 42 us
    pallas_call x11, Pallas kernels: 21.5 us -> 15 us  [call(): pl.pallas_call(body, out_shape=tuple(outs), in_specs=[pl.BlockSpec(memory...]
    all_to_all x4, waiting for transfers between devices: 22.7 us -> 28.5 us  [across(): return lax.all_to_all(block, 'dp', 0, 0, tiled=True)]
  transfers between devices with their start and end apart: 9 -> 9, of which waited for: 7 -> 7; matrix products, arithmetic and copies ran while one was open for 0% -> 0% of each run, Pallas kernels for 11% -> 6%
where the time goes in v6:
time: 126 us; the launch traced here: 124 us
  starting transfers between devices  62.3 us (49%)
  waiting for transfers between devices  42 us (33%)
  Pallas kernels  15 us (12%)
  local copies, waits for them, and re-layouts  3.5 us (3%)
    ppermute x3, starting transfers between devices, mirrored(): lax.ppermute(value, 'section', [(i, sections - 1 - i) for i in range(sect...  32.6 us
    all_to_all x4, waiting for transfers between devices, across(): return lax.all_to_all(block, 'dp', 0, 0, tiled=True)  28.5 us
    all_to_all x4, starting transfers between devices, across(): return lax.all_to_all(block, 'dp', 0, 0, tiled=True)  22.3 us
    pallas_call x11, Pallas kernels, call(): pl.pallas_call(body, out_shape=tuple(outs), in_specs=[pl.BlockSpec(memory...  15 us
    ppermute x3, waiting for transfers between devices, mirrored(): lax.ppermute(value, 'section', [(i, sections - 1 - i) for i in range(sect...  11.3 us
    ppermute x2, starting transfers between devices, shifted(): return lax.ppermute(value, 'section', pairs)  7.44 us
    unnamed x34, local copies, waits for them, and re-layouts  3.5 us
  transfers between devices with their start and end apart: 9, of which 7 were waited for; matrix products, arithmetic and copies ran while one was open for 0% of the time, Pallas kernels for 6%

profile of v6, /device:TPU:1, one launch (start us, length us, event | category | flops | bytes accessed | tf_op | source)
XLA Modules:
  0.0 123.7 jit_solution(14635327466817003219)
XLA Ops:
  0.6 0.7 copy-done.12
  1.3 1.0 copy-done.2
  2.3 0.6 pick.1
  2.9 14.2 %collective-permute-start.1 = (bf16[128,768]{1,0:T(8,128)(2,1)S(1)}, bf16[128,768]{1,0:T(8,128)(2,1)S(1)}, u32[]{:S(2)}, u32[]{:S(2)}) collective-permute-start(bf16[128,768]{1,0:T(8,128)(2,1)S(1)} %get-tuple-element.36), channel_id=1, source_target_pairs={{0,496},{16,480},{32,464},{48,448},{64,432},{80,416},{96,400},{112... | collective-permute-start | bytes 589832 | tf_op jit(solution)/shard_map/ppermute | solution.py:26
  17.2 0.0 copy-start.11
  17.2 0.6 copy-done.11
  17.9 0.8 start.1
  18.7 7.3 %collective-permute-done.1.refs_0_.refs_2_ = bf16[128,768]{1,0:T(8,128)(2,1)S(1)} collective-permute-done((bf16[128,768]{1,0:T(8,128)(2,1)S(1)}, bf16[128,768]{1,0:T(8,128)(2,1)S(1)}, u32[]{:S(2)}, u32[]{:S(2)}) %collective-permute-start.1) | collective-permute-done | bytes 196640 | tf_op jit(solution)/shard_map/ppermute | solution.py:26
  26.1 1.1 fetched.1
  27.1 7.9 %all-to-all-start = ((bf16[16,8,1920]{2,1,0:T(8,128)(2,1)}), bf16[16,8,1920]{2,1,0:T(8,128)(2,1)S(1)}, u32[]{:S(2)}, u32[]{:S(2)}) async-start(bf16[16,8,1920]{2,1,0:T(8,128)(2,1)} %bitcast.6), calls=%async_computation | async-start | bytes 983040 | tf_op jit(solution)/shard_map/all_to_all | solution.py:21
  35.1 7.9 %collective-permute-start = (bf16[2,128,768]{2,1,0:T(8,128)(2,1)S(1)}, bf16[2,128,768]{2,1,0:T(8,128)(2,1)S(1)}, u32[]{:S(2)}, u32[]{:S(2)}) collective-permute-start(bf16[2,128,768]{2,1,0:T(8,128)(2,1)S(1)} %get-tuple-element.32), channel_id=1, source_target_pairs={{0,496},{16,480},{32,464},{48,448},{64,432},{80,416},{96,400},{112... | collective-permute-start | bytes 1179656 | tf_op jit(solution)/shard_map/ppermute | solution.py:26
  43.0 7.5 %all-to-all-done = bf16[16,8,1920]{2,1,0:T(8,128)(2,1)S(1)} async-done(((bf16[16,8,1920]{2,1,0:T(8,128)(2,1)}), bf16[16,8,1920]{2,1,0:T(8,128)(2,1)S(1)}, u32[]{:S(2)}, u32[]{:S(2)}) %all-to-all-start) | async-done | bytes 491552 | tf_op jit(solution)/shard_map/all_to_all | solution.py:21
  50.4 1.1 middle.1
  51.6 4.8 %all-to-all-start.1 = ((bf16[16,8,1152]{2,1,0:T(8,128)(2,1)}), bf16[16,8,1152]{2,1,0:T(8,128)(2,1)S(1)}, u32[]{:S(2)}, u32[]{:S(2)}) async-start(bf16[16,8,1152]{2,1,0:T(8,128)(2,1)} %bitcast.8), calls=%async_computation.1 | async-start | bytes 589824 | tf_op jit(solution)/shard_map/all_to_all | solution.py:21
  56.4 3.9 %collective-permute-done.refs_2_.arrived = bf16[2,128,768]{2,1,0:T(8,128)(2,1)S(1)} collective-permute-done((bf16[2,128,768]{2,1,0:T(8,128)(2,1)S(1)}, bf16[2,128,768]{2,1,0:T(8,128)(2,1)S(1)}, u32[]{:S(2)}, u32[]{:S(2)}) %collective-permute-start) | collective-permute-done | bytes 393248 | tf_op jit(solution)/shard_map/ppermute | solution.py:26
  60.3 1.1 copy-done.15
  61.4 1.4 %other.1 = (bf16[128,640]{1,0:T(8,128)(2,1)S(1)}, bf16[512,768]{1,0:T(8,128)(2,1)}) custom-call(s32[2,32]{1,0:T(2,128)S(1)} %bitcast.40, s32[2,32]{1,0:T(2,128)S(1)} %bitcast.41, bf16[2,128,768]{2,1,0:T(8,128)(2,1)S(1)} %collective-permute-done.refs_2_.arrived, bf16[128,768]{1,0:T(8,128)(2,1)S(1)} %bitcast.33, bf16[768,512]{1,0:T(8,128)(2,1)S(1)} %copy-done.15, ...), custom_call_target="tpu_custom_call" | custom-call | flops 12884901888 | bytes 6291456 | tf_op jit(solution)/shard_map/other/pallas_call | solution.py:335
  62.8 3.7 %all-to-all-done.1 = bf16[16,8,1152]{2,1,0:T(8,128)(2,1)S(1)} async-done(((bf16[16,8,1152]{2,1,0:T(8,128)(2,1)}), bf16[16,8,1152]{2,1,0:T(8,128)(2,1)S(1)}, u32[]{:S(2)}, u32[]{:S(2)}) %all-to-all-start.1) | async-done | bytes 294944 | tf_op jit(solution)/shard_map/all_to_all | solution.py:21
  66.5 0.5 first.1
  67.0 5.5 %collective-permute-start.3 = (bf16[128,768]{1,0:T(8,128)(2,1)S(1)}, bf16[128,768]{1,0:T(8,128)(2,1)S(1)}, u32[]{:S(2)}, u32[]{:S(2)}) collective-permute-start(bf16[128,768]{1,0:T(8,128)(2,1)S(1)} %get-tuple-element.42), channel_id=1, source_target_pairs={{16,0},{32,16},{48,32},{64,48},{80,64},{96,80},{112,96},{128,112},... | collective-permute-start | bytes 589832 | tf_op jit(solution)/shard_map/ppermute | solution.py:32
  72.6 1.9 %collective-permute-start.2 = (bf16[128,768]{1,0:T(8,128)(2,1)S(1)}, bf16[128,768]{1,0:T(8,128)(2,1)S(1)}, u32[]{:S(2)}, u32[]{:S(2)}) collective-permute-start(bf16[128,768]{1,0:T(8,128)(2,1)S(1)} %get-tuple-element.41.refs_4_), channel_id=1, source_target_pairs={{0,16},{16,32},{32,48},{48,64},{64,80},{80,96},{96,112},{112,128},... | collective-permute-start | bytes 589832 | tf_op jit(solution)/shard_map/ppermute | solution.py:32
  74.5 1.0 terms.1
  75.5 2.2 %collective-permute-done.3.refs_2_ = bf16[128,768]{1,0:T(8,128)(2,1)S(1)} collective-permute-done((bf16[128,768]{1,0:T(8,128)(2,1)S(1)}, bf16[128,768]{1,0:T(8,128)(2,1)S(1)}, u32[]{:S(2)}, u32[]{:S(2)}) %collective-permute-start.3) | collective-permute-done | bytes 196640 | tf_op jit(solution)/shard_map/ppermute | solution.py:32
  77.8 1.8 %second.1 = (bf16[128,1664]{1,0:T(8,128)(2,1)}, bf16[512,768]{1,0:T(8,128)(2,1)}, bf16[128,768]{1,0:T(8,128)(2,1)}) custom-call(bf16[512,768]{1,0:T(8,128)(2,1)} %get-tuple-element.39.refs_0_, bf16[128,768]{1,0:T(8,128)(2,1)S(1)} %collective-permute-done.2.refs_1_, ...), custom_call_target="tpu_custom_call", output_to_operand_aliasing={{1}: (0, {})} | custom-call | flops 2147483648 | bytes 1048576 | tf_op jit(solution)/shard_map/second/pallas_call | solution.py:335
  79.6 4.7 %all-to-all-start.2 = ((bf16[16,8,1664]{2,1,0:T(8,128)(2,1)}), bf16[16,8,1664]{2,1,0:T(8,128)(2,1)S(1)}, u32[]{:S(2)}, u32[]{:S(2)}) async-start(bf16[16,8,1664]{2,1,0:T(8,128)(2,1)} %bitcast.10), calls=%async_computation.2 | async-start | bytes 851968 | tf_op jit(solution)/shard_map/all_to_all | solution.py:21
  84.3 10.5 %collective-permute-start.4 = (bf16[128,768]{1,0:T(8,128)(2,1)}, bf16[128,768]{1,0:T(8,128)(2,1)}, u32[]{:S(2)}, u32[]{:S(2)}) collective-permute-start(bf16[128,768]{1,0:T(8,128)(2,1)} %get-tuple-element.44.refs_1_), channel_id=1, source_target_pairs={{0,496},{16,480},{32,464},{48,448},{64,432},{80,416},{96,400},{112... | collective-permute-start | bytes 589832 | tf_op jit(solution)/shard_map/ppermute | solution.py:26
  94.8 3.2 %all-to-all-done.2 = bf16[16,8,1664]{2,1,0:T(8,128)(2,1)S(1)} async-done(((bf16[16,8,1664]{2,1,0:T(8,128)(2,1)}), bf16[16,8,1664]{2,1,0:T(8,128)(2,1)S(1)}, u32[]{:S(2)}, u32[]{:S(2)}) %all-to-all-start.2) | async-done | bytes 426016 | tf_op jit(solution)/shard_map/all_to_all | solution.py:21
  98.0 1.1 late.1
  99.0 4.8 %all-to-all-start.3 = ((bf16[16,8,2176]{2,1,0:T(8,128)(2,1)}), bf16[16,8,2176]{2,1,0:T(8,128)(2,1)S(1)}, u32[]{:S(2)}, u32[]{:S(2)}) async-start(bf16[16,8,2176]{2,1,0:T(8,128)(2,1)} %bitcast.12), calls=%async_computation.3 | async-start | bytes 1114112 | tf_op jit(solution)/shard_map/all_to_all | solution.py:21
  103.9 1.8 %stash.4 = (bf16[1,2,128,768]{3,2,1,0:T(8,128)(2,1)}, f32[8,128]{1,0:T(8,128)S(1)}) custom-call(s32[2,32]{1,0:T(2,128)S(1)} %bitcast.42, bf16[1,2,128,768]{3,2,1,0:T(8,128)(2,1)S(1)} %copy-done.3, bf16[2,128,768]{2,1,0:T(8,128)(2,1)S(1)} %collective-permute-done.refs_2_.arrived, bf16[128,768]{1,0:T(8,128)(2,1)} %collective-permute-done.4.partner1), custom_call_target="tpu_custom_call" | custom-call | flops 12884901888 | bytes 6291456 | tf_op jit(solution)/shard_map/stash/pallas_call | solution.py:335
  105.7 14.2 %all-to-all-done.3 = bf16[16,8,2176]{2,1,0:T(8,128)(2,1)S(1)} async-done(((bf16[16,8,2176]{2,1,0:T(8,128)(2,1)}), bf16[16,8,2176]{2,1,0:T(8,128)(2,1)S(1)}, u32[]{:S(2)}, u32[]{:S(2)}) %all-to-all-start.3) | async-done | bytes 557088 | tf_op jit(solution)/shard_map/all_to_all | solution.py:21
  119.9 3.8 %last.1 = (bf16[512,768]{1,0:T(8,128)(2,1)}, bf16[128,768]{1,0:T(8,128)(2,1)}, bf16[128,768]{1,0:T(8,128)(2,1)}, f32[1,768]{1,0:T(1,128)}, bf16[768,512]{1,0:T(8,128)(2,1)}) custom-call(bf16[512,768]{1,0:T(8,128)(2,1)} %get-tuple-element.43.refs_0_, bf16[128,768]{1,0:T(8,128)(2,1)} %get-tuple-element.44.refs_1_, ...), custom_call_target="tpu_custom_call", output_to_operand_aliasing={{0}: (0, {}), {1}: (1, {})} | custom-call | flops 2147483648 | bytes 1048576 | tf_op jit(solution)/shard_map/last/pallas_call | solution.py:335
  (31 shorter events, 0.1 us)
Async XLA Ops:
  0.6 0.7 copy-start.12
  1.3 1.0 copy-start.2
  2.3 14.9 %copy-start = (bf16[1,768,512]{2,1,0:T(8,128)(2,1)S(1)}, bf16[1,768,512]{2,1,0:T(8,128)(2,1)}, u32[]{:S(2)}) copy-start(bf16[1,768,512]{2,1,0:T(8,128)(2,1)} %param.14) | copy-start | bytes 2359300
  2.3 14.9 %copy-start.1 = (bf16[1,512,768]{2,1,0:T(8,128)(2,1)S(1)}, bf16[1,512,768]{2,1,0:T(8,128)(2,1)}, u32[]{:S(2)}) copy-start(bf16[1,512,768]{2,1,0:T(8,128)(2,1)} %param.15) | copy-start | bytes 2359300
  2.3 14.9 %copy-start.4 = (bf16[1,128,768]{2,1,0:T(8,128)(2,1)S(1)}, bf16[1,128,768]{2,1,0:T(8,128)(2,1)}, u32[]{:S(2)}) copy-start(bf16[1,128,768]{2,1,0:T(8,128)(2,1)} %param.9) | copy-start | bytes 589828
  2.3 14.9 %copy-start.6 = (bf16[1,128,768]{2,1,0:T(8,128)(2,1)S(1)}, bf16[1,128,768]{2,1,0:T(8,128)(2,1)}, u32[]{:S(2)}) copy-start(bf16[1,128,768]{2,1,0:T(8,128)(2,1)} %param.11) | copy-start | bytes 589828
  2.9 23.1 %collective-permute-start.1 = (bf16[128,768]{1,0:T(8,128)(2,1)S(1)}, bf16[128,768]{1,0:T(8,128)(2,1)S(1)}, u32[]{:S(2)}, u32[]{:S(2)}) collective-permute-start(bf16[128,768]{1,0:T(8,128)(2,1)S(1)} %get-tuple-element.36), channel_id=1, source_target_pairs={{0,496},{16,480},{32,464},{48,448},{64,432},{80,416},{96,400},{112... | collective-permute-start | bytes 589832 | tf_op jit(solution)/shard_map/ppermute | solution.py:26
  17.2 0.7 copy-start.11
  18.7 8.4 %copy-start.14 = (bf16[768,512]{1,0:T(8,128)(2,1)}, bf16[768,512]{1,0:T(8,128)(2,1)S(1)}, u32[]{:S(2)}) copy-start(bf16[768,512]{1,0:T(8,128)(2,1)S(1)} %get-tuple-element.33.refs_4_.refs_1_.refs_5_) | copy-start | bytes 2359300
  26.1 1.1 copy-start.9
  27.1 23.3 %all-to-all-start = ((bf16[16,8,1920]{2,1,0:T(8,128)(2,1)}), bf16[16,8,1920]{2,1,0:T(8,128)(2,1)S(1)}, u32[]{:S(2)}, u32[]{:S(2)}) async-start(bf16[16,8,1920]{2,1,0:T(8,128)(2,1)} %bitcast.6), calls=%async_computation | async-start | bytes 983040 | tf_op jit(solution)/shard_map/all_to_all | solution.py:21
  35.1 25.2 %collective-permute-start = (bf16[2,128,768]{2,1,0:T(8,128)(2,1)S(1)}, bf16[2,128,768]{2,1,0:T(8,128)(2,1)S(1)}, u32[]{:S(2)}, u32[]{:S(2)}) collective-permute-start(bf16[2,128,768]{2,1,0:T(8,128)(2,1)S(1)} %get-tuple-element.32), channel_id=1, source_target_pairs={{0,496},{16,480},{32,464},{48,448},{64,432},{80,416},{96,400},{112... | collective-permute-start | bytes 1179656 | tf_op jit(solution)/shard_map/ppermute | solution.py:26
  51.6 14.9 %all-to-all-start.1 = ((bf16[16,8,1152]{2,1,0:T(8,128)(2,1)}), bf16[16,8,1152]{2,1,0:T(8,128)(2,1)S(1)}, u32[]{:S(2)}, u32[]{:S(2)}) async-start(bf16[16,8,1152]{2,1,0:T(8,128)(2,1)} %bitcast.8), calls=%async_computation.1 | async-start | bytes 589824 | tf_op jit(solution)/shard_map/all_to_all | solution.py:21
  56.3 3.9 %copy-start.13 = (s32[32,2]{0,1:T(2,128)S(1)}, s32[32,2]{0,1:T(2,128)}, u32[]{:S(2)}) copy-start(s32[32,2]{0,1:T(2,128)} %param.17) | copy-start | bytes 772
  60.3 1.1 copy-start.15
  61.4 5.1 %copy-start.7 = (bf16[1,128,768]{2,1,0:T(8,128)(2,1)S(1)}, bf16[1,128,768]{2,1,0:T(8,128)(2,1)}, u32[]{:S(2)}) copy-start(bf16[1,128,768]{2,1,0:T(8,128)(2,1)} %param.11) | copy-start | bytes 589828
  61.4 5.1 %copy-start.10 = (bf16[128,768]{1,0:T(8,128)(2,1)S(1)}, bf16[128,768]{1,0:T(8,128)(2,1)}, u32[]{:S(2)}) copy-start(bf16[128,768]{1,0:T(8,128)(2,1)} %copy-done.9) | copy-start | bytes 589828
  67.0 10.7 %collective-permute-start.3 = (bf16[128,768]{1,0:T(8,128)(2,1)S(1)}, bf16[128,768]{1,0:T(8,128)(2,1)S(1)}, u32[]{:S(2)}, u32[]{:S(2)}) collective-permute-start(bf16[128,768]{1,0:T(8,128)(2,1)S(1)} %get-tuple-element.42), channel_id=1, source_target_pairs={{16,0},{32,16},{48,32},{64,48},{80,64},{96,80},{112,96},{128,112},... | collective-permute-start | bytes 589832 | tf_op jit(solution)/shard_map/ppermute | solution.py:32
  72.6 5.2 %collective-permute-start.2 = (bf16[128,768]{1,0:T(8,128)(2,1)S(1)}, bf16[128,768]{1,0:T(8,128)(2,1)S(1)}, u32[]{:S(2)}, u32[]{:S(2)}) collective-permute-start(bf16[128,768]{1,0:T(8,128)(2,1)S(1)} %get-tuple-element.41.refs_4_), channel_id=1, source_target_pairs={{0,16},{16,32},{32,48},{48,64},{64,80},{80,96},{96,112},{112,128},... | collective-permute-start | bytes 589832 | tf_op jit(solution)/shard_map/ppermute | solution.py:32
  74.5 3.3 %copy-start.5 = (bf16[128,768]{1,0:T(8,128)(2,1)S(1)}, bf16[128,768]{1,0:T(8,128)(2,1)}, u32[]{:S(2)}) copy-start(bf16[128,768]{1,0:T(8,128)(2,1)} %refs_3_.1) | copy-start | bytes 589828
  74.5 3.3 %copy-start.16 = (bf16[768,512]{1,0:T(8,128)(2,1)S(1)}, bf16[768,512]{1,0:T(8,128)(2,1)}, u32[]{:S(2)}) copy-start(bf16[768,512]{1,0:T(8,128)(2,1)} %copy-done.14) | copy-start | bytes 2359300
  79.6 18.4 %all-to-all-start.2 = ((bf16[16,8,1664]{2,1,0:T(8,128)(2,1)}), bf16[16,8,1664]{2,1,0:T(8,128)(2,1)S(1)}, u32[]{:S(2)}, u32[]{:S(2)}) async-start(bf16[16,8,1664]{2,1,0:T(8,128)(2,1)} %bitcast.10), calls=%async_computation.2 | async-start | bytes 851968 | tf_op jit(solution)/shard_map/all_to_all | solution.py:21
  84.3 19.6 %collective-permute-start.4 = (bf16[128,768]{1,0:T(8,128)(2,1)}, bf16[128,768]{1,0:T(8,128)(2,1)}, u32[]{:S(2)}, u32[]{:S(2)}) collective-permute-start(bf16[128,768]{1,0:T(8,128)(2,1)} %get-tuple-element.44.refs_1_), channel_id=1, source_target_pairs={{0,496},{16,480},{32,464},{48,448},{64,432},{80,416},{96,400},{112... | collective-permute-start | bytes 589832 | tf_op jit(solution)/shard_map/ppermute | solution.py:26
  99.0 4.8 %copy-start.3 = (bf16[1,2,128,768]{3,2,1,0:T(8,128)(2,1)S(1)}, bf16[1,2,128,768]{3,2,1,0:T(8,128)(2,1)}, u32[]{:S(2)}) copy-start(bf16[1,2,128,768]{3,2,1,0:T(8,128)(2,1)} %stash.5) | copy-start | bytes 1179652
  99.0 20.9 %all-to-all-start.3 = ((bf16[16,8,2176]{2,1,0:T(8,128)(2,1)}), bf16[16,8,2176]{2,1,0:T(8,128)(2,1)S(1)}, u32[]{:S(2)}, u32[]{:S(2)}) async-start(bf16[16,8,2176]{2,1,0:T(8,128)(2,1)} %bitcast.12), calls=%async_computation.3 | async-start | bytes 1114112 | tf_op jit(solution)/shard_map/all_to_all | solution.py:21
  103.8 16.1 %copy-start.8 = (bf16[1,128,768]{2,1,0:T(8,128)(2,1)S(1)}, bf16[1,128,768]{2,1,0:T(8,128)(2,1)}, u32[]{:S(2)}) copy-start(bf16[1,128,768]{2,1,0:T(8,128)(2,1)} %param.11) | copy-start | bytes 589828

commit v7 on v6

--- a/solution.py
+++ b/solution.py
@@ -140,12 +140,17 @@
     return [(source.at[pl.ds(i * step, step)], target.at[pl.ds(i * step, step)]) for i in range(count)]
 
 
+def scaled_weight(gain, down):
+    features, rank = down.shape
+    tall = jnp.broadcast_to(gain[...].astype(F32), (LANES, features)).T
+    return down[...].astype(F32) * jnp.concatenate([tall] * (rank // LANES), axis=1)
+
+
 def start_kernel(tokens, upstream, gain, down, up, other, payload, weight, column_sum, both, *, peers, rank):
     both[0] = other[...]
     both[1] = tokens[...]
-    rows, features = tokens.shape
-    tall = jnp.broadcast_to(gain[...].astype(F32), (LANES, features)).T
-    exact = down[...].astype(F32) * jnp.concatenate([tall] * (rank // LANES), axis=1)
+    rows = tokens.shape[0]
+    exact = scaled_weight(gain, down)
     rounded = exact.astype(BF16)
     weight[...] = rounded
     one = jnp.sum(rounded.astype(F32), axis=0, keepdims=True)
@@ -214,31 +219,33 @@
     )[0]
 
 
-def other_kernel(
-    fetch, evict, arrived, tokens, weight, column_sum, payload, kept, chosen, sems, *, rank
-):
+def other_kernel(fetch, evict, arrived, tokens, weight, column_sum, part, sums, kept, chosen, sems):
     place = lax.axis_index("section")
     chosen[...] = jnp.where(fetch[1, place] == evict[0, place], tokens[...], arrived[0])
     (saved,) = copies([(chosen, kept.at[pl.ds(0, tokens.shape[0])])], sems)
-    part, sums = hidden_part(chosen[...], weight[...], column_sum[...])
-    payload[:, :rank] = part.astype(BF16)
-    payload[:, rank:] = in_lanes([0.0] * 6 + sums).astype(BF16)
+    part[...], columns = hidden_part(chosen[...], weight[...], column_sum[...])
+    sums[...] = in_lanes(columns)
     saved.wait()
 
 
 def terms_kernel(
-    kept_in, got, fetched, upstream, gain, down, kept, gain_term, scaled, sems, *, rank
+    kept_in, got, fetched, upstream, gain, down, part, sums, active_back, after, payload, kept, gain_term, scaled, sems,
+    *, peers, rank
 ):
     scaled[...], gain_term[...] = backward(
         fetched[...], upstream[...], got[:, rank : 2 * rank], got[:, 2 * rank :].astype(F32), gain[...].astype(F32), down[...]
     )[1:]
     rows = scaled.shape[0]
-    (saved,) = copies([(scaled, kept.at[pl.ds(rows, rows)])], sems)
-    saved.wait()
+    saved = copies([(scaled, kept.at[pl.ds(rows, rows)]), (upstream, kept.at[pl.ds(3 * rows, rows)])], sems)
+    payload[:, :rank] = part[...].astype(BF16)
+    payload[:, rank : 2 * rank] = to_all(active_back[...], peers)
+    payload[:, 2 * rank :] = sums[...].astype(BF16)
+    for one in saved:
+        one.wait()
 
 
 def second_kernel(
-    kept_in, before, after, fresh, own, weight, column_sum, up, side, payload, kept, tokens_out, tokens, upstream, sems,
+    kept_in, before, after, fresh, own, gain, down, column_sum, up, prior, payload, kept, tokens_out, tokens, upstream, sems,
     *, rank
 ):
     place = lax.axis_index("section")
@@ -249,29 +256,26 @@
     upstream[...] = jnp.where(place == lax.axis_size("section") - 1, own[...], after[...])
     second = pltpu.make_async_copy(upstream, kept.at[pl.ds(2 * rows, rows)], sems.at[1])
     second.start()
-    part, sums = hidden_part(tokens[...], weight[...], column_sum[...])
+    payload[:, rank : 2 * rank] = times_transposed(upstream[...], up[...]).astype(BF16)
+    part, sums = hidden_part(tokens[...], scaled_weight(gain, down).astype(BF16), column_sum[...])
     payload[:, :rank] = part.astype(BF16)
-    payload[:, rank : 2 * rank] = times_transposed(upstream[...], up[...]).astype(BF16)
-    payload[:, 2 * rank : 3 * rank] = side[:, :rank]
-    payload[:, 3 * rank :] = (side[:, rank:].astype(F32) + in_lanes(sums)).astype(BF16)
+    payload[:, 2 * rank :] = in_lanes(sums).astype(BF16)
     first.wait()
     second.wait()
 
 
-def late_kernel(got, columns, active_back, payload, *, peers, rank, width):
+def late_kernel(got, side, columns, payload, *, peers, rank, width):
     column_sums = [columns[peer : peer + 1, :] for peer in range(peers)]
-    sums = got[:, 3 * rank :].astype(F32)
-    hidden_f = finish_hidden(got[:, :rank], sums, 0, column_sums, width)[0]
+    hidden_f = finish_hidden(got[:, :rank], got[:, 2 * rank :].astype(F32), 0, column_sums, width)[0]
     slope = summed(got[:, rank : 2 * rank], peers)
-    hidden, mean, inverse = finish_hidden(got[:, 2 * rank : 3 * rank], sums, 6, column_sums, width)
+    hidden, mean, inverse = finish_hidden(side[:, :rank], side[:, 2 * rank :].astype(F32), 0, column_sums, width)
     active, bent = gelu_and_slope(hidden)
     grad_hidden = (slope * bent).astype(BF16)
     payload[:, :rank] = to_all(gelu(hidden_f), peers)
     payload[:, rank : 2 * rank] = to_all(grad_hidden.astype(F32), peers)
     payload[:, 2 * rank : 3 * rank] = to_all(active, peers)
-    payload[:, 3 * rank : 4 * rank] = to_all(active_back[...], peers)
     stats = back_stats(grad_hidden, hidden, mean, inverse, columns[peers : peers + 1, :], width)
-    payload[:, 4 * rank :] = to_all(stats, peers)
+    payload[:, 3 * rank :] = to_all(stats, peers)
 
 
 def stash_kernel(evict, stash, arrived, partner1, stash_out, done):
@@ -283,12 +287,12 @@
 
 
 def last_kernel(
-    kept_in, tokens_in, done, got, got0, upstream0, gain_term0, gain, down, up,
+    kept_in, tokens_in, done, got, side, got0, gain_term0, gain, down, up,
     up_grad_out, out_out, grad_out, gain_grad, down_grad_out, kept, tokens, up_grad, out, grad, down_grad,
     sems, up_sems, down_sems, *, rank
 ):
-    rows = upstream0.shape[0]
-    span = pl.ds(2 * rows, rows)
+    rows = tokens.shape[0]
+    span = pl.ds(2 * rows, 2 * rows)
     loads = copies(
         [
             (kept_in.at[span], kept.at[span]),
@@ -300,9 +304,10 @@
     product = jnp.dot(got[:, :rank], up[...], preferred_element_type=F32)
     loads[0].wait()
     upstream = kept[2 * rows : 3 * rows]
+    upstream0 = kept[3 * rows :]
     up_grad[...] = transposed_times(
-        jnp.concatenate([got[:, 3 * rank : 4 * rank], got[:, 2 * rank : 3 * rank]], axis=0),
-        jnp.concatenate([upstream0[...], upstream], axis=0),
+        jnp.concatenate([side[:, rank : 2 * rank], got[:, 2 * rank : 3 * rank]], axis=0),
+        jnp.concatenate([upstream0, upstream], axis=0),
     ).astype(BF16)
     loads[1].wait()
     out[...] = (tokens[...].astype(F32) + product).astype(BF16)
@@ -311,7 +316,7 @@
     out_store = pltpu.make_async_copy(out, out_out, sems.at[3])
     out_store.start()
     grad[...], scaled, gain_term = backward(
-        kept[:rows], upstream, got[:, rank : 2 * rank], got[:, 4 * rank :].astype(F32), gain[...].astype(F32), down[...]
+        kept[:rows], upstream, got[:, rank : 2 * rank], got[:, 3 * rank :].astype(F32), gain[...].astype(F32), down[...]
     )
     grad_store = pltpu.make_async_copy(grad, grad_out, sems.at[4])
     grad_store.start()
@@ -400,12 +405,12 @@
         name="middle",
     )
     got0 = across(payload)
-    other, kept = call(
-        bound(other_kernel, rank=rank),
-        [shape(rows, rank + LANES), shape(rank, features)],
+    part1, sums1, kept = call(
+        other_kernel,
+        [shape(rows, rank, dtype=F32), shape(rows, LANES, dtype=F32), shape(rank, features)],
         [fetch, evict, both, tokens0, weight, column_sum],
         smem=(0, 1),
-        left_outs=(1,),
+        left_outs=(2,),
         scratch=[tile, sems((1,))],
         cost=LONG,
         name="other",
@@ -413,39 +418,41 @@
     first_out, first_grad = call(
         bound(first_kernel, rank=rank),
         [shape(rows, features)] * 2,
-        [got0, tokens0, fetched0, grad0, norm_gain, down, up, other],
+        [got0, tokens0, fetched0, grad0, norm_gain, down, up, sums1],
         left=(7,),
         name="first",
     )
     before_out = shifted(first_out, 1)
     after_grad = shifted(first_grad, -1)
-    kept, gain_term0 = call(
-        bound(terms_kernel, rank=rank),
-        [shape(rank, features), shape(1, features, dtype=F32)],
-        [kept, got0, fetched0, grad0, norm_gain, down],
-        left=(0,),
-        left_outs=(0,),
-        aliases=[(0, 0)],
-        scratch=[tile, sems((1,))],
+    payload, kept, gain_term0 = call(
+        bound(terms_kernel, peers=peers, rank=rank),
+        [shape(rows, 2 * rank + LANES), shape(rank, features), shape(1, features, dtype=F32)],
+        [kept, got0, fetched0, grad0, norm_gain, down, part1, sums1, active_back, first_grad],
+        left=(0, 9),
+        left_outs=(1,),
+        aliases=[(0, 1)],
+        scratch=[tile, sems((2,))],
         cost=LONG,
         name="terms",
     )
+    side = across(payload)
     payload, kept, tokens1 = call(
         bound(second_kernel, rank=rank),
-        [shape(rows, 3 * rank + LANES), shape(rank, features), shape(rows, features)],
-        [kept, before_out, after_grad, fresh_input, first_out, weight, column_sum, up, other],
-        left=(0,),
+        [shape(rows, 2 * rank + LANES), shape(rank, features), shape(rows, features)],
+        [kept, before_out, after_grad, fresh_input, first_out, norm_gain, down, column_sum, up, gain_term0],
+        left=(0, 9),
         left_outs=(1, 2),
         aliases=[(0, 1)],
         scratch=[tile, tile, sems((2,))],
+        cost=2,
         name="second",
     )
     got = across(payload)
     partner1 = mirrored(tokens1)
     (payload,) = call(
         bound(late_kernel, peers=peers, rank=rank, width=width),
-        [shape(rows, 4 * rank + LANES)],
-        [got, columns, active_back],
+        [shape(rows, 3 * rank + LANES)],
+        [got, side, columns],
         name="late",
     )
     got1 = across(payload)
@@ -466,12 +473,12 @@
             shape(1, features, dtype=F32),
             shape(features, rank),
         ],
-        [kept, tokens1, done, got1, got0, grad0, gain_term0, norm_gain, down, up],
+        [kept, tokens1, done, got1, side, got0, gain_term0, norm_gain, down, up],
         left=(0, 1, 2),
         left_outs=(0, 1, 2, 4),
         aliases=[(0, 0), (1, 1)],
         scratch=[
-            pltpu.VMEM((3 * rows, features), BF16),
+            pltpu.VMEM((4 * rows, features), BF16),
             tile,
             pltpu.VMEM((rank, features), BF16),
             tile,

time: 126 us -> 134 us (1.063)
  waiting for transfers between devices: 42 us -> 48.2 us
  Pallas kernels: 15 us -> 17.5 us
    all_to_all x4 -> x5, waiting for transfers between devices: 28.5 us -> 36.9 us  [across(): return lax.all_to_all(block, 'dp', 0, 0, tiled=True)]
    ppermute x3, starting transfers between devices: 32.6 us -> 28.1 us  [mirrored(): lax.ppermute(value, 'section', [(i, sections - 1 - i) for i in range(sect...]
    all_to_all x4 -> x5, starting transfers between devices: 22.3 us -> 25.9 us  [across(): return lax.all_to_all(block, 'dp', 0, 0, tiled=True)]
    pallas_call x11, Pallas kernels: 15 us -> 17.5 us  [call(): pl.pallas_call(body, out_shape=tuple(outs), in_specs=[pl.BlockSpec(memory...]
    ppermute x2, waiting for transfers between devices: 2.24 us -> 0.01 us  [shifted(): return lax.ppermute(value, 'section', pairs)]
  transfers between devices with their start and end apart: 9 -> 10, of which waited for: 7 -> 7; matrix products, arithmetic and copies ran while one was open for 0% -> 0% of each run, Pallas kernels for 6% -> 8%
where the time goes in v7:
time: 134 us; the launch traced here: 132 us
  starting transfers between devices  61.4 us (46%)
  waiting for transfers between devices  48.2 us (36%)
  Pallas kernels  17.5 us (13%)
  local copies, waits for them, and re-layouts  4.19 us (3%)
    all_to_all x5, waiting for transfers between devices, across(): return lax.all_to_all(block, 'dp', 0, 0, tiled=True)  36.9 us
    ppermute x3, starting transfers between devices, mirrored(): lax.ppermute(value, 'section', [(i, sections - 1 - i) for i in range(sect...  28.1 us
    all_to_all x5, starting transfers between devices, across(): return lax.all_to_all(block, 'dp', 0, 0, tiled=True)  25.9 us
    pallas_call x11, Pallas kernels, call(): pl.pallas_call(body, out_shape=tuple(outs), in_specs=[pl.BlockSpec(memory...  17.5 us
    ppermute x3, waiting for transfers between devices, mirrored(): lax.ppermute(value, 'section', [(i, sections - 1 - i) for i in range(sect...  11.3 us
    ppermute x2, starting transfers between devices, shifted(): return lax.ppermute(value, 'section', pairs)  7.43 us
    unnamed x34, local copies, waits for them, and re-layouts  4.19 us
  transfers between devices with their start and end apart: 10, of which 7 were waited for; matrix products, arithmetic and copies ran while one was open for 0% of the time, Pallas kernels for 8%

profile of v7, /device:TPU:1, one launch (start us, length us, event | category | flops | bytes accessed | tf_op | source)
XLA Modules:
  0.0 132.2 jit_solution(6923099028913502461)
XLA Ops:
  0.6 0.7 copy-done.11
  1.3 1.0 copy-done.2
  2.9 14.2 %collective-permute-start.1 = (bf16[128,768]{1,0:T(8,128)(2,1)S(1)}, bf16[128,768]{1,0:T(8,128)(2,1)S(1)}, u32[]{:S(2)}, u32[]{:S(2)}) collective-permute-start(bf16[128,768]{1,0:T(8,128)(2,1)S(1)} %get-tuple-element.38), channel_id=1, source_target_pairs={{0,496},{16,480},{32,464},{48,448},{64,432},{80,416},{96,400},{112... | collective-permute-start | bytes 589832 | tf_op jit(solution)/shard_map/ppermute | solution.py:26
  17.2 0.6 copy-done.10
  17.9 0.8 start.1
  18.7 7.4 %collective-permute-done.1.refs_0_.refs_2_ = bf16[128,768]{1,0:T(8,128)(2,1)S(1)} collective-permute-done((bf16[128,768]{1,0:T(8,128)(2,1)S(1)}, bf16[128,768]{1,0:T(8,128)(2,1)S(1)}, u32[]{:S(2)}, u32[]{:S(2)}) %collective-permute-start.1) | collective-permute-done | bytes 196640 | tf_op jit(solution)/shard_map/ppermute | solution.py:26
  26.1 1.1 fetched.1
  27.1 7.9 %all-to-all-start = ((bf16[16,8,1920]{2,1,0:T(8,128)(2,1)}), bf16[16,8,1920]{2,1,0:T(8,128)(2,1)S(1)}, u32[]{:S(2)}, u32[]{:S(2)}) async-start(bf16[16,8,1920]{2,1,0:T(8,128)(2,1)} %bitcast.6), calls=%async_computation | async-start | bytes 983040 | tf_op jit(solution)/shard_map/all_to_all | solution.py:21
  35.1 7.9 %collective-permute-start = (bf16[2,128,768]{2,1,0:T(8,128)(2,1)S(1)}, bf16[2,128,768]{2,1,0:T(8,128)(2,1)S(1)}, u32[]{:S(2)}, u32[]{:S(2)}) collective-permute-start(bf16[2,128,768]{2,1,0:T(8,128)(2,1)S(1)} %get-tuple-element.34), channel_id=1, source_target_pairs={{0,496},{16,480},{32,464},{48,448},{64,432},{80,416},{96,400},{112... | collective-permute-start | bytes 1179656 | tf_op jit(solution)/shard_map/ppermute | solution.py:26
  43.0 7.5 %all-to-all-done = bf16[16,8,1920]{2,1,0:T(8,128)(2,1)S(1)} async-done(((bf16[16,8,1920]{2,1,0:T(8,128)(2,1)}), bf16[16,8,1920]{2,1,0:T(8,128)(2,1)S(1)}, u32[]{:S(2)}, u32[]{:S(2)}) %all-to-all-start) | async-done | bytes 491552 | tf_op jit(solution)/shard_map/all_to_all | solution.py:21
  50.4 1.1 middle.1
  51.6 4.8 %all-to-all-start.1 = ((bf16[16,8,1152]{2,1,0:T(8,128)(2,1)}), bf16[16,8,1152]{2,1,0:T(8,128)(2,1)S(1)}, u32[]{:S(2)}, u32[]{:S(2)}) async-start(bf16[16,8,1152]{2,1,0:T(8,128)(2,1)} %bitcast.8), calls=%async_computation.1 | async-start | bytes 589824 | tf_op jit(solution)/shard_map/all_to_all | solution.py:21
  56.4 3.9 %collective-permute-done.arrived = bf16[2,128,768]{2,1,0:T(8,128)(2,1)S(1)} collective-permute-done((bf16[2,128,768]{2,1,0:T(8,128)(2,1)S(1)}, bf16[2,128,768]{2,1,0:T(8,128)(2,1)S(1)}, u32[]{:S(2)}, u32[]{:S(2)}) %collective-permute-start) | collective-permute-done | bytes 393248 | tf_op jit(solution)/shard_map/ppermute | solution.py:26
  60.3 1.1 copy-done.14
  61.4 1.4 %other.1 = (f32[128,512]{1,0:T(8,128)S(1)}, f32[128,128]{1,0:T(8,128)S(1)}, bf16[512,768]{1,0:T(8,128)(2,1)}) custom-call(s32[2,32]{1,0:T(2,128)S(1)} %bitcast.44, s32[2,32]{1,0:T(2,128)S(1)} %bitcast.45, bf16[2,128,768]{2,1,0:T(8,128)(2,1)S(1)} %collective-permute-done.arrived, bf16[128,768]{1,0:T(8,128)(2,1)S(1)} %bitcast.38, ...), custom_call_target="tpu_custom_call" | custom-call | flops 12884901888 | bytes 6291456 | tf_op jit(solution)/shard_map/other/pallas_call | solution.py:340
  62.8 0.7 copy-done.15
  63.5 3.0 %all-to-all-done.1 = bf16[16,8,1152]{2,1,0:T(8,128)(2,1)S(1)} async-done(((bf16[16,8,1152]{2,1,0:T(8,128)(2,1)}), bf16[16,8,1152]{2,1,0:T(8,128)(2,1)S(1)}, u32[]{:S(2)}, u32[]{:S(2)}) %all-to-all-start.1) | async-done | bytes 294944 | tf_op jit(solution)/shard_map/all_to_all | solution.py:21
  66.5 1.2 first.1
  67.7 5.5 %collective-permute-start.3 = (bf16[128,768]{1,0:T(8,128)(2,1)}, bf16[128,768]{1,0:T(8,128)(2,1)S(1)}, u32[]{:S(2)}, u32[]{:S(2)}) collective-permute-start(bf16[128,768]{1,0:T(8,128)(2,1)} %get-tuple-element.44.refs_9_), channel_id=1, source_target_pairs={{16,0},{32,16},{48,32},{64,48},{80,64},{96,80},{112,96},{128,112},... | collective-permute-start | bytes 589832 | tf_op jit(solution)/shard_map/ppermute | solution.py:32
  73.2 1.9 %collective-permute-start.2 = (bf16[128,768]{1,0:T(8,128)(2,1)S(1)}, bf16[128,768]{1,0:T(8,128)(2,1)}, u32[]{:S(2)}, u32[]{:S(2)}) collective-permute-start(bf16[128,768]{1,0:T(8,128)(2,1)S(1)} %get-tuple-element.46.refs_4_), channel_id=1, source_target_pairs={{0,16},{16,32},{32,48},{48,64},{64,80},{80,96},{96,112},{112,128},... | collective-permute-start | bytes 589832 | tf_op jit(solution)/shard_map/ppermute | solution.py:32
  75.2 1.8 %terms.1 = (bf16[128,1152]{1,0:T(8,128)(2,1)}, bf16[512,768]{1,0:T(8,128)(2,1)}, f32[1,768]{1,0:T(1,128)S(1)}) custom-call(bf16[512,768]{1,0:T(8,128)(2,1)} %get-tuple-element.37.refs_0_, bf16[128,1152]{1,0:T(8,128)(2,1)S(1)} %bitcast.23, bf16[128,768]{1,0:T(8,128)(2,1)S(1)} %copy-done.9, ...), custom_call_target="tpu_custom_call", output_to_operand_aliasing={{1}: (0, {})} | custom-call | flops 12884901888 | bytes 6291456 | tf_op jit(solution)/shard_map/terms/pallas_call | solution.py:340
  77.0 6.0 %all-to-all-start.3 = ((bf16[16,8,1152]{2,1,0:T(8,128)(2,1)}), bf16[16,8,1152]{2,1,0:T(8,128)(2,1)S(1)}, u32[]{:S(2)}, u32[]{:S(2)}) async-start(bf16[16,8,1152]{2,1,0:T(8,128)(2,1)} %bitcast.12), calls=%async_computation.3 | async-start | bytes 589824 | tf_op jit(solution)/shard_map/all_to_all | solution.py:21
  83.0 2.8 %second.1 = (bf16[128,1152]{1,0:T(8,128)(2,1)}, bf16[512,768]{1,0:T(8,128)(2,1)}, bf16[128,768]{1,0:T(8,128)(2,1)}) custom-call(bf16[512,768]{1,0:T(8,128)(2,1)} %get-tuple-element.45.refs_0_, bf16[128,768]{1,0:T(8,128)(2,1)} %collective-permute-done.2.refs_1_, bf16[128,768]{1,0:T(8,128)(2,1)S(1)} %collective-permute-done.3.refs_2_, ...), custom_call_target="tpu_custom_call", output_to_operand_aliasing={{1}: (0, {})} | custom-call | flops 4294967296 | bytes 2097152 | tf_op jit(solution)/shard_map/second/pallas_call | solution.py:340
  85.8 9.8 %all-to-all-done.3 = bf16[16,8,1152]{2,1,0:T(8,128)(2,1)S(1)} async-done(((bf16[16,8,1152]{2,1,0:T(8,128)(2,1)}), bf16[16,8,1152]{2,1,0:T(8,128)(2,1)S(1)}, u32[]{:S(2)}, u32[]{:S(2)}) %all-to-all-start.3) | async-done | bytes 294944 | tf_op jit(solution)/shard_map/all_to_all | solution.py:21
  95.6 3.5 %all-to-all-start.2 = ((bf16[16,8,1152]{2,1,0:T(8,128)(2,1)}), bf16[16,8,1152]{2,1,0:T(8,128)(2,1)S(1)}, u32[]{:S(2)}, u32[]{:S(2)}) async-start(bf16[16,8,1152]{2,1,0:T(8,128)(2,1)} %bitcast.10), calls=%async_computation.2 | async-start | bytes 589824 | tf_op jit(solution)/shard_map/all_to_all | solution.py:21
  99.2 5.9 %collective-permute-start.4 = (bf16[128,768]{1,0:T(8,128)(2,1)}, bf16[128,768]{1,0:T(8,128)(2,1)}, u32[]{:S(2)}, u32[]{:S(2)}) collective-permute-start(bf16[128,768]{1,0:T(8,128)(2,1)} %get-tuple-element.49.refs_1_), channel_id=1, source_target_pairs={{0,496},{16,480},{32,464},{48,448},{64,432},{80,416},{96,400},{112... | collective-permute-start | bytes 589832 | tf_op jit(solution)/shard_map/ppermute | solution.py:26
  105.1 6.0 %all-to-all-done.2 = bf16[16,8,1152]{2,1,0:T(8,128)(2,1)S(1)} async-done(((bf16[16,8,1152]{2,1,0:T(8,128)(2,1)}), bf16[16,8,1152]{2,1,0:T(8,128)(2,1)S(1)}, u32[]{:S(2)}, u32[]{:S(2)}) %all-to-all-start.2) | async-done | bytes 294944 | tf_op jit(solution)/shard_map/all_to_all | solution.py:21
  111.1 1.0 late.1
  112.1 3.7 %all-to-all-start.4 = ((bf16[16,8,1664]{2,1,0:T(8,128)(2,1)}), bf16[16,8,1664]{2,1,0:T(8,128)(2,1)S(1)}, u32[]{:S(2)}, u32[]{:S(2)}) async-start(bf16[16,8,1664]{2,1,0:T(8,128)(2,1)} %bitcast.14), calls=%async_computation.4 | async-start | bytes 851968 | tf_op jit(solution)/shard_map/all_to_all | solution.py:21
  115.9 1.7 %stash.4 = (bf16[1,2,128,768]{3,2,1,0:T(8,128)(2,1)}, f32[8,128]{1,0:T(8,128)S(1)}) custom-call(s32[2,32]{1,0:T(2,128)S(1)} %bitcast.46, bf16[1,2,128,768]{3,2,1,0:T(8,128)(2,1)S(1)} %copy-done.3, bf16[2,128,768]{2,1,0:T(8,128)(2,1)S(1)} %collective-permute-done.arrived, bf16[128,768]{1,0:T(8,128)(2,1)} %collective-permute-done.4.partner1), custom_call_target="tpu_custom_call" | custom-call | flops 12884901888 | bytes 6291456 | tf_op jit(solution)/shard_map/stash/pallas_call | solution.py:340
  117.6 10.6 %all-to-all-done.4 = bf16[16,8,1664]{2,1,0:T(8,128)(2,1)S(1)} async-done(((bf16[16,8,1664]{2,1,0:T(8,128)(2,1)}), bf16[16,8,1664]{2,1,0:T(8,128)(2,1)S(1)}, u32[]{:S(2)}, u32[]{:S(2)}) %all-to-all-start.4) | async-done | bytes 426016 | tf_op jit(solution)/shard_map/all_to_all | solution.py:21
  128.3 3.9 %last.1 = (bf16[512,768]{1,0:T(8,128)(2,1)}, bf16[128,768]{1,0:T(8,128)(2,1)}, bf16[128,768]{1,0:T(8,128)(2,1)}, f32[1,768]{1,0:T(1,128)}, bf16[768,512]{1,0:T(8,128)(2,1)}) custom-call(bf16[512,768]{1,0:T(8,128)(2,1)} %get-tuple-element.48.refs_0_, bf16[128,768]{1,0:T(8,128)(2,1)} %get-tuple-element.49.refs_1_, ...), custom_call_target="tpu_custom_call", output_to_operand_aliasing={{0}: (0, {}), {1}: (1, {})} | custom-call | flops 2147483648 | bytes 1048576 | tf_op jit(solution)/shard_map/last/pallas_call | solution.py:340
  (33 shorter events, 0.7 us)
Async XLA Ops:
  0.6 0.7 copy-start.11
  1.3 1.0 copy-start.2
  2.3 14.9 %copy-start = (bf16[1,768,512]{2,1,0:T(8,128)(2,1)S(1)}, bf16[1,768,512]{2,1,0:T(8,128)(2,1)}, u32[]{:S(2)}) copy-start(bf16[1,768,512]{2,1,0:T(8,128)(2,1)} %param.14) | copy-start | bytes 2359300
  2.3 14.9 %copy-start.1 = (bf16[1,512,768]{2,1,0:T(8,128)(2,1)S(1)}, bf16[1,512,768]{2,1,0:T(8,128)(2,1)}, u32[]{:S(2)}) copy-start(bf16[1,512,768]{2,1,0:T(8,128)(2,1)} %param.15) | copy-start | bytes 2359300
  2.3 14.9 %copy-start.4 = (bf16[1,128,768]{2,1,0:T(8,128)(2,1)S(1)}, bf16[1,128,768]{2,1,0:T(8,128)(2,1)}, u32[]{:S(2)}) copy-start(bf16[1,128,768]{2,1,0:T(8,128)(2,1)} %param.9) | copy-start | bytes 589828
  2.3 14.9 %copy-start.5 = (bf16[1,128,768]{2,1,0:T(8,128)(2,1)S(1)}, bf16[1,128,768]{2,1,0:T(8,128)(2,1)}, u32[]{:S(2)}) copy-start(bf16[1,128,768]{2,1,0:T(8,128)(2,1)} %param.11) | copy-start | bytes 589828
  2.9 23.1 %collective-permute-start.1 = (bf16[128,768]{1,0:T(8,128)(2,1)S(1)}, bf16[128,768]{1,0:T(8,128)(2,1)S(1)}, u32[]{:S(2)}, u32[]{:S(2)}) collective-permute-start(bf16[128,768]{1,0:T(8,128)(2,1)S(1)} %get-tuple-element.38), channel_id=1, source_target_pairs={{0,496},{16,480},{32,464},{48,448},{64,432},{80,416},{96,400},{112... | collective-permute-start | bytes 589832 | tf_op jit(solution)/shard_map/ppermute | solution.py:26
  17.2 0.7 copy-start.10
  18.7 8.4 %copy-start.13 = (bf16[768,512]{1,0:T(8,128)(2,1)}, bf16[768,512]{1,0:T(8,128)(2,1)S(1)}, u32[]{:S(2)}) copy-start(bf16[768,512]{1,0:T(8,128)(2,1)S(1)} %get-tuple-element.35.weight.refs_1_) | copy-start | bytes 2359300
  26.1 1.1 copy-start.8
  27.1 23.3 %all-to-all-start = ((bf16[16,8,1920]{2,1,0:T(8,128)(2,1)}), bf16[16,8,1920]{2,1,0:T(8,128)(2,1)S(1)}, u32[]{:S(2)}, u32[]{:S(2)}) async-start(bf16[16,8,1920]{2,1,0:T(8,128)(2,1)} %bitcast.6), calls=%async_computation | async-start | bytes 983040 | tf_op jit(solution)/shard_map/all_to_all | solution.py:21
  35.1 25.2 %collective-permute-start = (bf16[2,128,768]{2,1,0:T(8,128)(2,1)S(1)}, bf16[2,128,768]{2,1,0:T(8,128)(2,1)S(1)}, u32[]{:S(2)}, u32[]{:S(2)}) collective-permute-start(bf16[2,128,768]{2,1,0:T(8,128)(2,1)S(1)} %get-tuple-element.34), channel_id=1, source_target_pairs={{0,496},{16,480},{32,464},{48,448},{64,432},{80,416},{96,400},{112... | collective-permute-start | bytes 1179656 | tf_op jit(solution)/shard_map/ppermute | solution.py:26
  51.6 14.9 %all-to-all-start.1 = ((bf16[16,8,1152]{2,1,0:T(8,128)(2,1)}), bf16[16,8,1152]{2,1,0:T(8,128)(2,1)S(1)}, u32[]{:S(2)}, u32[]{:S(2)}) async-start(bf16[16,8,1152]{2,1,0:T(8,128)(2,1)} %bitcast.8), calls=%async_computation.1 | async-start | bytes 589824 | tf_op jit(solution)/shard_map/all_to_all | solution.py:21
  56.3 3.9 %copy-start.12 = (s32[32,2]{0,1:T(2,128)S(1)}, s32[32,2]{0,1:T(2,128)}, u32[]{:S(2)}) copy-start(s32[32,2]{0,1:T(2,128)} %param.17) | copy-start | bytes 772
  60.3 1.1 copy-start.14
  61.4 5.1 %copy-start.6 = (bf16[1,128,768]{2,1,0:T(8,128)(2,1)S(1)}, bf16[1,128,768]{2,1,0:T(8,128)(2,1)}, u32[]{:S(2)}) copy-start(bf16[1,128,768]{2,1,0:T(8,128)(2,1)} %param.11) | copy-start | bytes 589828
  61.4 5.1 %copy-start.9 = (bf16[128,768]{1,0:T(8,128)(2,1)S(1)}, bf16[128,768]{1,0:T(8,128)(2,1)}, u32[]{:S(2)}) copy-start(bf16[128,768]{1,0:T(8,128)(2,1)} %copy-done.8) | copy-start | bytes 589828
  62.8 0.7 copy-start.15
  66.5 8.7 %copy-start.16 = (f32[128,512]{1,0:T(8,128)S(1)}, f32[128,512]{1,0:T(8,128)}, u32[]{:S(2)}) copy-start(f32[128,512]{1,0:T(8,128)} %copy-done.15) | copy-start | bytes 786436
  67.7 15.2 %collective-permute-start.3 = (bf16[128,768]{1,0:T(8,128)(2,1)}, bf16[128,768]{1,0:T(8,128)(2,1)S(1)}, u32[]{:S(2)}, u32[]{:S(2)}) collective-permute-start(bf16[128,768]{1,0:T(8,128)(2,1)} %get-tuple-element.44.refs_9_), channel_id=1, source_target_pairs={{16,0},{32,16},{48,32},{64,48},{80,64},{96,80},{112,96},{128,112},... | collective-permute-start | bytes 589832 | tf_op jit(solution)/shard_map/ppermute | solution.py:32
  73.2 9.7 %collective-permute-start.2 = (bf16[128,768]{1,0:T(8,128)(2,1)S(1)}, bf16[128,768]{1,0:T(8,128)(2,1)}, u32[]{:S(2)}, u32[]{:S(2)}) collective-permute-start(bf16[128,768]{1,0:T(8,128)(2,1)S(1)} %get-tuple-element.46.refs_4_), channel_id=1, source_target_pairs={{0,16},{16,32},{32,48},{48,64},{64,80},{80,96},{96,112},{112,128},... | collective-permute-start | bytes 589832 | tf_op jit(solution)/shard_map/ppermute | solution.py:32
  77.0 6.0 %copy-start.7 = (bf16[128,768]{1,0:T(8,128)(2,1)S(1)}, bf16[128,768]{1,0:T(8,128)(2,1)}, u32[]{:S(2)}) copy-start(bf16[128,768]{1,0:T(8,128)(2,1)} %refs_3_.1) | copy-start | bytes 589828
  77.0 18.6 %all-to-all-start.3 = ((bf16[16,8,1152]{2,1,0:T(8,128)(2,1)}), bf16[16,8,1152]{2,1,0:T(8,128)(2,1)S(1)}, u32[]{:S(2)}, u32[]{:S(2)}) async-start(bf16[16,8,1152]{2,1,0:T(8,128)(2,1)} %bitcast.12), calls=%async_computation.3 | async-start | bytes 589824 | tf_op jit(solution)/shard_map/all_to_all | solution.py:21
  95.6 15.5 %all-to-all-start.2 = ((bf16[16,8,1152]{2,1,0:T(8,128)(2,1)}), bf16[16,8,1152]{2,1,0:T(8,128)(2,1)S(1)}, u32[]{:S(2)}, u32[]{:S(2)}) async-start(bf16[16,8,1152]{2,1,0:T(8,128)(2,1)} %bitcast.10), calls=%async_computation.2 | async-start | bytes 589824 | tf_op jit(solution)/shard_map/all_to_all | solution.py:21
  99.2 16.7 %collective-permute-start.4 = (bf16[128,768]{1,0:T(8,128)(2,1)}, bf16[128,768]{1,0:T(8,128)(2,1)}, u32[]{:S(2)}, u32[]{:S(2)}) collective-permute-start(bf16[128,768]{1,0:T(8,128)(2,1)} %get-tuple-element.49.refs_1_), channel_id=1, source_target_pairs={{0,496},{16,480},{32,464},{48,448},{64,432},{80,416},{96,400},{112... | collective-permute-start | bytes 589832 | tf_op jit(solution)/shard_map/ppermute | solution.py:26
  112.1 3.7 %copy-start.3 = (bf16[1,2,128,768]{3,2,1,0:T(8,128)(2,1)S(1)}, bf16[1,2,128,768]{3,2,1,0:T(8,128)(2,1)}, u32[]{:S(2)}) copy-start(bf16[1,2,128,768]{3,2,1,0:T(8,128)(2,1)} %stash.5) | copy-start | bytes 1179652
  112.1 16.1 %all-to-all-start.4 = ((bf16[16,8,1664]{2,1,0:T(8,128)(2,1)}), bf16[16,8,1664]{2,1,0:T(8,128)(2,1)S(1)}, u32[]{:S(2)}, u32[]{:S(2)}) async-start(bf16[16,8,1664]{2,1,0:T(8,128)(2,1)} %bitcast.14), calls=%async_computation.4 | async-start | bytes 851968 | tf_op jit(solution)/shard_map/all_to_all | solution.py:21

commit v8 on v6

--- a/solution.py
+++ b/solution.py
@@ -26,10 +26,11 @@
     return lax.ppermute(value, "section", [(i, sections - 1 - i) for i in range(sections)])
 
 
-def shifted(value, by):
+def swapped(value, first):
     sections = lax.axis_size("section")
-    pairs = [(i, i + by) for i in range(sections) if 0 <= i + by < sections]
-    return lax.ppermute(value, "section", pairs)
+    pairs = [(i, i + 1) for i in range(first, sections - 1, 2)]
+    alone = [(sections - 1, sections - 1)] if (sections - first) % 2 else []
+    return lax.ppermute(value, "section", pairs + [(j, i) for i, j in pairs] + alone)
 
 
 def pieces(value):
@@ -140,61 +141,81 @@
     return [(source.at[pl.ds(i * step, step)], target.at[pl.ds(i * step, step)]) for i in range(count)]
 
 
-def start_kernel(tokens, upstream, gain, down, up, other, payload, weight, column_sum, both, *, peers, rank):
+def scaled_weight(gain, down):
+    features, rank = down.shape
+    tall = jnp.broadcast_to(gain[...].astype(F32), (LANES, features)).T
+    return down[...].astype(F32) * jnp.concatenate([tall] * (rank // LANES), axis=1)
+
+
+def start_kernel(
+    tokens, upstream, gain, down, up, other, payload, weight, column_sum, sums, both, parts, sems, *, peers, rank
+):
     both[0] = other[...]
     both[1] = tokens[...]
-    rows, features = tokens.shape
-    tall = jnp.broadcast_to(gain[...].astype(F32), (LANES, features)).T
-    exact = down[...].astype(F32) * jnp.concatenate([tall] * (rank // LANES), axis=1)
+    rows = tokens.shape[0]
+    parts[:, rank : 2 * rank] = times_transposed(upstream[...], up[...]).astype(BF16)
+    exact = scaled_weight(gain, down)
     rounded = exact.astype(BF16)
     weight[...] = rounded
     one = jnp.sum(rounded.astype(F32), axis=0, keepdims=True)
     column_sum[...] = one
-    two = jnp.sum(exact, axis=0, keepdims=True)
-    half = rank // 2
-    row = lax.broadcasted_iota(jnp.int32, (rows // peers, half), 0)
-    block = jnp.zeros((rows // peers, half), F32)
-    for i, piece in enumerate(pieces(one)[:2] + pieces(two)[:2]):
-        block = jnp.where(row == 2 * i, piece[:, :half], block)
-        block = jnp.where(row == 2 * i + 1, piece[:, half:], block)
-    part, sums = hidden_part(tokens[...], rounded, one)
-    payload[:, :rank] = part.astype(BF16)
-    payload[:, rank : 2 * rank] = times_transposed(upstream[...], up[...]).astype(BF16)
-    payload[:, 2 * rank : 2 * rank + half] = to_all(block, peers)
-    payload[:, 2 * rank + half :] = in_lanes(sums).astype(BF16)
-
-
-def fetched_kernel(tokens, weight, column_sum, early, payload, *, rank):
-    part, sums = hidden_part(tokens[...], weight[...], column_sum[...])
-    block = early.shape[1] - LANES
-    payload[:, :block] = early[:, :block]
-    payload[:, block : block + rank] = part.astype(BF16)
-    payload[:, block + rank :] = (early[:, block:].astype(F32) + in_lanes([0.0] * 6 + sums)).astype(BF16)
+    row = lax.broadcasted_iota(jnp.int32, (rows // peers, LANES), 0)
+    block = jnp.zeros((rows // peers, LANES), F32)
+    quarters = rank // LANES
+    for i, piece in enumerate(pieces(jnp.sum(exact, axis=0, keepdims=True))[:2]):
+        for j in range(quarters):
+            block = jnp.where(row == i * quarters + j, piece[:, j * LANES : (j + 1) * LANES], block)
+    parts[:, 2 * rank :] = to_all(block, peers)
+    part, columns = hidden_part(tokens[...], rounded, one)
+    sums[...] = in_lanes(columns)
+    parts[:, :rank] = part.astype(BF16)
+    (saved,) = copies([(parts, payload.at[:, pl.ds(0, 2 * rank + LANES)])], sems)
+    saved.wait()
+
+
+def fetched_kernel(early, tokens, weight, column_sum, sums0, payload, parts, sums, sems, *, rank):
+    first = 2 * rank + LANES
+    part, columns = hidden_part(tokens[...], weight[...], column_sum[...])
+    parts[...] = part.astype(BF16)
+    sums[...] = (sums0[...] + in_lanes([0.0] * 6 + columns)).astype(BF16)
+    for one in copies(
+        [
+            (parts, payload.at[:, pl.ds(first, rank)]),
+            (sums, payload.at[:, pl.ds(first + rank, LANES)]),
+        ],
+        sems,
+    ):
+        one.wait()
 
 
 def middle_kernel(got, payload, columns_out, active_back, columns, sems, *, peers, rank, width):
-    half = rank // 2
-    blocks = got[:, 2 * rank : 2 * rank + half].astype(F32).reshape(peers, -1, half)
+    first = 2 * rank + LANES
+    blocks = got[:, 2 * rank : first].astype(F32).reshape(peers, -1, LANES)
     row = lax.broadcasted_iota(jnp.int32, blocks.shape[1:], 0)
-
-    def joined(block, first):
-        left = jnp.sum(jnp.where((row == first) | (row == first + 2), block, 0.0), axis=0, keepdims=True)
-        right = jnp.sum(jnp.where((row == first + 1) | (row == first + 3), block, 0.0), axis=0, keepdims=True)
-        return jnp.concatenate([left, right], axis=1)
+    quarters = rank // LANES
+
+    def joined(block):
+        return jnp.concatenate(
+            [
+                jnp.sum(jnp.where((row == i) | (row == quarters + i), block, 0.0), axis=0, keepdims=True)
+                for i in range(quarters)
+            ],
+            axis=1,
+        )
 
     column_sums = []
     for peer in range(peers):
-        column_sums.append(joined(blocks[peer], 0))
+        column_sums.append(joined(blocks[peer]))
         columns[peer : peer + 1, :] = column_sums[peer]
-    column_exact = joined(jnp.sum(blocks, axis=0), 4)
+    column_exact = joined(jnp.sum(blocks, axis=0))
     columns[peers : peers + 1, :] = column_exact
     columns[peers + 1 :, :] = jnp.zeros((7, rank), F32)
     (saved,) = copies([(columns, columns_out)], sems)
-    sums = got[:, 3 * rank + half :].astype(F32)
+    sums = got[:, first + rank :].astype(F32)
     hidden_f = finish_hidden(got[:, :rank], sums, 0, column_sums, width)[0]
     slope = summed(got[:, rank : 2 * rank], peers)
     hidden, mean, inverse = finish_hidden(
-        got[:, 2 * rank + half : 3 * rank + half], sums, 6, column_sums, width
+        got[:, first : first + rank], sums, 6, column_sums, width
     )
     active, bent = gelu_and_slope(hidden)
     active_back[...] = active
@@ -205,13 +226,14 @@
     saved.wait()
 
 
-def first_kernel(got, tokens, fetched, upstream, gain, down, up, after, out, grad, *, rank):
-    out[...] = (
-        tokens[...].astype(F32) + jnp.dot(got[:, :rank], up[...], preferred_element_type=F32)
-    ).astype(BF16)
-    grad[...] = backward(
+def first_kernel(got, tokens, fetched, upstream, gain, down, up, after, beside_out, across_out, *, rank):
+    out = (tokens[...].astype(F32) + jnp.dot(got[:, :rank], up[...], preferred_element_type=F32)).astype(BF16)
+    grad = backward(
         fetched[...], upstream[...], got[:, rank : 2 * rank], got[:, 2 * rank :].astype(F32), gain[...].astype(F32), down[...]
     )[0]
+    odd = lax.rem(lax.axis_index("section"), 2) == 1
+    across_out[...] = jnp.where(odd, out, grad)
+    beside_out[...] = jnp.where(odd, grad, out)
 
 
 def other_kernel(
@@ -227,51 +249,76 @@
 
 
 def terms_kernel(
-    kept_in, got, fetched, upstream, gain, down, kept, gain_term, scaled, sems, *, rank
+    kept_in, got, fetched, upstream, gain, down, active_back, kept, gain_term, payload, scaled, active, sems, *, peers, rank
 ):
+    active[...] = to_all(active_back[...], peers)
+    (ready,) = copies([(active, payload.at[:, pl.ds(3 * rank, rank)])], sems.at[pl.ds(1, 1)])
     scaled[...], gain_term[...] = backward(
         fetched[...], upstream[...], got[:, rank : 2 * rank], got[:, 2 * rank :].astype(F32), gain[...].astype(F32), down[...]
     )[1:]
     rows = scaled.shape[0]
     (saved,) = copies([(scaled, kept.at[pl.ds(rows, rows)])], sems)
     saved.wait()
+    ready.wait()
 
 
 def second_kernel(
-    kept_in, before, after, fresh, own, weight, column_sum, up, side, payload, kept, tokens_out, tokens, upstream, sems,
+    kept_in, beside_in, across_in, fresh, still, weight, column_sum, up, side, payload, kept, tokens_out, tokens, upstream, parts, sems,
     *, rank
 ):
     place = lax.axis_index("section")
-    rows = before.shape[0]
-    tokens[...] = jnp.where(place == 0, fresh[...], before[...])
+    odd = lax.rem(place, 2) == 1
+    rows = fresh.shape[0]
+    tokens[...] = jnp.where(place == 0, fresh[...], jnp.where(odd, beside_in[...], across_in[...]))
     first = pltpu.make_async_copy(tokens, tokens_out, sems.at[0])
     first.start()
-    upstream[...] = jnp.where(place == lax.axis_size("section") - 1, own[...], after[...])
+    upstream[...] = jnp.where(odd, across_in[...], beside_in[...])
     second = pltpu.make_async_copy(upstream, kept.at[pl.ds(2 * rows, rows)], sems.at[1])
     second.start()
+    parts[:, 2 * rank : 3 * rank] = side[:, :rank]
+    parts[:, rank : 2 * rank] = times_transposed(upstream[...], up[...]).astype(BF16)
+    span = pl.ds(rank, 2 * rank)
+    third = pltpu.make_async_copy(parts.at[:, span], payload.at[:, span], sems.at[2])
+    third.start()
     part, sums = hidden_part(tokens[...], weight[...], column_sum[...])
-    payload[:, :rank] = part.astype(BF16)
-    payload[:, rank : 2 * rank] = times_transposed(upstream[...], up[...]).astype(BF16)
-    payload[:, 2 * rank : 3 * rank] = side[:, :rank]
-    payload[:, 3 * rank :] = (side[:, rank:].astype(F32) + in_lanes(sums)).astype(BF16)
-    first.wait()
-    second.wait()
-
-
-def late_kernel(got, columns, active_back, payload, *, peers, rank, width):
+    parts[:, :rank] = part.astype(BF16)
+    span = pl.ds(0, rank)
+    fourth = pltpu.make_async_copy(parts.at[:, span], payload.at[:, span], sems.at[3])
+    fourth.start()
+    parts[:, 3 * rank :] = (side[:, rank:].astype(F32) + in_lanes(sums)).astype(BF16)
+    span = pl.ds(3 * rank, LANES)
+    fifth = pltpu.make_async_copy(parts.at[:, span], payload.at[:, span], sems.at[4])
+    fifth.start()
+    for one in (first, second, third, fourth, fifth):
+        one.wait()
+
+
+def late_kernel(filled, got, columns, payload, parts, last, sems, *, peers, rank, width):
     column_sums = [columns[peer : peer + 1, :] for peer in range(peers)]
     sums = got[:, 3 * rank :].astype(F32)
-    hidden_f = finish_hidden(got[:, :rank], sums, 0, column_sums, width)[0]
-    slope = summed(got[:, rank : 2 * rank], peers)
+    stores = []
+
+    def store(source, first, lanes):
+        stores.append(pltpu.make_async_copy(source, payload.at[:, pl.ds(first, lanes)], sems.at[len(stores)]))
+        stores[-1].start()
+
     hidden, mean, inverse = finish_hidden(got[:, 2 * rank : 3 * rank], sums, 6, column_sums, width)
     active, bent = gelu_and_slope(hidden)
+    parts[0] = to_all(active, peers)
+    store(parts.at[0], 2 * rank, rank)
+    slope = summed(got[:, rank : 2 * rank], peers)
     grad_hidden = (slope * bent).astype(BF16)
-    payload[:, :rank] = to_all(gelu(hidden_f), peers)
-    payload[:, rank : 2 * rank] = to_all(grad_hidden.astype(F32), peers)
-    payload[:, 2 * rank : 3 * rank] = to_all(active, peers)
-    payload[:, 3 * rank : 4 * rank] = to_all(active_back[...], peers)
-    stats = back_stats(grad_hidden, hidden, mean, inverse, columns[peers : peers + 1, :], width)
-    payload[:, 4 * rank :] = to_all(stats, peers)
+    parts[1] = to_all(grad_hidden.astype(F32), peers)
+    store(parts.at[1], rank, rank)
+    last[...] = to_all(
+        back_stats(grad_hidden, hidden, mean, inverse, columns[peers : peers + 1, :], width), peers
+    )
+    store(last, 4 * rank, LANES)
+    hidden_f = finish_hidden(got[:, :rank], sums, 0, column_sums, width)[0]
+    parts[2] = to_all(gelu(hidden_f), peers)
+    store(parts.at[2], 0, rank)
+    for one in stores:
+        one.wait()
 
 
 def stash_kernel(evict, stash, arrived, partner1, stash_out, done):
@@ -283,49 +330,57 @@
 
 
 def last_kernel(
-    kept_in, tokens_in, done, got, got0, upstream0, gain_term0, gain, down, up,
-    up_grad_out, out_out, grad_out, gain_grad, down_grad_out, kept, tokens, up_grad, out, grad, down_grad,
-    sems, up_sems, down_sems, *, rank
+    kept_in, tokens_in, done, got, got0, upstream0_in, gain_term0, gain, down, up,
+    up_grad_out, out_out, grad_out, gain_grad, down_grad_out, tiles, up_grad, out, grad, down_grad,
+    load_sems, sems, up_sems, down_sems, *, rank
 ):
-    rows = upstream0.shape[0]
-    span = pl.ds(2 * rows, rows)
+    rows = tokens_in.shape[0]
     loads = copies(
         [
-            (kept_in.at[span], kept.at[span]),
-            (tokens_in, tokens),
-            (kept_in.at[pl.ds(0, 2 * rows)], kept.at[pl.ds(0, 2 * rows)]),
+            (kept_in.at[pl.ds(2 * rows, rows)], tiles.at[0]),
+            (tokens_in, tiles.at[1]),
+            (kept_in.at[pl.ds(0, rows)], tiles.at[2]),
+            (kept_in.at[pl.ds(rows, rows)], tiles.at[3]),
         ],
-        sems,
-    )
+        load_sems,
+    )
+    grad_hidden = got[:, rank : 2 * rank]
     product = jnp.dot(got[:, :rank], up[...], preferred_element_type=F32)
+    grad_scaled = times_transposed(grad_hidden, down[...])
+    sums = got[:, 4 * rank :].astype(F32)
+    mean, inverse, first, second = [from_lanes(sums, 3 * i) for i in range(4)]
+    grad_normed = grad_scaled * gain[...].astype(F32)
+    active_both = jnp.concatenate([got[:, 3 * rank : 4 * rank], got[:, 2 * rank : 3 * rank]], axis=0)
+    hidden_both = jnp.concatenate([got0[:, rank : 2 * rank], grad_hidden], axis=0)
+    stores = []
+
+    def store(source, target, sem):
+        stores.append(pltpu.make_async_copy(source, target, sem))
+        stores[-1].start()
+
     loads[0].wait()
-    upstream = kept[2 * rows : 3 * rows]
-    up_grad[...] = transposed_times(
-        jnp.concatenate([got[:, 3 * rank : 4 * rank], got[:, 2 * rank : 3 * rank]], axis=0),
-        jnp.concatenate([upstream0[...], upstream], axis=0),
-    ).astype(BF16)
-    loads[1].wait()
-    out[...] = (tokens[...].astype(F32) + product).astype(BF16)
-    loads[2].wait()
-    up_stores = copies(chunks(up_grad, up_grad_out, CHUNKS), up_sems)
-    out_store = pltpu.make_async_copy(out, out_out, sems.at[3])
-    out_store.start()
-    grad[...], scaled, gain_term = backward(
-        kept[:rows], upstream, got[:, rank : 2 * rank], got[:, 4 * rank :].astype(F32), gain[...].astype(F32), down[...]
-    )
-    grad_store = pltpu.make_async_copy(grad, grad_out, sems.at[4])
-    grad_store.start()
-    gain_grad[...] = gain_term0[...] + gain_term
-    tokens_both = jnp.concatenate([kept[rows : 2 * rows], scaled], axis=0)
-    hidden_both = jnp.concatenate([got0[:, rank : 2 * rank], got[:, rank : 2 * rank]], axis=0)
-    down_stores = []
-    step = down_grad.shape[0] // 2
-    for i, (part, target) in enumerate(chunks(down_grad, down_grad_out, 2)):
-        part[...] = transposed_times(tokens_both[:, i * step : (i + 1) * step], hidden_both).astype(BF16)
-        for j, (source, place) in enumerate(chunks(part, target, CHUNKS // 2)):
-            down_stores.append(pltpu.make_async_copy(source, place, down_sems.at[i * (CHUNKS // 2) + j]))
-            down_stores[-1].start()
-    for one in up_stores + down_stores + [out_store, grad_store]:
+    upstream = tiles[0]
+    upstream_both = jnp.concatenate([upstream0_in[...], upstream], axis=0)
+    step = rank // CHUNKS
+    for i, (part, target) in enumerate(chunks(up_grad, up_grad_out, CHUNKS)):
+        part[...] = transposed_times(active_both[:, i * step : (i + 1) * step], upstream_both).astype(BF16)
+        if i == 0:
+            loads[1].wait()
+            loads[2].wait()
+            loads[3].wait()
+        store(part, target, up_sems.at[i])
+    out[...] = (tiles[1].astype(F32) + product).astype(BF16)
+    store(out, out_out, sems.at[0])
+    normed = (tiles[2].astype(F32) - mean) * inverse
+    grad[...] = (upstream.astype(F32) + inverse * (grad_normed - first - normed * second)).astype(BF16)
+    store(grad, grad_out, sems.at[1])
+    gain_grad[...] = gain_term0[...] + jnp.sum(grad_scaled * normed, axis=0, keepdims=True)
+    scaled_both = jnp.concatenate([tiles[3], (normed * gain[...].astype(F32)).astype(BF16)], axis=0)
+    step = down_grad.shape[0] // CHUNKS
+    for i, (part, target) in enumerate(chunks(down_grad, down_grad_out, CHUNKS)):
+        part[...] = transposed_times(scaled_both[:, i * step : (i + 1) * step], hidden_both).astype(BF16)
+        store(part, target, down_sems.at[i])
+    for one in stores:
         one.wait()
 
 
@@ -364,7 +419,6 @@
     def shape(*dims, dtype=BF16):
         return jax.ShapeDtypeStruct(dims, dtype)
 
-    half = rank // 2
     tile = pltpu.VMEM((rows, features), BF16)
     sems = pltpu.SemaphoreType.DMA
     fetch, evict = fetch_slot.T, evict_slot.T
@@ -377,16 +431,28 @@
         name="pick",
     )
     fetched0 = mirrored(picked)
-    early, weight, column_sum, both = call(
+    early, weight, column_sum, sums0, both = call(
         bound(start_kernel, peers=peers, rank=rank),
-        [shape(rows, 2 * rank + half + LANES), shape(features, rank), shape(1, rank, dtype=F32), shape(2, rows, features)],
+        [
+            shape(rows, 3 * rank + 2 * LANES),
+            shape(features, rank),
+            shape(1, rank, dtype=F32),
+            shape(rows, LANES, dtype=F32),
+            shape(2, rows, features),
+        ],
         [tokens0, grad0, norm_gain, down, up, other],
+        left_outs=(0,),
+        scratch=[pltpu.VMEM((rows, 2 * rank + LANES), BF16), sems((1,))],
         name="start",
     )
     (payload,) = call(
         bound(fetched_kernel, rank=rank),
-        [shape(rows, 3 * rank + half + LANES)],
-        [fetched0, weight, column_sum, early],
+        [shape(rows, 3 * rank + 2 * LANES)],
+        [early, fetched0, weight, column_sum, sums0],
+        left=(0,),
+        left_outs=(0,),
+        aliases=[(0, 0)],
+        scratch=[pltpu.VMEM((rows, rank), BF16), pltpu.VMEM((rows, LANES), BF16), sems((2,))],
         name="fetched",
     )
     got = across(payload)
@@ -410,34 +476,34 @@
         cost=LONG,
         name="other",
     )
-    first_out, first_grad = call(
+    beside_out, across_out = call(
         bound(first_kernel, rank=rank),
         [shape(rows, features)] * 2,
         [got0, tokens0, fetched0, grad0, norm_gain, down, up, other],
         left=(7,),
         name="first",
     )
-    before_out = shifted(first_out, 1)
-    after_grad = shifted(first_grad, -1)
-    kept, gain_term0 = call(
-        bound(terms_kernel, rank=rank),
-        [shape(rank, features), shape(1, features, dtype=F32)],
-        [kept, got0, fetched0, grad0, norm_gain, down],
+    beside_in = swapped(beside_out, 0)
+    across_in = swapped(across_out, 1)
+    kept, gain_term0, filled = call(
+        bound(terms_kernel, peers=peers, rank=rank),
+        [shape(rank, features), shape(1, features, dtype=F32), shape(rows, 4 * rank + LANES)],
+        [kept, got0, fetched0, grad0, norm_gain, down, active_back],
         left=(0,),
-        left_outs=(0,),
+        left_outs=(0, 2),
         aliases=[(0, 0)],
-        scratch=[tile, sems((1,))],
+        scratch=[tile, pltpu.VMEM((rows, rank), BF16), sems((2,))],
         cost=LONG,
         name="terms",
     )
     payload, kept, tokens1 = call(
         bound(second_kernel, rank=rank),
         [shape(rows, 3 * rank + LANES), shape(rank, features), shape(rows, features)],
-        [kept, before_out, after_grad, fresh_input, first_out, weight, column_sum, up, other],
-        left=(0,),
-        left_outs=(1, 2),
+        [kept, beside_in, across_in, fresh_input, beside_out, weight, column_sum, up, other],
+        left=(0, 4),
+        left_outs=(0, 1, 2),
         aliases=[(0, 1)],
-        scratch=[tile, tile, sems((2,))],
+        scratch=[tile, tile, pltpu.VMEM((rows, 3 * rank + LANES), BF16), sems((5,))],
         name="second",
     )
     got = across(payload)
@@ -445,7 +511,11 @@
     (payload,) = call(
         bound(late_kernel, peers=peers, rank=rank, width=width),
         [shape(rows, 4 * rank + LANES)],
-        [got, columns, active_back],
+        [filled, got, columns],
+        left=(0,),
+        left_outs=(0,),
+        aliases=[(0, 0)],
+        scratch=[pltpu.VMEM((3, rows, rank), BF16), pltpu.VMEM((rows, LANES), BF16), sems((4,))],
         name="late",
     )
     got1 = across(payload)
@@ -471,13 +541,13 @@
         left_outs=(0, 1, 2, 4),
         aliases=[(0, 0), (1, 1)],
         scratch=[
-            pltpu.VMEM((3 * rows, features), BF16),
-            tile,
+            pltpu.VMEM((4, rows, features), BF16),
             pltpu.VMEM((rank, features), BF16),
             tile,
             tile,
             pltpu.VMEM((features, rank), BF16),
-            sems((5,)),
+            sems((4,)),
+            sems((2,)),
             sems((CHUNKS,)),
             sems((CHUNKS,)),
         ],

time: 126 us -> 125 us (level)
  the two profiles are of different devices: /device:TPU:1 before, /device:TPU:134 now
where the time goes in v8:
time: 125 us; the launch traced here: 124 us
  waiting for transfers between devices  56.1 us (45%)
  starting transfers between devices  48.9 us (39%)
  Pallas kernels  14.8 us (12%)
  local copies, waits for them, and re-layouts  3.63 us (3%)
    all_to_all x4, waiting for transfers between devices, across(): return lax.all_to_all(block, 'dp', 0, 0, tiled=True)  43.1 us
    all_to_all x4, starting transfers between devices, across(): return lax.all_to_all(block, 'dp', 0, 0, tiled=True)  19.7 us
    ppermute x3, starting transfers between devices, mirrored(): lax.ppermute(value, 'section', [(i, sections - 1 - i) for i in range(sect...  19.1 us
    pallas_call x11, Pallas kernels, call(): pl.pallas_call(body, out_shape=tuple(outs), in_specs=[pl.BlockSpec(memory...  14.8 us
    ppermute x3, waiting for transfers between devices, mirrored(): lax.ppermute(value, 'section', [(i, sections - 1 - i) for i in range(sect...  13 us
    ppermute x2, starting transfers between devices, swapped(): lax.ppermute(value, 'section', pairs + [(j, i) for i, j in pairs] + alone)  10.1 us
    unnamed x34, local copies, waits for them, and re-layouts  3.63 us
  transfers between devices with their start and end apart: 9, of which 6 were waited for; matrix products, arithmetic and copies ran while one was open for 0% of the time, Pallas kernels for 6%

profile of v8, /device:TPU:134, one launch (start us, length us, event | category | flops | bytes accessed | tf_op | source)
XLA Modules:
  0.0 124.4 jit_solution(556670583892709691)
XLA Ops:
  0.6 0.7 copy-done.12
  1.3 1.0 copy-done.2
  2.3 0.6 pick.1
  2.9 6.7 %collective-permute-start.1 = (bf16[128,768]{1,0:T(8,128)(2,1)S(1)}, bf16[128,768]{1,0:T(8,128)(2,1)S(1)}, u32[]{:S(2)}, u32[]{:S(2)}) collective-permute-start(bf16[128,768]{1,0:T(8,128)(2,1)S(1)} %get-tuple-element.39), channel_id=1, source_target_pairs={{0,496},{16,480},{32,464},{48,448},{64,432},{80,416},{96,400},{112... | collective-permute-start | bytes 589832 | tf_op jit(solution)/shard_map/ppermute | solution.py:26
  9.6 0.6 copy-done.11
  10.3 1.5 %start.1 = (bf16[128,1792]{1,0:T(8,128)(2,1)}, bf16[768,512]{1,0:T(8,128)(2,1)S(1)}, f32[1,512]{1,0:T(1,128)S(1)}, f32[128,128]{1,0:T(8,128)S(1)}, bf16[2,128,768]{2,1,0:T(8,128)(2,1)S(1)}) custom-call(bf16[128,768]{1,0:T(8,128)(2,1)S(1)} %bitcast.32, bf16[128,768]{1,0:T(8,128)(2,1)S(1)} %bitcast.35, bf16[1,768]{1,0:T(2,128)(2,1)S(1)} %copy-done.11, ...), custom_call_target="tpu_custom_call" | custom-call | flops 2147483648 | bytes 1048576 | tf_op jit(solution)/shard_map/start/pallas_call | solution.py:390
  11.7 0.0 copy-start.14
  11.7 8.7 %collective-permute-done.1.refs_1_.refs_2_ = bf16[128,768]{1,0:T(8,128)(2,1)S(1)} collective-permute-done((bf16[128,768]{1,0:T(8,128)(2,1)S(1)}, bf16[128,768]{1,0:T(8,128)(2,1)S(1)}, u32[]{:S(2)}, u32[]{:S(2)}) %collective-permute-start.1) | collective-permute-done | bytes 196640 | tf_op jit(solution)/shard_map/ppermute | solution.py:26
  20.4 1.0 fetched.1
  21.4 7.2 %all-to-all-start = ((bf16[16,8,1792]{2,1,0:T(8,128)(2,1)}), bf16[16,8,1792]{2,1,0:T(8,128)(2,1)S(1)}, u32[]{:S(2)}, u32[]{:S(2)}) async-start(bf16[16,8,1792]{2,1,0:T(8,128)(2,1)} %bitcast.6), calls=%async_computation | async-start | bytes 917504 | tf_op jit(solution)/shard_map/all_to_all | solution.py:21
  28.7 7.6 %collective-permute-start = (bf16[2,128,768]{2,1,0:T(8,128)(2,1)S(1)}, bf16[2,128,768]{2,1,0:T(8,128)(2,1)S(1)}, u32[]{:S(2)}, u32[]{:S(2)}) collective-permute-start(bf16[2,128,768]{2,1,0:T(8,128)(2,1)S(1)} %get-tuple-element.34), channel_id=1, source_target_pairs={{0,496},{16,480},{32,464},{48,448},{64,432},{80,416},{96,400},{112... | collective-permute-start | bytes 1179656 | tf_op jit(solution)/shard_map/ppermute | solution.py:26
  36.2 8.9 %all-to-all-done = bf16[16,8,1792]{2,1,0:T(8,128)(2,1)S(1)} async-done(((bf16[16,8,1792]{2,1,0:T(8,128)(2,1)}), bf16[16,8,1792]{2,1,0:T(8,128)(2,1)S(1)}, u32[]{:S(2)}, u32[]{:S(2)}) %all-to-all-start) | async-done | bytes 458784 | tf_op jit(solution)/shard_map/all_to_all | solution.py:21
  45.1 1.1 middle.1
  46.3 3.5 %all-to-all-start.1 = ((bf16[16,8,1152]{2,1,0:T(8,128)(2,1)}), bf16[16,8,1152]{2,1,0:T(8,128)(2,1)S(1)}, u32[]{:S(2)}, u32[]{:S(2)}) async-start(bf16[16,8,1152]{2,1,0:T(8,128)(2,1)} %bitcast.8), calls=%async_computation.1 | async-start | bytes 589824 | tf_op jit(solution)/shard_map/all_to_all | solution.py:21
  49.9 4.3 %collective-permute-done.refs_2_.arrived = bf16[2,128,768]{2,1,0:T(8,128)(2,1)S(1)} collective-permute-done((bf16[2,128,768]{2,1,0:T(8,128)(2,1)S(1)}, bf16[2,128,768]{2,1,0:T(8,128)(2,1)S(1)}, u32[]{:S(2)}, u32[]{:S(2)}) %collective-permute-start) | collective-permute-done | bytes 393248 | tf_op jit(solution)/shard_map/ppermute | solution.py:26
  54.2 1.1 copy-done.15
  55.3 1.4 %other.1 = (bf16[128,640]{1,0:T(8,128)(2,1)S(1)}, bf16[512,768]{1,0:T(8,128)(2,1)}) custom-call(s32[2,32]{1,0:T(2,128)S(1)} %bitcast.40, s32[2,32]{1,0:T(2,128)S(1)} %bitcast.41, bf16[2,128,768]{2,1,0:T(8,128)(2,1)S(1)} %collective-permute-done.refs_2_.arrived, bf16[128,768]{1,0:T(8,128)(2,1)S(1)} %bitcast.33, bf16[768,512]{1,0:T(8,128)(2,1)S(1)} %copy-done.15, ...), custom_call_target="tpu_custom_call" | custom-call | flops 12884901888 | bytes 6291456 | tf_op jit(solution)/shard_map/other/pallas_call | solution.py:390
  56.7 5.3 %all-to-all-done.1 = bf16[16,8,1152]{2,1,0:T(8,128)(2,1)S(1)} async-done(((bf16[16,8,1152]{2,1,0:T(8,128)(2,1)}), bf16[16,8,1152]{2,1,0:T(8,128)(2,1)S(1)}, u32[]{:S(2)}, u32[]{:S(2)}) %all-to-all-start.1) | async-done | bytes 294944 | tf_op jit(solution)/shard_map/all_to_all | solution.py:21
  62.1 0.6 first.1
  62.6 1.9 %collective-permute-start.3 = (bf16[128,768]{1,0:T(8,128)(2,1)S(1)}, bf16[128,768]{1,0:T(8,128)(2,1)S(1)}, u32[]{:S(2)}, u32[]{:S(2)}) collective-permute-start(bf16[128,768]{1,0:T(8,128)(2,1)S(1)} %get-tuple-element.46), channel_id=1, source_target_pairs={{16,32},{48,64},{80,96},{112,128},{144,160},{176,192},{208,224},{2... | collective-permute-start | bytes 589832 | tf_op jit(solution)/shard_map/ppermute | solution.py:33
  64.5 8.2 %collective-permute-start.2 = (bf16[128,768]{1,0:T(8,128)(2,1)S(1)}, bf16[128,768]{1,0:T(8,128)(2,1)S(1)}, u32[]{:S(2)}, u32[]{:S(2)}) collective-permute-start(bf16[128,768]{1,0:T(8,128)(2,1)S(1)} %get-tuple-element.45.refs_4_), channel_id=1, source_target_pairs={{0,16},{32,48},{64,80},{96,112},{128,144},{160,176},{192,208},{224... | collective-permute-start | bytes 589832 | tf_op jit(solution)/shard_map/ppermute | solution.py:33
  72.8 1.1 terms.1
  73.9 0.1 copy-done.16
  74.0 1.3 %second.1 = (bf16[128,1664]{1,0:T(8,128)(2,1)}, bf16[512,768]{1,0:T(8,128)(2,1)}, bf16[128,768]{1,0:T(8,128)(2,1)}) custom-call(bf16[512,768]{1,0:T(8,128)(2,1)} %get-tuple-element.43.refs_0_, bf16[128,768]{1,0:T(8,128)(2,1)S(1)} %collective-permute-done.2.refs_1_, ...), custom_call_target="tpu_custom_call", output_to_operand_aliasing={{1}: (0, {})} | custom-call | flops 2147483648 | bytes 1048576 | tf_op jit(solution)/shard_map/second/pallas_call | solution.py:390
  75.3 5.1 %all-to-all-start.2 = ((bf16[16,8,1664]{2,1,0:T(8,128)(2,1)}), bf16[16,8,1664]{2,1,0:T(8,128)(2,1)S(1)}, u32[]{:S(2)}, u32[]{:S(2)}) async-start(bf16[16,8,1664]{2,1,0:T(8,128)(2,1)} %bitcast.10), calls=%async_computation.2 | async-start | bytes 851968 | tf_op jit(solution)/shard_map/all_to_all | solution.py:21
  80.4 4.9 %collective-permute-start.4 = (bf16[128,768]{1,0:T(8,128)(2,1)}, bf16[128,768]{1,0:T(8,128)(2,1)}, u32[]{:S(2)}, u32[]{:S(2)}) collective-permute-start(bf16[128,768]{1,0:T(8,128)(2,1)} %get-tuple-element.48.refs_1_), channel_id=1, source_target_pairs={{0,496},{16,480},{32,464},{48,448},{64,432},{80,416},{96,400},{112... | collective-permute-start | bytes 589832 | tf_op jit(solution)/shard_map/ppermute | solution.py:26
  85.3 11.9 %all-to-all-done.2 = bf16[16,8,1664]{2,1,0:T(8,128)(2,1)S(1)} async-done(((bf16[16,8,1664]{2,1,0:T(8,128)(2,1)}), bf16[16,8,1664]{2,1,0:T(8,128)(2,1)S(1)}, u32[]{:S(2)}, u32[]{:S(2)}) %all-to-all-start.2) | async-done | bytes 426016 | tf_op jit(solution)/shard_map/all_to_all | solution.py:21
  97.2 1.0 late.1
  98.3 3.8 %all-to-all-start.3 = ((bf16[16,8,2176]{2,1,0:T(8,128)(2,1)}), bf16[16,8,2176]{2,1,0:T(8,128)(2,1)S(1)}, u32[]{:S(2)}, u32[]{:S(2)}) async-start(bf16[16,8,2176]{2,1,0:T(8,128)(2,1)} %bitcast.12), calls=%async_computation.3 | async-start | bytes 1114112 | tf_op jit(solution)/shard_map/all_to_all | solution.py:21
  102.1 1.8 %stash.4 = (bf16[1,2,128,768]{3,2,1,0:T(8,128)(2,1)}, f32[8,128]{1,0:T(8,128)S(1)}) custom-call(s32[2,32]{1,0:T(2,128)S(1)} %bitcast.42, bf16[1,2,128,768]{3,2,1,0:T(8,128)(2,1)S(1)} %copy-done.3, bf16[2,128,768]{2,1,0:T(8,128)(2,1)S(1)} %collective-permute-done.refs_2_.arrived, bf16[128,768]{1,0:T(8,128)(2,1)} %collective-permute-done.4.partner1), custom_call_target="tpu_custom_call" | custom-call | flops 12884901888 | bytes 6291456 | tf_op jit(solution)/shard_map/stash/pallas_call | solution.py:390
  103.9 16.9 %all-to-all-done.3 = bf16[16,8,2176]{2,1,0:T(8,128)(2,1)S(1)} async-done(((bf16[16,8,2176]{2,1,0:T(8,128)(2,1)}), bf16[16,8,2176]{2,1,0:T(8,128)(2,1)S(1)}, u32[]{:S(2)}, u32[]{:S(2)}) %all-to-all-start.3) | async-done | bytes 557088 | tf_op jit(solution)/shard_map/all_to_all | solution.py:21
  120.9 3.6 %last.1 = (bf16[512,768]{1,0:T(8,128)(2,1)}, bf16[128,768]{1,0:T(8,128)(2,1)}, bf16[128,768]{1,0:T(8,128)(2,1)}, f32[1,768]{1,0:T(1,128)}, bf16[768,512]{1,0:T(8,128)(2,1)}) custom-call(bf16[512,768]{1,0:T(8,128)(2,1)} %get-tuple-element.47.refs_0_, bf16[128,768]{1,0:T(8,128)(2,1)} %get-tuple-element.48.refs_1_, ...), custom_call_target="tpu_custom_call", output_to_operand_aliasing={{0}: (0, {}), {1}: (1, {})} | custom-call | flops 2147483648 | bytes 1048576 | tf_op jit(solution)/shard_map/last/pallas_call | solution.py:390
  (31 shorter events, 0.1 us)
Async XLA Ops:
  0.6 0.7 copy-start.12
  1.3 1.0 copy-start.2
  2.3 7.3 %copy-start = (bf16[1,768,512]{2,1,0:T(8,128)(2,1)S(1)}, bf16[1,768,512]{2,1,0:T(8,128)(2,1)}, u32[]{:S(2)}) copy-start(bf16[1,768,512]{2,1,0:T(8,128)(2,1)} %param.14) | copy-start | bytes 2359300
  2.3 7.3 %copy-start.1 = (bf16[1,512,768]{2,1,0:T(8,128)(2,1)S(1)}, bf16[1,512,768]{2,1,0:T(8,128)(2,1)}, u32[]{:S(2)}) copy-start(bf16[1,512,768]{2,1,0:T(8,128)(2,1)} %param.15) | copy-start | bytes 2359300
  2.3 7.3 %copy-start.4 = (bf16[1,128,768]{2,1,0:T(8,128)(2,1)S(1)}, bf16[1,128,768]{2,1,0:T(8,128)(2,1)}, u32[]{:S(2)}) copy-start(bf16[1,128,768]{2,1,0:T(8,128)(2,1)} %param.9) | copy-start | bytes 589828
  2.3 7.3 %copy-start.6 = (bf16[1,128,768]{2,1,0:T(8,128)(2,1)S(1)}, bf16[1,128,768]{2,1,0:T(8,128)(2,1)}, u32[]{:S(2)}) copy-start(bf16[1,128,768]{2,1,0:T(8,128)(2,1)} %param.11) | copy-start | bytes 589828
  2.9 17.5 %collective-permute-start.1 = (bf16[128,768]{1,0:T(8,128)(2,1)S(1)}, bf16[128,768]{1,0:T(8,128)(2,1)S(1)}, u32[]{:S(2)}, u32[]{:S(2)}) collective-permute-start(bf16[128,768]{1,0:T(8,128)(2,1)S(1)} %get-tuple-element.39), channel_id=1, source_target_pairs={{0,496},{16,480},{32,464},{48,448},{64,432},{80,416},{96,400},{112... | collective-permute-start | bytes 589832 | tf_op jit(solution)/shard_map/ppermute | solution.py:26
  9.6 0.7 copy-start.11
  11.7 9.7 %copy-start.14 = (bf16[768,512]{1,0:T(8,128)(2,1)}, bf16[768,512]{1,0:T(8,128)(2,1)S(1)}, u32[]{:S(2)}) copy-start(bf16[768,512]{1,0:T(8,128)(2,1)S(1)} %get-tuple-element.35.refs_4_.refs_2_.refs_5_) | copy-start | bytes 2359300
  20.4 1.0 copy-start.9
  21.4 23.7 %all-to-all-start = ((bf16[16,8,1792]{2,1,0:T(8,128)(2,1)}), bf16[16,8,1792]{2,1,0:T(8,128)(2,1)S(1)}, u32[]{:S(2)}, u32[]{:S(2)}) async-start(bf16[16,8,1792]{2,1,0:T(8,128)(2,1)} %bitcast.6), calls=%async_computation | async-start | bytes 917504 | tf_op jit(solution)/shard_map/all_to_all | solution.py:21
  28.7 25.5 %collective-permute-start = (bf16[2,128,768]{2,1,0:T(8,128)(2,1)S(1)}, bf16[2,128,768]{2,1,0:T(8,128)(2,1)S(1)}, u32[]{:S(2)}, u32[]{:S(2)}) collective-permute-start(bf16[2,128,768]{2,1,0:T(8,128)(2,1)S(1)} %get-tuple-element.34), channel_id=1, source_target_pairs={{0,496},{16,480},{32,464},{48,448},{64,432},{80,416},{96,400},{112... | collective-permute-start | bytes 1179656 | tf_op jit(solution)/shard_map/ppermute | solution.py:26
  46.3 15.7 %all-to-all-start.1 = ((bf16[16,8,1152]{2,1,0:T(8,128)(2,1)}), bf16[16,8,1152]{2,1,0:T(8,128)(2,1)S(1)}, u32[]{:S(2)}, u32[]{:S(2)}) async-start(bf16[16,8,1152]{2,1,0:T(8,128)(2,1)} %bitcast.8), calls=%async_computation.1 | async-start | bytes 589824 | tf_op jit(solution)/shard_map/all_to_all | solution.py:21
  49.9 4.3 %copy-start.13 = (s32[32,2]{0,1:T(2,128)S(1)}, s32[32,2]{0,1:T(2,128)}, u32[]{:S(2)}) copy-start(s32[32,2]{0,1:T(2,128)} %param.17) | copy-start | bytes 772
  54.2 1.1 copy-start.15
  55.3 6.7 %copy-start.7 = (bf16[1,128,768]{2,1,0:T(8,128)(2,1)S(1)}, bf16[1,128,768]{2,1,0:T(8,128)(2,1)}, u32[]{:S(2)}) copy-start(bf16[1,128,768]{2,1,0:T(8,128)(2,1)} %param.11) | copy-start | bytes 589828
  55.3 6.7 %copy-start.10 = (bf16[128,768]{1,0:T(8,128)(2,1)S(1)}, bf16[128,768]{1,0:T(8,128)(2,1)}, u32[]{:S(2)}) copy-start(bf16[128,768]{1,0:T(8,128)(2,1)} %copy-done.9) | copy-start | bytes 589828
  62.6 11.2 %collective-permute-start.3 = (bf16[128,768]{1,0:T(8,128)(2,1)S(1)}, bf16[128,768]{1,0:T(8,128)(2,1)S(1)}, u32[]{:S(2)}, u32[]{:S(2)}) collective-permute-start(bf16[128,768]{1,0:T(8,128)(2,1)S(1)} %get-tuple-element.46), channel_id=1, source_target_pairs={{16,32},{48,64},{80,96},{112,128},{144,160},{176,192},{208,224},{2... | collective-permute-start | bytes 589832 | tf_op jit(solution)/shard_map/ppermute | solution.py:33
  64.5 9.3 %collective-permute-start.2 = (bf16[128,768]{1,0:T(8,128)(2,1)S(1)}, bf16[128,768]{1,0:T(8,128)(2,1)S(1)}, u32[]{:S(2)}, u32[]{:S(2)}) collective-permute-start(bf16[128,768]{1,0:T(8,128)(2,1)S(1)} %get-tuple-element.45.refs_4_), channel_id=1, source_target_pairs={{0,16},{32,48},{64,80},{96,112},{128,144},{160,176},{192,208},{224... | collective-permute-start | bytes 589832 | tf_op jit(solution)/shard_map/ppermute | solution.py:33
  72.7 1.1 copy-start.5
  72.7 1.2 copy-start.16
  75.3 22.0 %all-to-all-start.2 = ((bf16[16,8,1664]{2,1,0:T(8,128)(2,1)}), bf16[16,8,1664]{2,1,0:T(8,128)(2,1)S(1)}, u32[]{:S(2)}, u32[]{:S(2)}) async-start(bf16[16,8,1664]{2,1,0:T(8,128)(2,1)} %bitcast.10), calls=%async_computation.2 | async-start | bytes 851968 | tf_op jit(solution)/shard_map/all_to_all | solution.py:21
  80.4 21.8 %collective-permute-start.4 = (bf16[128,768]{1,0:T(8,128)(2,1)}, bf16[128,768]{1,0:T(8,128)(2,1)}, u32[]{:S(2)}, u32[]{:S(2)}) collective-permute-start(bf16[128,768]{1,0:T(8,128)(2,1)} %get-tuple-element.48.refs_1_), channel_id=1, source_target_pairs={{0,496},{16,480},{32,464},{48,448},{64,432},{80,416},{96,400},{112... | collective-permute-start | bytes 589832 | tf_op jit(solution)/shard_map/ppermute | solution.py:26
  98.3 3.9 %copy-start.3 = (bf16[1,2,128,768]{3,2,1,0:T(8,128)(2,1)S(1)}, bf16[1,2,128,768]{3,2,1,0:T(8,128)(2,1)}, u32[]{:S(2)}) copy-start(bf16[1,2,128,768]{3,2,1,0:T(8,128)(2,1)} %stash.5) | copy-start | bytes 1179652
  98.3 22.6 %all-to-all-start.3 = ((bf16[16,8,2176]{2,1,0:T(8,128)(2,1)}), bf16[16,8,2176]{2,1,0:T(8,128)(2,1)S(1)}, u32[]{:S(2)}, u32[]{:S(2)}) async-start(bf16[16,8,2176]{2,1,0:T(8,128)(2,1)} %bitcast.12), calls=%async_computation.3 | async-start | bytes 1114112 | tf_op jit(solution)/shard_map/all_to_all | solution.py:21
  102.1 18.7 %copy-start.8 = (bf16[1,128,768]{2,1,0:T(8,128)(2,1)S(1)}, bf16[1,128,768]{2,1,0:T(8,128)(2,1)}, u32[]{:S(2)}) copy-start(bf16[1,128,768]{2,1,0:T(8,128)(2,1)} %param.11) | copy-start | bytes 589828

commit v9 on v8

--- a/solution.py
+++ b/solution.py
@@ -26,11 +26,10 @@
     return lax.ppermute(value, "section", [(i, sections - 1 - i) for i in range(sections)])
 
 
-def swapped(value, first):
+def shifted(value, by):
     sections = lax.axis_size("section")
-    pairs = [(i, i + 1) for i in range(first, sections - 1, 2)]
-    alone = [(sections - 1, sections - 1)] if (sections - first) % 2 else []
-    return lax.ppermute(value, "section", pairs + [(j, i) for i, j in pairs] + alone)
+    pairs = [(i, i + by) for i in range(sections) if 0 <= i + by < sections]
+    return lax.ppermute(value, "section", pairs)
 
 
 def pieces(value):
@@ -226,14 +225,13 @@
     saved.wait()
 
 
-def first_kernel(got, tokens, fetched, upstream, gain, down, up, after, beside_out, across_out, *, rank):
-    out = (tokens[...].astype(F32) + jnp.dot(got[:, :rank], up[...], preferred_element_type=F32)).astype(BF16)
-    grad = backward(
+def first_kernel(got, tokens, fetched, upstream, gain, down, up, after, out, grad, *, rank):
+    out[...] = (
+        tokens[...].astype(F32) + jnp.dot(got[:, :rank], up[...], preferred_element_type=F32)
+    ).astype(BF16)
+    grad[...] = backward(
         fetched[...], upstream[...], got[:, rank : 2 * rank], got[:, 2 * rank :].astype(F32), gain[...].astype(F32), down[...]
     )[0]
-    odd = lax.rem(lax.axis_index("section"), 2) == 1
-    across_out[...] = jnp.where(odd, out, grad)
-    beside_out[...] = jnp.where(odd, grad, out)
 
 
 def other_kernel(
@@ -263,16 +261,15 @@
 
 
 def second_kernel(
-    kept_in, beside_in, across_in, fresh, still, weight, column_sum, up, side, payload, kept, tokens_out, tokens, upstream, parts, sems,
+    kept_in, before, after, fresh, own, weight, column_sum, up, side, payload, kept, tokens_out, tokens, upstream, parts, sems,
     *, rank
 ):
     place = lax.axis_index("section")
-    odd = lax.rem(place, 2) == 1
-    rows = fresh.shape[0]
-    tokens[...] = jnp.where(place == 0, fresh[...], jnp.where(odd, beside_in[...], across_in[...]))
+    rows = before.shape[0]
+    tokens[...] = jnp.where(place == 0, fresh[...], before[...])
     first = pltpu.make_async_copy(tokens, tokens_out, sems.at[0])
     first.start()
-    upstream[...] = jnp.where(odd, across_in[...], beside_in[...])
+    upstream[...] = jnp.where(place == lax.axis_size("section") - 1, own[...], after[...])
     second = pltpu.make_async_copy(upstream, kept.at[pl.ds(2 * rows, rows)], sems.at[1])
     second.start()
     parts[:, 2 * rank : 3 * rank] = side[:, :rank]
@@ -476,15 +473,15 @@
         cost=LONG,
         name="other",
     )
-    beside_out, across_out = call(
+    first_out, first_grad = call(
         bound(first_kernel, rank=rank),
         [shape(rows, features)] * 2,
         [got0, tokens0, fetched0, grad0, norm_gain, down, up, other],
         left=(7,),
         name="first",
     )
-    beside_in = swapped(beside_out, 0)
-    across_in = swapped(across_out, 1)
+    before_out = shifted(first_out, 1)
+    after_grad = shifted(first_grad, -1)
     kept, gain_term0, filled = call(
         bound(terms_kernel, peers=peers, rank=rank),
         [shape(rank, features), shape(1, features, dtype=F32), shape(rows, 4 * rank + LANES)],
@@ -499,8 +496,8 @@
     payload, kept, tokens1 = call(
         bound(second_kernel, rank=rank),
         [shape(rows, 3 * rank + LANES), shape(rank, features), shape(rows, features)],
-        [kept, beside_in, across_in, fresh_input, beside_out, weight, column_sum, up, other],
-        left=(0, 4),
+        [kept, before_out, after_grad, fresh_input, first_out, weight, column_sum, up, other],
+        left=(0,),
         left_outs=(0, 1, 2),
         aliases=[(0, 1)],
         scratch=[tile, tile, pltpu.VMEM((rows, 3 * rank + LANES), BF16), sems((5,))],

time: 125 us -> 124 us (level)
  the two profiles are of different devices: /device:TPU:134 before, /device:TPU:1 now
where the time goes in v9:
time: 124 us; the launch traced here: 123 us
  starting transfers between devices  62 us (50%)
  waiting for transfers between devices  42 us (34%)
  Pallas kernels  14.8 us (12%)
  local copies, waits for them, and re-layouts  3.5 us (3%)
    ppermute x3, starting transfers between devices, mirrored(): lax.ppermute(value, 'section', [(i, sections - 1 - i) for i in range(sect...  31.6 us
    all_to_all x4, waiting for transfers between devices, across(): return lax.all_to_all(block, 'dp', 0, 0, tiled=True)  27.9 us
    all_to_all x4, starting transfers between devices, across(): return lax.all_to_all(block, 'dp', 0, 0, tiled=True)  22.9 us
    pallas_call x11, Pallas kernels, call(): pl.pallas_call(body, out_shape=tuple(outs), in_specs=[pl.BlockSpec(memory...  14.8 us
    ppermute x3, waiting for transfers between devices, mirrored(): lax.ppermute(value, 'section', [(i, sections - 1 - i) for i in range(sect...  11.7 us
    ppermute x2, starting transfers between devices, shifted(): return lax.ppermute(value, 'section', pairs)  7.42 us
    unnamed x34, local copies, waits for them, and re-layouts  3.5 us
  transfers between devices with their start and end apart: 9, of which 7 were waited for; matrix products, arithmetic and copies ran while one was open for 0% of the time, Pallas kernels for 6%

profile of v9, /device:TPU:1, one launch (start us, length us, event | category | flops | bytes accessed | tf_op | source)
XLA Modules:
  0.0 123.2 jit_solution(11794192700510587769)
XLA Ops:
  0.6 0.7 copy-done.12
  1.3 1.0 copy-done.2
  2.3 0.6 pick.1
  2.9 14.2 %collective-permute-start.1 = (bf16[128,768]{1,0:T(8,128)(2,1)S(1)}, bf16[128,768]{1,0:T(8,128)(2,1)S(1)}, u32[]{:S(2)}, u32[]{:S(2)}) collective-permute-start(bf16[128,768]{1,0:T(8,128)(2,1)S(1)} %get-tuple-element.39), channel_id=1, source_target_pairs={{0,496},{16,480},{32,464},{48,448},{64,432},{80,416},{96,400},{112... | collective-permute-start | bytes 589832 | tf_op jit(solution)/shard_map/ppermute | solution.py:26
  17.2 0.0 copy-start.11
  17.2 0.6 copy-done.11
  17.9 1.5 %start.1 = (bf16[128,1792]{1,0:T(8,128)(2,1)}, bf16[768,512]{1,0:T(8,128)(2,1)S(1)}, f32[1,512]{1,0:T(1,128)S(1)}, f32[128,128]{1,0:T(8,128)S(1)}, bf16[2,128,768]{2,1,0:T(8,128)(2,1)S(1)}) custom-call(bf16[128,768]{1,0:T(8,128)(2,1)S(1)} %bitcast.32, bf16[128,768]{1,0:T(8,128)(2,1)S(1)} %bitcast.35, bf16[1,768]{1,0:T(2,128)(2,1)S(1)} %copy-done.11, ...), custom_call_target="tpu_custom_call" | custom-call | flops 2147483648 | bytes 1048576 | tf_op jit(solution)/shard_map/start/pallas_call | solution.py:387
  19.3 6.7 %collective-permute-done.1.refs_1_.refs_2_ = bf16[128,768]{1,0:T(8,128)(2,1)S(1)} collective-permute-done((bf16[128,768]{1,0:T(8,128)(2,1)S(1)}, bf16[128,768]{1,0:T(8,128)(2,1)S(1)}, u32[]{:S(2)}, u32[]{:S(2)}) %collective-permute-start.1) | collective-permute-done | bytes 196640 | tf_op jit(solution)/shard_map/ppermute | solution.py:26
  26.1 1.0 fetched.1
  27.1 8.0 %all-to-all-start = ((bf16[16,8,1792]{2,1,0:T(8,128)(2,1)}), bf16[16,8,1792]{2,1,0:T(8,128)(2,1)S(1)}, u32[]{:S(2)}, u32[]{:S(2)}) async-start(bf16[16,8,1792]{2,1,0:T(8,128)(2,1)} %bitcast.6), calls=%async_computation | async-start | bytes 917504 | tf_op jit(solution)/shard_map/all_to_all | solution.py:21
  35.0 7.9 %collective-permute-start = (bf16[2,128,768]{2,1,0:T(8,128)(2,1)S(1)}, bf16[2,128,768]{2,1,0:T(8,128)(2,1)S(1)}, u32[]{:S(2)}, u32[]{:S(2)}) collective-permute-start(bf16[2,128,768]{2,1,0:T(8,128)(2,1)S(1)} %get-tuple-element.34), channel_id=1, source_target_pairs={{0,496},{16,480},{32,464},{48,448},{64,432},{80,416},{96,400},{112... | collective-permute-start | bytes 1179656 | tf_op jit(solution)/shard_map/ppermute | solution.py:26
  42.9 6.8 %all-to-all-done = bf16[16,8,1792]{2,1,0:T(8,128)(2,1)S(1)} async-done(((bf16[16,8,1792]{2,1,0:T(8,128)(2,1)}), bf16[16,8,1792]{2,1,0:T(8,128)(2,1)S(1)}, u32[]{:S(2)}, u32[]{:S(2)}) %all-to-all-start) | async-done | bytes 458784 | tf_op jit(solution)/shard_map/all_to_all | solution.py:21
  49.7 1.1 middle.1
  50.9 4.4 %all-to-all-start.1 = ((bf16[16,8,1152]{2,1,0:T(8,128)(2,1)}), bf16[16,8,1152]{2,1,0:T(8,128)(2,1)S(1)}, u32[]{:S(2)}, u32[]{:S(2)}) async-start(bf16[16,8,1152]{2,1,0:T(8,128)(2,1)} %bitcast.8), calls=%async_computation.1 | async-start | bytes 589824 | tf_op jit(solution)/shard_map/all_to_all | solution.py:21
  55.3 4.9 %collective-permute-done.refs_2_.arrived = bf16[2,128,768]{2,1,0:T(8,128)(2,1)S(1)} collective-permute-done((bf16[2,128,768]{2,1,0:T(8,128)(2,1)S(1)}, bf16[2,128,768]{2,1,0:T(8,128)(2,1)S(1)}, u32[]{:S(2)}, u32[]{:S(2)}) %collective-permute-start) | collective-permute-done | bytes 393248 | tf_op jit(solution)/shard_map/ppermute | solution.py:26
  60.2 1.1 copy-done.15
  61.4 1.4 %other.1 = (bf16[128,640]{1,0:T(8,128)(2,1)S(1)}, bf16[512,768]{1,0:T(8,128)(2,1)}) custom-call(s32[2,32]{1,0:T(2,128)S(1)} %bitcast.40, s32[2,32]{1,0:T(2,128)S(1)} %bitcast.41, bf16[2,128,768]{2,1,0:T(8,128)(2,1)S(1)} %collective-permute-done.refs_2_.arrived, bf16[128,768]{1,0:T(8,128)(2,1)S(1)} %bitcast.33, bf16[768,512]{1,0:T(8,128)(2,1)S(1)} %copy-done.15, ...), custom_call_target="tpu_custom_call" | custom-call | flops 12884901888 | bytes 6291456 | tf_op jit(solution)/shard_map/other/pallas_call | solution.py:387
  62.8 2.8 %all-to-all-done.1 = bf16[16,8,1152]{2,1,0:T(8,128)(2,1)S(1)} async-done(((bf16[16,8,1152]{2,1,0:T(8,128)(2,1)}), bf16[16,8,1152]{2,1,0:T(8,128)(2,1)S(1)}, u32[]{:S(2)}, u32[]{:S(2)}) %all-to-all-start.1) | async-done | bytes 294944 | tf_op jit(solution)/shard_map/all_to_all | solution.py:21
  65.5 0.5 first.1
  66.1 5.4 %collective-permute-start.3 = (bf16[128,768]{1,0:T(8,128)(2,1)S(1)}, bf16[128,768]{1,0:T(8,128)(2,1)S(1)}, u32[]{:S(2)}, u32[]{:S(2)}) collective-permute-start(bf16[128,768]{1,0:T(8,128)(2,1)S(1)} %get-tuple-element.46), channel_id=1, source_target_pairs={{16,0},{32,16},{48,32},{64,48},{80,64},{96,80},{112,96},{128,112},... | collective-permute-start | bytes 589832 | tf_op jit(solution)/shard_map/ppermute | solution.py:32
  71.5 2.0 %collective-permute-start.2 = (bf16[128,768]{1,0:T(8,128)(2,1)S(1)}, bf16[128,768]{1,0:T(8,128)(2,1)S(1)}, u32[]{:S(2)}, u32[]{:S(2)}) collective-permute-start(bf16[128,768]{1,0:T(8,128)(2,1)S(1)} %get-tuple-element.45.refs_4_), channel_id=1, source_target_pairs={{0,16},{16,32},{32,48},{48,64},{64,80},{80,96},{96,112},{112,128},... | collective-permute-start | bytes 589832 | tf_op jit(solution)/shard_map/ppermute | solution.py:32
  73.5 1.1 terms.1
  74.6 2.3 %collective-permute-done.3.refs_2_ = bf16[128,768]{1,0:T(8,128)(2,1)S(1)} collective-permute-done((bf16[128,768]{1,0:T(8,128)(2,1)S(1)}, bf16[128,768]{1,0:T(8,128)(2,1)S(1)}, u32[]{:S(2)}, u32[]{:S(2)}) %collective-permute-start.3) | collective-permute-done | bytes 196640 | tf_op jit(solution)/shard_map/ppermute | solution.py:32
  77.0 1.3 %second.1 = (bf16[128,1664]{1,0:T(8,128)(2,1)}, bf16[512,768]{1,0:T(8,128)(2,1)}, bf16[128,768]{1,0:T(8,128)(2,1)}) custom-call(bf16[512,768]{1,0:T(8,128)(2,1)} %get-tuple-element.43.refs_0_, bf16[128,768]{1,0:T(8,128)(2,1)S(1)} %collective-permute-done.2.refs_1_, ...), custom_call_target="tpu_custom_call", output_to_operand_aliasing={{1}: (0, {})} | custom-call | flops 2147483648 | bytes 1048576 | tf_op jit(solution)/shard_map/second/pallas_call | solution.py:387
  78.3 6.2 %all-to-all-start.2 = ((bf16[16,8,1664]{2,1,0:T(8,128)(2,1)}), bf16[16,8,1664]{2,1,0:T(8,128)(2,1)S(1)}, u32[]{:S(2)}, u32[]{:S(2)}) async-start(bf16[16,8,1664]{2,1,0:T(8,128)(2,1)} %bitcast.10), calls=%async_computation.2 | async-start | bytes 851968 | tf_op jit(solution)/shard_map/all_to_all | solution.py:21
  84.5 9.5 %collective-permute-start.4 = (bf16[128,768]{1,0:T(8,128)(2,1)}, bf16[128,768]{1,0:T(8,128)(2,1)}, u32[]{:S(2)}, u32[]{:S(2)}) collective-permute-start(bf16[128,768]{1,0:T(8,128)(2,1)} %get-tuple-element.48.refs_1_), channel_id=1, source_target_pairs={{0,496},{16,480},{32,464},{48,448},{64,432},{80,416},{96,400},{112... | collective-permute-start | bytes 589832 | tf_op jit(solution)/shard_map/ppermute | solution.py:26
  94.0 3.6 %all-to-all-done.2 = bf16[16,8,1664]{2,1,0:T(8,128)(2,1)S(1)} async-done(((bf16[16,8,1664]{2,1,0:T(8,128)(2,1)}), bf16[16,8,1664]{2,1,0:T(8,128)(2,1)S(1)}, u32[]{:S(2)}, u32[]{:S(2)}) %all-to-all-start.2) | async-done | bytes 426016 | tf_op jit(solution)/shard_map/all_to_all | solution.py:21
  97.6 1.0 late.1
  98.6 4.4 %all-to-all-start.3 = ((bf16[16,8,2176]{2,1,0:T(8,128)(2,1)}), bf16[16,8,2176]{2,1,0:T(8,128)(2,1)S(1)}, u32[]{:S(2)}, u32[]{:S(2)}) async-start(bf16[16,8,2176]{2,1,0:T(8,128)(2,1)} %bitcast.12), calls=%async_computation.3 | async-start | bytes 1114112 | tf_op jit(solution)/shard_map/all_to_all | solution.py:21
  103.0 1.8 %stash.4 = (bf16[1,2,128,768]{3,2,1,0:T(8,128)(2,1)}, f32[8,128]{1,0:T(8,128)S(1)}) custom-call(s32[2,32]{1,0:T(2,128)S(1)} %bitcast.42, bf16[1,2,128,768]{3,2,1,0:T(8,128)(2,1)S(1)} %copy-done.3, bf16[2,128,768]{2,1,0:T(8,128)(2,1)S(1)} %collective-permute-done.refs_2_.arrived, bf16[128,768]{1,0:T(8,128)(2,1)} %collective-permute-done.4.partner1), custom_call_target="tpu_custom_call" | custom-call | flops 12884901888 | bytes 6291456 | tf_op jit(solution)/shard_map/stash/pallas_call | solution.py:387
  104.8 14.8 %all-to-all-done.3 = bf16[16,8,2176]{2,1,0:T(8,128)(2,1)S(1)} async-done(((bf16[16,8,2176]{2,1,0:T(8,128)(2,1)}), bf16[16,8,2176]{2,1,0:T(8,128)(2,1)S(1)}, u32[]{:S(2)}, u32[]{:S(2)}) %all-to-all-start.3) | async-done | bytes 557088 | tf_op jit(solution)/shard_map/all_to_all | solution.py:21
  119.6 3.6 %last.1 = (bf16[512,768]{1,0:T(8,128)(2,1)}, bf16[128,768]{1,0:T(8,128)(2,1)}, bf16[128,768]{1,0:T(8,128)(2,1)}, f32[1,768]{1,0:T(1,128)}, bf16[768,512]{1,0:T(8,128)(2,1)}) custom-call(bf16[512,768]{1,0:T(8,128)(2,1)} %get-tuple-element.47.refs_0_, bf16[128,768]{1,0:T(8,128)(2,1)} %get-tuple-element.48.refs_1_, ...), custom_call_target="tpu_custom_call", output_to_operand_aliasing={{0}: (0, {}), {1}: (1, {})} | custom-call | flops 2147483648 | bytes 1048576 | tf_op jit(solution)/shard_map/last/pallas_call | solution.py:387
  (31 shorter events, 0.1 us)
Async XLA Ops:
  0.6 0.7 copy-start.12
  1.3 1.0 copy-start.2
  2.3 14.9 %copy-start = (bf16[1,768,512]{2,1,0:T(8,128)(2,1)S(1)}, bf16[1,768,512]{2,1,0:T(8,128)(2,1)}, u32[]{:S(2)}) copy-start(bf16[1,768,512]{2,1,0:T(8,128)(2,1)} %param.14) | copy-start | bytes 2359300
  2.3 14.9 %copy-start.1 = (bf16[1,512,768]{2,1,0:T(8,128)(2,1)S(1)}, bf16[1,512,768]{2,1,0:T(8,128)(2,1)}, u32[]{:S(2)}) copy-start(bf16[1,512,768]{2,1,0:T(8,128)(2,1)} %param.15) | copy-start | bytes 2359300
  2.3 14.9 %copy-start.4 = (bf16[1,128,768]{2,1,0:T(8,128)(2,1)S(1)}, bf16[1,128,768]{2,1,0:T(8,128)(2,1)}, u32[]{:S(2)}) copy-start(bf16[1,128,768]{2,1,0:T(8,128)(2,1)} %param.9) | copy-start | bytes 589828
  2.3 14.9 %copy-start.6 = (bf16[1,128,768]{2,1,0:T(8,128)(2,1)S(1)}, bf16[1,128,768]{2,1,0:T(8,128)(2,1)}, u32[]{:S(2)}) copy-start(bf16[1,128,768]{2,1,0:T(8,128)(2,1)} %param.11) | copy-start | bytes 589828
  2.9 23.1 %collective-permute-start.1 = (bf16[128,768]{1,0:T(8,128)(2,1)S(1)}, bf16[128,768]{1,0:T(8,128)(2,1)S(1)}, u32[]{:S(2)}, u32[]{:S(2)}) collective-permute-start(bf16[128,768]{1,0:T(8,128)(2,1)S(1)} %get-tuple-element.39), channel_id=1, source_target_pairs={{0,496},{16,480},{32,464},{48,448},{64,432},{80,416},{96,400},{112... | collective-permute-start | bytes 589832 | tf_op jit(solution)/shard_map/ppermute | solution.py:26
  17.2 0.7 copy-start.11
  19.3 7.7 %copy-start.14 = (bf16[768,512]{1,0:T(8,128)(2,1)}, bf16[768,512]{1,0:T(8,128)(2,1)S(1)}, u32[]{:S(2)}) copy-start(bf16[768,512]{1,0:T(8,128)(2,1)S(1)} %get-tuple-element.35.refs_4_.refs_2_.refs_5_) | copy-start | bytes 2359300
  26.1 1.0 copy-start.9
  27.1 22.6 %all-to-all-start = ((bf16[16,8,1792]{2,1,0:T(8,128)(2,1)}), bf16[16,8,1792]{2,1,0:T(8,128)(2,1)S(1)}, u32[]{:S(2)}, u32[]{:S(2)}) async-start(bf16[16,8,1792]{2,1,0:T(8,128)(2,1)} %bitcast.6), calls=%async_computation | async-start | bytes 917504 | tf_op jit(solution)/shard_map/all_to_all | solution.py:21
  35.0 25.2 %collective-permute-start = (bf16[2,128,768]{2,1,0:T(8,128)(2,1)S(1)}, bf16[2,128,768]{2,1,0:T(8,128)(2,1)S(1)}, u32[]{:S(2)}, u32[]{:S(2)}) collective-permute-start(bf16[2,128,768]{2,1,0:T(8,128)(2,1)S(1)} %get-tuple-element.34), channel_id=1, source_target_pairs={{0,496},{16,480},{32,464},{48,448},{64,432},{80,416},{96,400},{112... | collective-permute-start | bytes 1179656 | tf_op jit(solution)/shard_map/ppermute | solution.py:26
  50.9 14.7 %all-to-all-start.1 = ((bf16[16,8,1152]{2,1,0:T(8,128)(2,1)}), bf16[16,8,1152]{2,1,0:T(8,128)(2,1)S(1)}, u32[]{:S(2)}, u32[]{:S(2)}) async-start(bf16[16,8,1152]{2,1,0:T(8,128)(2,1)} %bitcast.8), calls=%async_computation.1 | async-start | bytes 589824 | tf_op jit(solution)/shard_map/all_to_all | solution.py:21
  55.3 5.0 %copy-start.13 = (s32[32,2]{0,1:T(2,128)S(1)}, s32[32,2]{0,1:T(2,128)}, u32[]{:S(2)}) copy-start(s32[32,2]{0,1:T(2,128)} %param.17) | copy-start | bytes 772
  60.2 1.1 copy-start.15
  61.4 4.2 %copy-start.7 = (bf16[1,128,768]{2,1,0:T(8,128)(2,1)S(1)}, bf16[1,128,768]{2,1,0:T(8,128)(2,1)}, u32[]{:S(2)}) copy-start(bf16[1,128,768]{2,1,0:T(8,128)(2,1)} %param.11) | copy-start | bytes 589828
  61.4 4.2 %copy-start.10 = (bf16[128,768]{1,0:T(8,128)(2,1)S(1)}, bf16[128,768]{1,0:T(8,128)(2,1)}, u32[]{:S(2)}) copy-start(bf16[128,768]{1,0:T(8,128)(2,1)} %copy-done.9) | copy-start | bytes 589828
  66.1 10.9 %collective-permute-start.3 = (bf16[128,768]{1,0:T(8,128)(2,1)S(1)}, bf16[128,768]{1,0:T(8,128)(2,1)S(1)}, u32[]{:S(2)}, u32[]{:S(2)}) collective-permute-start(bf16[128,768]{1,0:T(8,128)(2,1)S(1)} %get-tuple-element.46), channel_id=1, source_target_pairs={{16,0},{32,16},{48,32},{64,48},{80,64},{96,80},{112,96},{128,112},... | collective-permute-start | bytes 589832 | tf_op jit(solution)/shard_map/ppermute | solution.py:32
  71.5 5.5 %collective-permute-start.2 = (bf16[128,768]{1,0:T(8,128)(2,1)S(1)}, bf16[128,768]{1,0:T(8,128)(2,1)S(1)}, u32[]{:S(2)}, u32[]{:S(2)}) collective-permute-start(bf16[128,768]{1,0:T(8,128)(2,1)S(1)} %get-tuple-element.45.refs_4_), channel_id=1, source_target_pairs={{0,16},{16,32},{32,48},{48,64},{64,80},{80,96},{96,112},{112,128},... | collective-permute-start | bytes 589832 | tf_op jit(solution)/shard_map/ppermute | solution.py:32
  73.5 3.4 %copy-start.5 = (bf16[128,768]{1,0:T(8,128)(2,1)S(1)}, bf16[128,768]{1,0:T(8,128)(2,1)}, u32[]{:S(2)}) copy-start(bf16[128,768]{1,0:T(8,128)(2,1)} %refs_3_.1) | copy-start | bytes 589828
  73.5 3.4 %copy-start.16 = (bf16[768,512]{1,0:T(8,128)(2,1)S(1)}, bf16[768,512]{1,0:T(8,128)(2,1)}, u32[]{:S(2)}) copy-start(bf16[768,512]{1,0:T(8,128)(2,1)} %copy-done.14) | copy-start | bytes 2359300
  78.3 19.3 %all-to-all-start.2 = ((bf16[16,8,1664]{2,1,0:T(8,128)(2,1)}), bf16[16,8,1664]{2,1,0:T(8,128)(2,1)S(1)}, u32[]{:S(2)}, u32[]{:S(2)}) async-start(bf16[16,8,1664]{2,1,0:T(8,128)(2,1)} %bitcast.10), calls=%async_computation.2 | async-start | bytes 851968 | tf_op jit(solution)/shard_map/all_to_all | solution.py:21
  84.5 18.6 %collective-permute-start.4 = (bf16[128,768]{1,0:T(8,128)(2,1)}, bf16[128,768]{1,0:T(8,128)(2,1)}, u32[]{:S(2)}, u32[]{:S(2)}) collective-permute-start(bf16[128,768]{1,0:T(8,128)(2,1)} %get-tuple-element.48.refs_1_), channel_id=1, source_target_pairs={{0,496},{16,480},{32,464},{48,448},{64,432},{80,416},{96,400},{112... | collective-permute-start | bytes 589832 | tf_op jit(solution)/shard_map/ppermute | solution.py:26
  98.6 4.4 %copy-start.3 = (bf16[1,2,128,768]{3,2,1,0:T(8,128)(2,1)S(1)}, bf16[1,2,128,768]{3,2,1,0:T(8,128)(2,1)}, u32[]{:S(2)}) copy-start(bf16[1,2,128,768]{3,2,1,0:T(8,128)(2,1)} %stash.5) | copy-start | bytes 1179652
  98.6 21.0 %all-to-all-start.3 = ((bf16[16,8,2176]{2,1,0:T(8,128)(2,1)}), bf16[16,8,2176]{2,1,0:T(8,128)(2,1)S(1)}, u32[]{:S(2)}, u32[]{:S(2)}) async-start(bf16[16,8,2176]{2,1,0:T(8,128)(2,1)} %bitcast.12), calls=%async_computation.3 | async-start | bytes 1114112 | tf_op jit(solution)/shard_map/all_to_all | solution.py:21
  103.0 16.6 %copy-start.8 = (bf16[1,128,768]{2,1,0:T(8,128)(2,1)S(1)}, bf16[1,128,768]{2,1,0:T(8,128)(2,1)}, u32[]{:S(2)}) copy-start(bf16[1,128,768]{2,1,0:T(8,128)(2,1)} %param.11) | copy-start | bytes 589828

commit v10 on v8

--- a/solution.py
+++ b/solution.py
@@ -188,7 +188,7 @@
         one.wait()
 
 
-def middle_kernel(got, payload, columns_out, active_back, columns, sems, *, peers, rank, width):
+def middle_kernel(got, payload, columns_out, columns, sems, *, peers, rank, width):
     first = 2 * rank + LANES
     blocks = got[:, 2 * rank : first].astype(F32).reshape(peers, -1, LANES)
     row = lax.broadcasted_iota(jnp.int32, blocks.shape[1:], 0)
@@ -218,18 +218,18 @@
         got[:, first : first + rank], sums, 6, column_sums, width
     )
     active, bent = gelu_and_slope(hidden)
-    active_back[...] = active
     grad_hidden = (slope * bent).astype(BF16)
     payload[:, :rank] = to_all(gelu(hidden_f), peers)
     payload[:, rank : 2 * rank] = to_all(grad_hidden.astype(F32), peers)
-    payload[:, 2 * rank :] = to_all(back_stats(grad_hidden, hidden, mean, inverse, column_exact, width), peers)
+    payload[:, 2 * rank : 3 * rank] = to_all(active, peers)
+    payload[:, 3 * rank :] = to_all(back_stats(grad_hidden, hidden, mean, inverse, column_exact, width), peers)
     saved.wait()
 
 
 def first_kernel(got, tokens, fetched, upstream, gain, down, up, after, beside_out, across_out, *, rank):
     out = (tokens[...].astype(F32) + jnp.dot(got[:, :rank], up[...], preferred_element_type=F32)).astype(BF16)
     grad = backward(
-        fetched[...], upstream[...], got[:, rank : 2 * rank], got[:, 2 * rank :].astype(F32), gain[...].astype(F32), down[...]
+        fetched[...], upstream[...], got[:, rank : 2 * rank], got[:, 3 * rank :].astype(F32), gain[...].astype(F32), down[...]
     )[0]
     odd = lax.rem(lax.axis_index("section"), 2) == 1
     across_out[...] = jnp.where(odd, out, grad)
@@ -249,17 +249,14 @@
 
 
 def terms_kernel(
-    kept_in, got, fetched, upstream, gain, down, active_back, kept, gain_term, payload, scaled, active, sems, *, peers, rank
+    kept_in, got, fetched, upstream, gain, down, kept, gain_term, scaled, sems, *, rank
 ):
-    active[...] = to_all(active_back[...], peers)
-    (ready,) = copies([(active, payload.at[:, pl.ds(3 * rank, rank)])], sems.at[pl.ds(1, 1)])
     scaled[...], gain_term[...] = backward(
-        fetched[...], upstream[...], got[:, rank : 2 * rank], got[:, 2 * rank :].astype(F32), gain[...].astype(F32), down[...]
+        fetched[...], upstream[...], got[:, rank : 2 * rank], got[:, 3 * rank :].astype(F32), gain[...].astype(F32), down[...]
     )[1:]
     rows = scaled.shape[0]
     (saved,) = copies([(scaled, kept.at[pl.ds(rows, rows)])], sems)
     saved.wait()
-    ready.wait()
 
 
 def second_kernel(
@@ -293,7 +290,7 @@
         one.wait()
 
 
-def late_kernel(filled, got, columns, payload, parts, last, sems, *, peers, rank, width):
+def late_kernel(got, columns, payload, parts, last, sems, *, peers, rank, width):
     column_sums = [columns[peer : peer + 1, :] for peer in range(peers)]
     sums = got[:, 3 * rank :].astype(F32)
     stores = []
@@ -313,7 +310,7 @@
     last[...] = to_all(
         back_stats(grad_hidden, hidden, mean, inverse, columns[peers : peers + 1, :], width), peers
     )
-    store(last, 4 * rank, LANES)
+    store(last, 3 * rank, LANES)
     hidden_f = finish_hidden(got[:, :rank], sums, 0, column_sums, width)[0]
     parts[2] = to_all(gelu(hidden_f), peers)
     store(parts.at[2], 0, rank)
@@ -347,10 +344,10 @@
     grad_hidden = got[:, rank : 2 * rank]
     product = jnp.dot(got[:, :rank], up[...], preferred_element_type=F32)
     grad_scaled = times_transposed(grad_hidden, down[...])
-    sums = got[:, 4 * rank :].astype(F32)
+    sums = got[:, 3 * rank :].astype(F32)
     mean, inverse, first, second = [from_lanes(sums, 3 * i) for i in range(4)]
     grad_normed = grad_scaled * gain[...].astype(F32)
-    active_both = jnp.concatenate([got[:, 3 * rank : 4 * rank], got[:, 2 * rank : 3 * rank]], axis=0)
+    active_both = jnp.concatenate([got0[:, 2 * rank : 3 * rank], got[:, 2 * rank : 3 * rank]], axis=0)
     hidden_both = jnp.concatenate([got0[:, rank : 2 * rank], grad_hidden], axis=0)
     stores = []
 
@@ -457,9 +454,9 @@
     )
     got = across(payload)
     both = mirrored(both)
-    payload, columns, active_back = call(
+    payload, columns = call(
         bound(middle_kernel, peers=peers, rank=rank, width=width),
-        [shape(rows, 2 * rank + LANES), shape(peers + 8, rank, dtype=F32), shape(own, rank, dtype=F32)],
+        [shape(rows, 3 * rank + LANES), shape(peers + 8, rank, dtype=F32)],
         [got],
         left_outs=(1,),
         scratch=[pltpu.VMEM((peers + 8, rank), F32), sems((1,))],
@@ -485,14 +482,14 @@
     )
     beside_in = swapped(beside_out, 0)
     across_in = swapped(across_out, 1)
-    kept, gain_term0, filled = call(
-        bound(terms_kernel, peers=peers, rank=rank),
-        [shape(rank, features), shape(1, features, dtype=F32), shape(rows, 4 * rank + LANES)],
-        [kept, got0, fetched0, grad0, norm_gain, down, active_back],
+    kept, gain_term0 = call(
+        bound(terms_kernel, rank=rank),
+        [shape(rank, features), shape(1, features, dtype=F32)],
+        [kept, got0, fetched0, grad0, norm_gain, down],
         left=(0,),
-        left_outs=(0, 2),
+        left_outs=(0,),
         aliases=[(0, 0)],
-        scratch=[tile, pltpu.VMEM((rows, rank), BF16), sems((2,))],
+        scratch=[tile, sems((1,))],
         cost=LONG,
         name="terms",
     )
@@ -510,11 +507,9 @@
     partner1 = mirrored(tokens1)
     (payload,) = call(
         bound(late_kernel, peers=peers, rank=rank, width=width),
-        [shape(rows, 4 * rank + LANES)],
-        [filled, got, columns],
-        left=(0,),
+        [shape(rows, 3 * rank + LANES)],
+        [got, columns],
         left_outs=(0,),
-        aliases=[(0, 0)],
         scratch=[pltpu.VMEM((3, rows, rank), BF16), pltpu.VMEM((rows, LANES), BF16), sems((4,))],
         name="late",
     )

time: 125 us -> 124 us (level)
  the two profiles are of different devices: /device:TPU:134 before, /device:TPU:1 now
where the time goes in v10:
time: 124 us; the launch traced here: 123 us
  starting transfers between devices  58.6 us (47%)
  waiting for transfers between devices  45.5 us (37%)
  Pallas kernels  14.7 us (12%)
  local copies, waits for them, and re-layouts  3.49 us (3%)
    ppermute x3, starting transfers between devices, mirrored(): lax.ppermute(value, 'section', [(i, sections - 1 - i) for i in range(sect...  31.7 us
    all_to_all x4, waiting for transfers between devices, across(): return lax.all_to_all(block, 'dp', 0, 0, tiled=True)  31.5 us
    all_to_all x4, starting transfers between devices, across(): return lax.all_to_all(block, 'dp', 0, 0, tiled=True)  19.6 us
    pallas_call x11, Pallas kernels, call(): pl.pallas_call(body, out_shape=tuple(outs), in_specs=[pl.BlockSpec(memory...  14.7 us
    ppermute x3, waiting for transfers between devices, mirrored(): lax.ppermute(value, 'section', [(i, sections - 1 - i) for i in range(sect...  11.6 us
    ppermute x2, starting transfers between devices, swapped(): lax.ppermute(value, 'section', pairs + [(j, i) for i, j in pairs] + alone)  7.28 us
    unnamed x26, local copies, waits for them, and re-layouts  3.49 us
  transfers between devices with their start and end apart: 9, of which 7 were waited for; matrix products, arithmetic and copies ran while one was open for 0% of the time, Pallas kernels for 6%

profile of v10, /device:TPU:1, one launch (start us, length us, event | category | flops | bytes accessed | tf_op | source)
XLA Modules:
  0.0 123.2 jit_solution(1136278765886484180)
XLA Ops:
  0.6 0.7 copy-done.8
  1.3 1.0 copy-done.2
  2.3 0.6 pick.1
  2.9 14.2 %collective-permute-start.1 = (bf16[128,768]{1,0:T(8,128)(2,1)S(1)}, bf16[128,768]{1,0:T(8,128)(2,1)S(1)}, u32[]{:S(2)}, u32[]{:S(2)}) collective-permute-start(bf16[128,768]{1,0:T(8,128)(2,1)S(1)} %get-tuple-element.37), channel_id=1, source_target_pairs={{0,496},{16,480},{32,464},{48,448},{64,432},{80,416},{96,400},{112... | collective-permute-start | bytes 589832 | tf_op jit(solution)/shard_map/ppermute | solution.py:26
  17.2 0.6 copy-done.7
  17.9 1.5 %start.1 = (bf16[128,1792]{1,0:T(8,128)(2,1)}, bf16[768,512]{1,0:T(8,128)(2,1)S(1)}, f32[1,512]{1,0:T(1,128)S(1)}, f32[128,128]{1,0:T(8,128)S(1)}, bf16[2,128,768]{2,1,0:T(8,128)(2,1)S(1)}) custom-call(bf16[128,768]{1,0:T(8,128)(2,1)S(1)} %bitcast.32, bf16[128,768]{1,0:T(8,128)(2,1)S(1)} %bitcast.35, bf16[1,768]{1,0:T(2,128)(2,1)S(1)} %copy-done.7, ...), custom_call_target="tpu_custom_call" | custom-call | flops 2147483648 | bytes 1048576 | tf_op jit(solution)/shard_map/start/pallas_call | solution.py:387
  19.3 0.0 copy-start.10
  19.3 6.7 %collective-permute-done.1.refs_1_.refs_2_ = bf16[128,768]{1,0:T(8,128)(2,1)S(1)} collective-permute-done((bf16[128,768]{1,0:T(8,128)(2,1)S(1)}, bf16[128,768]{1,0:T(8,128)(2,1)S(1)}, u32[]{:S(2)}, u32[]{:S(2)}) %collective-permute-start.1) | collective-permute-done | bytes 196640 | tf_op jit(solution)/shard_map/ppermute | solution.py:26
  26.1 1.0 fetched.1
  27.0 8.0 %all-to-all-start = ((bf16[16,8,1792]{2,1,0:T(8,128)(2,1)}), bf16[16,8,1792]{2,1,0:T(8,128)(2,1)S(1)}, u32[]{:S(2)}, u32[]{:S(2)}) async-start(bf16[16,8,1792]{2,1,0:T(8,128)(2,1)} %bitcast.6), calls=%async_computation | async-start | bytes 917504 | tf_op jit(solution)/shard_map/all_to_all | solution.py:21
  35.0 7.9 %collective-permute-start = (bf16[2,128,768]{2,1,0:T(8,128)(2,1)S(1)}, bf16[2,128,768]{2,1,0:T(8,128)(2,1)S(1)}, u32[]{:S(2)}, u32[]{:S(2)}) collective-permute-start(bf16[2,128,768]{2,1,0:T(8,128)(2,1)S(1)} %get-tuple-element.32), channel_id=1, source_target_pairs={{0,496},{16,480},{32,464},{48,448},{64,432},{80,416},{96,400},{112... | collective-permute-start | bytes 1179656 | tf_op jit(solution)/shard_map/ppermute | solution.py:26
  42.9 6.8 %all-to-all-done = bf16[16,8,1792]{2,1,0:T(8,128)(2,1)S(1)} async-done(((bf16[16,8,1792]{2,1,0:T(8,128)(2,1)}), bf16[16,8,1792]{2,1,0:T(8,128)(2,1)S(1)}, u32[]{:S(2)}, u32[]{:S(2)}) %all-to-all-start) | async-done | bytes 458784 | tf_op jit(solution)/shard_map/all_to_all | solution.py:21
  49.7 1.2 middle.1
  50.9 4.4 %all-to-all-start.1 = ((bf16[16,8,1664]{2,1,0:T(8,128)(2,1)}), bf16[16,8,1664]{2,1,0:T(8,128)(2,1)S(1)}, u32[]{:S(2)}, u32[]{:S(2)}) async-start(bf16[16,8,1664]{2,1,0:T(8,128)(2,1)} %bitcast.8), calls=%async_computation.1 | async-start | bytes 851968 | tf_op jit(solution)/shard_map/all_to_all | solution.py:21
  55.3 4.9 %collective-permute-done.refs_2_.arrived = bf16[2,128,768]{2,1,0:T(8,128)(2,1)S(1)} collective-permute-done((bf16[2,128,768]{2,1,0:T(8,128)(2,1)S(1)}, bf16[2,128,768]{2,1,0:T(8,128)(2,1)S(1)}, u32[]{:S(2)}, u32[]{:S(2)}) %collective-permute-start) | collective-permute-done | bytes 393248 | tf_op jit(solution)/shard_map/ppermute | solution.py:26
  60.2 1.1 copy-done.11
  61.3 1.4 %other.1 = (bf16[128,640]{1,0:T(8,128)(2,1)S(1)}, bf16[512,768]{1,0:T(8,128)(2,1)}) custom-call(s32[2,32]{1,0:T(2,128)S(1)} %bitcast.40, s32[2,32]{1,0:T(2,128)S(1)} %bitcast.41, bf16[2,128,768]{2,1,0:T(8,128)(2,1)S(1)} %collective-permute-done.refs_2_.arrived, bf16[128,768]{1,0:T(8,128)(2,1)S(1)} %bitcast.33, bf16[768,512]{1,0:T(8,128)(2,1)S(1)} %copy-done.11, ...), custom_call_target="tpu_custom_call" | custom-call | flops 12884901888 | bytes 6291456 | tf_op jit(solution)/shard_map/other/pallas_call | solution.py:387
  62.7 5.4 %all-to-all-done.1 = bf16[16,8,1664]{2,1,0:T(8,128)(2,1)S(1)} async-done(((bf16[16,8,1664]{2,1,0:T(8,128)(2,1)}), bf16[16,8,1664]{2,1,0:T(8,128)(2,1)S(1)}, u32[]{:S(2)}, u32[]{:S(2)}) %all-to-all-start.1) | async-done | bytes 426016 | tf_op jit(solution)/shard_map/all_to_all | solution.py:21
  68.1 0.6 first.1
  68.7 5.4 %collective-permute-start.3 = (bf16[128,768]{1,0:T(8,128)(2,1)S(1)}, bf16[128,768]{1,0:T(8,128)(2,1)S(1)}, u32[]{:S(2)}, u32[]{:S(2)}) collective-permute-start(bf16[128,768]{1,0:T(8,128)(2,1)S(1)} %get-tuple-element.43), channel_id=1, source_target_pairs={{16,32},{48,64},{80,96},{112,128},{144,160},{176,192},{208,224},{2... | collective-permute-start | bytes 589832 | tf_op jit(solution)/shard_map/ppermute | solution.py:33
  74.0 1.9 %collective-permute-start.2 = (bf16[128,768]{1,0:T(8,128)(2,1)S(1)}, bf16[128,768]{1,0:T(8,128)(2,1)S(1)}, u32[]{:S(2)}, u32[]{:S(2)}) collective-permute-start(bf16[128,768]{1,0:T(8,128)(2,1)S(1)} %get-tuple-element.42.refs_4_), channel_id=1, source_target_pairs={{0,16},{32,48},{64,80},{96,112},{128,144},{160,176},{192,208},{224... | collective-permute-start | bytes 589832 | tf_op jit(solution)/shard_map/ppermute | solution.py:33
  76.0 1.0 terms.1
  77.0 2.4 %collective-permute-done.3.refs_2_ = bf16[128,768]{1,0:T(8,128)(2,1)S(1)} collective-permute-done((bf16[128,768]{1,0:T(8,128)(2,1)S(1)}, bf16[128,768]{1,0:T(8,128)(2,1)S(1)}, u32[]{:S(2)}, u32[]{:S(2)}) %collective-permute-start.3) | collective-permute-done | bytes 196640 | tf_op jit(solution)/shard_map/ppermute | solution.py:33
  79.4 1.3 %second.1 = (bf16[128,1664]{1,0:T(8,128)(2,1)}, bf16[512,768]{1,0:T(8,128)(2,1)}, bf16[128,768]{1,0:T(8,128)(2,1)}) custom-call(bf16[512,768]{1,0:T(8,128)(2,1)} %get-tuple-element.40.refs_0_, bf16[128,768]{1,0:T(8,128)(2,1)S(1)} %collective-permute-done.2.refs_1_, ...), custom_call_target="tpu_custom_call", output_to_operand_aliasing={{1}: (0, {})} | custom-call | flops 2147483648 | bytes 1048576 | tf_op jit(solution)/shard_map/second/pallas_call | solution.py:387
  80.7 3.6 %all-to-all-start.2 = ((bf16[16,8,1664]{2,1,0:T(8,128)(2,1)}), bf16[16,8,1664]{2,1,0:T(8,128)(2,1)S(1)}, u32[]{:S(2)}, u32[]{:S(2)}) async-start(bf16[16,8,1664]{2,1,0:T(8,128)(2,1)} %bitcast.10), calls=%async_computation.2 | async-start | bytes 851968 | tf_op jit(solution)/shard_map/all_to_all | solution.py:21
  84.3 9.6 %collective-permute-start.4 = (bf16[128,768]{1,0:T(8,128)(2,1)}, bf16[128,768]{1,0:T(8,128)(2,1)}, u32[]{:S(2)}, u32[]{:S(2)}) collective-permute-start(bf16[128,768]{1,0:T(8,128)(2,1)} %get-tuple-element.45.refs_1_), channel_id=1, source_target_pairs={{0,496},{16,480},{32,464},{48,448},{64,432},{80,416},{96,400},{112... | collective-permute-start | bytes 589832 | tf_op jit(solution)/shard_map/ppermute | solution.py:26
  93.9 5.3 %all-to-all-done.2 = bf16[16,8,1664]{2,1,0:T(8,128)(2,1)S(1)} async-done(((bf16[16,8,1664]{2,1,0:T(8,128)(2,1)}), bf16[16,8,1664]{2,1,0:T(8,128)(2,1)S(1)}, u32[]{:S(2)}, u32[]{:S(2)}) %all-to-all-start.2) | async-done | bytes 426016 | tf_op jit(solution)/shard_map/all_to_all | solution.py:21
  99.2 1.0 late.1
  100.2 3.7 %all-to-all-start.3 = ((bf16[16,8,1664]{2,1,0:T(8,128)(2,1)}), bf16[16,8,1664]{2,1,0:T(8,128)(2,1)S(1)}, u32[]{:S(2)}, u32[]{:S(2)}) async-start(bf16[16,8,1664]{2,1,0:T(8,128)(2,1)} %bitcast.12), calls=%async_computation.3 | async-start | bytes 851968 | tf_op jit(solution)/shard_map/all_to_all | solution.py:21
  103.9 1.7 %stash.4 = (bf16[1,2,128,768]{3,2,1,0:T(8,128)(2,1)}, f32[8,128]{1,0:T(8,128)S(1)}) custom-call(s32[2,32]{1,0:T(2,128)S(1)} %bitcast.42, bf16[1,2,128,768]{3,2,1,0:T(8,128)(2,1)S(1)} %copy-done.3, bf16[2,128,768]{2,1,0:T(8,128)(2,1)S(1)} %collective-permute-done.refs_2_.arrived, bf16[128,768]{1,0:T(8,128)(2,1)} %collective-permute-done.4.partner1), custom_call_target="tpu_custom_call" | custom-call | flops 12884901888 | bytes 6291456 | tf_op jit(solution)/shard_map/stash/pallas_call | solution.py:387
  105.6 14.0 %all-to-all-done.3 = bf16[16,8,1664]{2,1,0:T(8,128)(2,1)S(1)} async-done(((bf16[16,8,1664]{2,1,0:T(8,128)(2,1)}), bf16[16,8,1664]{2,1,0:T(8,128)(2,1)S(1)}, u32[]{:S(2)}, u32[]{:S(2)}) %all-to-all-start.3) | async-done | bytes 426016 | tf_op jit(solution)/shard_map/all_to_all | solution.py:21
  119.7 3.6 %last.1 = (bf16[512,768]{1,0:T(8,128)(2,1)}, bf16[128,768]{1,0:T(8,128)(2,1)}, bf16[128,768]{1,0:T(8,128)(2,1)}, f32[1,768]{1,0:T(1,128)}, bf16[768,512]{1,0:T(8,128)(2,1)}) custom-call(bf16[512,768]{1,0:T(8,128)(2,1)} %get-tuple-element.44.refs_0_, bf16[128,768]{1,0:T(8,128)(2,1)} %get-tuple-element.45.refs_1_, ...), custom_call_target="tpu_custom_call", output_to_operand_aliasing={{0}: (0, {}), {1}: (1, {})} | custom-call | flops 2147483648 | bytes 1048576 | tf_op jit(solution)/shard_map/last/pallas_call | solution.py:387
  (23 shorter events, 0.1 us)
Async XLA Ops:
  0.6 0.7 copy-start.8
  1.3 1.0 copy-start.2
  2.3 14.9 %copy-start = (bf16[1,768,512]{2,1,0:T(8,128)(2,1)S(1)}, bf16[1,768,512]{2,1,0:T(8,128)(2,1)}, u32[]{:S(2)}) copy-start(bf16[1,768,512]{2,1,0:T(8,128)(2,1)} %param.14) | copy-start | bytes 2359300
  2.3 14.9 %copy-start.1 = (bf16[1,512,768]{2,1,0:T(8,128)(2,1)S(1)}, bf16[1,512,768]{2,1,0:T(8,128)(2,1)}, u32[]{:S(2)}) copy-start(bf16[1,512,768]{2,1,0:T(8,128)(2,1)} %param.15) | copy-start | bytes 2359300
  2.3 14.9 %copy-start.4 = (bf16[1,128,768]{2,1,0:T(8,128)(2,1)S(1)}, bf16[1,128,768]{2,1,0:T(8,128)(2,1)}, u32[]{:S(2)}) copy-start(bf16[1,128,768]{2,1,0:T(8,128)(2,1)} %param.9) | copy-start | bytes 589828
  2.3 14.9 %copy-start.6 = (bf16[1,128,768]{2,1,0:T(8,128)(2,1)S(1)}, bf16[1,128,768]{2,1,0:T(8,128)(2,1)}, u32[]{:S(2)}) copy-start(bf16[1,128,768]{2,1,0:T(8,128)(2,1)} %param.11) | copy-start | bytes 589828
  2.9 23.1 %collective-permute-start.1 = (bf16[128,768]{1,0:T(8,128)(2,1)S(1)}, bf16[128,768]{1,0:T(8,128)(2,1)S(1)}, u32[]{:S(2)}, u32[]{:S(2)}) collective-permute-start(bf16[128,768]{1,0:T(8,128)(2,1)S(1)} %get-tuple-element.37), channel_id=1, source_target_pairs={{0,496},{16,480},{32,464},{48,448},{64,432},{80,416},{96,400},{112... | collective-permute-start | bytes 589832 | tf_op jit(solution)/shard_map/ppermute | solution.py:26
  17.2 0.7 copy-start.7
  19.3 7.7 %copy-start.10 = (bf16[768,512]{1,0:T(8,128)(2,1)}, bf16[768,512]{1,0:T(8,128)(2,1)S(1)}, u32[]{:S(2)}) copy-start(bf16[768,512]{1,0:T(8,128)(2,1)S(1)} %get-tuple-element.33.refs_4_.refs_2_.refs_5_) | copy-start | bytes 2359300
  27.0 22.6 %all-to-all-start = ((bf16[16,8,1792]{2,1,0:T(8,128)(2,1)}), bf16[16,8,1792]{2,1,0:T(8,128)(2,1)S(1)}, u32[]{:S(2)}, u32[]{:S(2)}) async-start(bf16[16,8,1792]{2,1,0:T(8,128)(2,1)} %bitcast.6), calls=%async_computation | async-start | bytes 917504 | tf_op jit(solution)/shard_map/all_to_all | solution.py:21
  35.0 25.2 %collective-permute-start = (bf16[2,128,768]{2,1,0:T(8,128)(2,1)S(1)}, bf16[2,128,768]{2,1,0:T(8,128)(2,1)S(1)}, u32[]{:S(2)}, u32[]{:S(2)}) collective-permute-start(bf16[2,128,768]{2,1,0:T(8,128)(2,1)S(1)} %get-tuple-element.32), channel_id=1, source_target_pairs={{0,496},{16,480},{32,464},{48,448},{64,432},{80,416},{96,400},{112... | collective-permute-start | bytes 1179656 | tf_op jit(solution)/shard_map/ppermute | solution.py:26
  50.9 17.2 %all-to-all-start.1 = ((bf16[16,8,1664]{2,1,0:T(8,128)(2,1)}), bf16[16,8,1664]{2,1,0:T(8,128)(2,1)S(1)}, u32[]{:S(2)}, u32[]{:S(2)}) async-start(bf16[16,8,1664]{2,1,0:T(8,128)(2,1)} %bitcast.8), calls=%async_computation.1 | async-start | bytes 851968 | tf_op jit(solution)/shard_map/all_to_all | solution.py:21
  55.3 4.9 %copy-start.9 = (s32[32,2]{0,1:T(2,128)S(1)}, s32[32,2]{0,1:T(2,128)}, u32[]{:S(2)}) copy-start(s32[32,2]{0,1:T(2,128)} %param.17) | copy-start | bytes 772
  60.2 1.1 copy-start.11
  68.7 10.7 %collective-permute-start.3 = (bf16[128,768]{1,0:T(8,128)(2,1)S(1)}, bf16[128,768]{1,0:T(8,128)(2,1)S(1)}, u32[]{:S(2)}, u32[]{:S(2)}) collective-permute-start(bf16[128,768]{1,0:T(8,128)(2,1)S(1)} %get-tuple-element.43), channel_id=1, source_target_pairs={{16,32},{48,64},{80,96},{112,128},{144,160},{176,192},{208,224},{2... | collective-permute-start | bytes 589832 | tf_op jit(solution)/shard_map/ppermute | solution.py:33
  74.0 5.3 %collective-permute-start.2 = (bf16[128,768]{1,0:T(8,128)(2,1)S(1)}, bf16[128,768]{1,0:T(8,128)(2,1)S(1)}, u32[]{:S(2)}, u32[]{:S(2)}) collective-permute-start(bf16[128,768]{1,0:T(8,128)(2,1)S(1)} %get-tuple-element.42.refs_4_), channel_id=1, source_target_pairs={{0,16},{32,48},{64,80},{96,112},{128,144},{160,176},{192,208},{224... | collective-permute-start | bytes 589832 | tf_op jit(solution)/shard_map/ppermute | solution.py:33
  76.0 3.4 %copy-start.5 = (bf16[128,768]{1,0:T(8,128)(2,1)S(1)}, bf16[128,768]{1,0:T(8,128)(2,1)}, u32[]{:S(2)}) copy-start(bf16[128,768]{1,0:T(8,128)(2,1)} %refs_3_.1) | copy-start | bytes 589828
  76.0 3.4 %copy-start.12 = (bf16[768,512]{1,0:T(8,128)(2,1)S(1)}, bf16[768,512]{1,0:T(8,128)(2,1)}, u32[]{:S(2)}) copy-start(bf16[768,512]{1,0:T(8,128)(2,1)} %copy-done.10) | copy-start | bytes 2359300
  80.7 18.5 %all-to-all-start.2 = ((bf16[16,8,1664]{2,1,0:T(8,128)(2,1)}), bf16[16,8,1664]{2,1,0:T(8,128)(2,1)S(1)}, u32[]{:S(2)}, u32[]{:S(2)}) async-start(bf16[16,8,1664]{2,1,0:T(8,128)(2,1)} %bitcast.10), calls=%async_computation.2 | async-start | bytes 851968 | tf_op jit(solution)/shard_map/all_to_all | solution.py:21
  84.3 19.6 %collective-permute-start.4 = (bf16[128,768]{1,0:T(8,128)(2,1)}, bf16[128,768]{1,0:T(8,128)(2,1)}, u32[]{:S(2)}, u32[]{:S(2)}) collective-permute-start(bf16[128,768]{1,0:T(8,128)(2,1)} %get-tuple-element.45.refs_1_), channel_id=1, source_target_pairs={{0,496},{16,480},{32,464},{48,448},{64,432},{80,416},{96,400},{112... | collective-permute-start | bytes 589832 | tf_op jit(solution)/shard_map/ppermute | solution.py:26
  100.1 3.7 %copy-start.3 = (bf16[1,2,128,768]{3,2,1,0:T(8,128)(2,1)S(1)}, bf16[1,2,128,768]{3,2,1,0:T(8,128)(2,1)}, u32[]{:S(2)}) copy-start(bf16[1,2,128,768]{3,2,1,0:T(8,128)(2,1)} %stash.5) | copy-start | bytes 1179652
  100.2 19.5 %all-to-all-start.3 = ((bf16[16,8,1664]{2,1,0:T(8,128)(2,1)}), bf16[16,8,1664]{2,1,0:T(8,128)(2,1)S(1)}, u32[]{:S(2)}, u32[]{:S(2)}) async-start(bf16[16,8,1664]{2,1,0:T(8,128)(2,1)} %bitcast.12), calls=%async_computation.3 | async-start | bytes 851968 | tf_op jit(solution)/shard_map/all_to_all | solution.py:21
